TPU v7x, 512 devices: a whole 4x8x8 slice. The times are simulated.
512 devices in a mesh: doc: 16 (over y, core), seq: 32 (over x, z).
Axes of the slice: x: 4, y: 8, z: 8, core: 2. Of those that a mesh axis runs over, the one named last changes fastest.
Arguments:
- text_query: bfloat16 [65536, 2048], P(('doc', 'seq')), parts along dimension 0, may hold values from -6 to 6
- stretch_kv: bfloat16 [65536, 4, 256], P(('doc', 'seq')), parts along dimension 0, may hold values from -6 to 6
- cache_kv: bfloat16 [4096, 4, 256], P(('doc', 'seq')), parts along dimension 0, may hold values from -6 to 6
- cross_query: bfloat16 [65536, 2048], P(('doc', 'seq')), parts along dimension 0, may hold values from -6 to 6
- image_kv: bfloat16 [512, 32, 4, 256], P(('doc', 'seq')), parts along dimension 0, may hold values from -6 to 6
- image_start: int32 [512], P('doc'), parts along dimension 0, may hold values from 0 to 4095, as said below
- image_stop: int32 [512], P('doc'), parts along dimension 0, may hold values from 1 to 4096, as said below
- image_lengths: int32 [512], P('doc'), parts along dimension 0, may hold values from 2 to 32
- cross_gate: float32 [16], P('doc'), parts along dimension 0, may hold values from 0.5 to 2
Outputs:
- self_context: bfloat16 [65536, 2048], P(('doc', 'seq')), parts along dimension 0
- cross_context: bfloat16 [65536, 2048], P(('doc', 'seq')), parts along dimension 0
There are 16 independent parts, one for each index of `doc`. A program takes and returns all parts, laid end to end along the dimension named above; each array names one. Nothing has to cross between parts.
Inputs may be any that keep to these rules, and one draw needn't show every extreme that they name: `image_start`: image i's span starts in rows i * 128 to (i + 1) * 128 - 1; image 0 starts at row 0. image_stop[i] > image_start[i] and image_stop[i] <= min((i + 2) * 128, 4096); the last image's span ends at 4096.
All inputs are finite; a program needn't handle non-finite values.
Results may differ from a plain program's by a relative error of at most 0.0049.
Values may be sent and summed in bfloat16 or wider, within the bound.
No kernel may reach another device: no remote copies, remote signals or barrier semaphores. Data moves between devices by JAX's collectives and lax.ppermute only.
A program may use at most 64 MiB of HBM per device.

v0:
```python
import math

import jax
import jax.numpy as jnp
from jax import lax
from jax.sharding import PartitionSpec as P

LOW_SCORE = -1e30


def normalize(scores, allowed):
    masked = jnp.where(allowed, scores, LOW_SCORE)
    highest = jnp.max(masked, axis=-1, keepdims=True)
    weights = jnp.where(allowed, jnp.exp(masked - highest), 0.0)
    present = jnp.any(allowed, axis=-1, keepdims=True)
    totals = jnp.sum(weights, axis=-1, keepdims=True) + jnp.where(present, 0.0, 1.0)
    return ((weights / totals).astype(jnp.bfloat16), present)


def shards(
    text_query,
    stretch_kv,
    cache_kv,
    cross_query,
    image_kv,
    image_start,
    image_stop,
    image_lengths,
    cross_gate,
):
    seq_width = lax.axis_size("seq")
    my_index = lax.axis_index("seq")
    row_count = text_query.shape[0]
    kv_heads = stretch_kv.shape[1]
    head_dim = stretch_kv.shape[2] // 2
    head_count = text_query.shape[1] // head_dim
    row_split = max(1, seq_width // head_count)
    local_heads = max(1, head_count // seq_width)
    parity = my_index % row_split
    copies = seq_width // kv_heads
    tokens = row_count * seq_width
    held_rows = tokens // row_split
    block_rows = min(held_rows, max(512, held_rows // 8))
    score_scale = 1.0 / math.sqrt(head_dim)
    gate_value = jnp.tanh(cross_gate[0])
    image_rows = image_kv.shape[1]
    image_count = image_start.shape[0]
    own_image = image_kv.reshape(image_rows, kv_heads, 2 * head_dim)

    def head_split(values):
        grouped = values.reshape(row_count // row_split, row_split, head_count, head_dim)
        grouped = jnp.transpose(grouped, (0, 2, 1, 3))
        return grouped.reshape(row_count // row_split, seq_width, local_heads * head_dim)

    def token_order(values):
        grouped = values.reshape(row_count // row_split, head_count, row_split, head_dim)
        grouped = jnp.transpose(grouped, (0, 2, 1, 3))
        return grouped.reshape(row_count, head_count * head_dim)

    def spread(values):
        return jnp.repeat(values, copies, axis=1)

    moved_query, moved_cross, moved_stretch, moved_cache, moved_image = (
        lax.all_to_all(head_split(text_query), "seq", split_axis=1, concat_axis=0, tiled=True),
        lax.all_to_all(head_split(cross_query), "seq", split_axis=1, concat_axis=0, tiled=True),
        lax.all_to_all(spread(stretch_kv), "seq", split_axis=1, concat_axis=0, tiled=True),
        lax.all_to_all(spread(cache_kv), "seq", split_axis=1, concat_axis=0, tiled=True),
        lax.all_to_all(spread(own_image), "seq", split_axis=1, concat_axis=0, tiled=True),
    )
    cached = moved_cache.shape[0]
    key_rows = jnp.concatenate([moved_cache[:, 0, :head_dim], moved_stretch[:, 0, :head_dim]], 0)
    value_rows = jnp.concatenate([moved_cache[:, 0, head_dim:], moved_stretch[:, 0, head_dim:]], 0)
    results = []
    for first_row in range(0, held_rows, block_rows):
        key_reach = cached + min(tokens, row_split * (first_row + block_rows))
        scores = (
            jnp.einsum(
                "qhd,kd->hqk",
                moved_query[first_row : first_row + block_rows],
                key_rows[:key_reach],
                preferred_element_type=jnp.float32,
            )
            * score_scale
        )
        columns = jnp.arange(key_reach)[None, None, :]
        positions = row_split * (first_row + jnp.arange(block_rows)[None, :, None]) + parity
        weights, present = normalize(scores, (columns < cached) | (columns - cached <= positions))
        results.append(
            jnp.einsum(
                "hqk,kd->qhd", weights, value_rows[:key_reach], preferred_element_type=jnp.float32
            ).astype(jnp.bfloat16)
        )
    self_heads = jnp.concatenate(results, 0)
    image_keys = moved_image[:, 0, :head_dim]
    image_values = moved_image[:, 0, head_dim:]
    pieces = []
    for first_row in range(0, held_rows, block_rows):
        first_token = row_split * first_row
        last_token = row_split * (first_row + block_rows - 1) + row_split - 1
        low_owner = max(0, first_token // row_count - 1)
        high_owner = min(image_count, last_token // row_count + 1)
        key_low = low_owner * image_rows
        key_high = high_owner * image_rows
        slot_start = jnp.repeat(image_start[low_owner:high_owner], image_rows)
        slot_stop = jnp.repeat(image_stop[low_owner:high_owner], image_rows)
        slot_length = jnp.repeat(image_lengths[low_owner:high_owner], image_rows)
        within = jnp.arange(key_high - key_low) % image_rows
        positions = row_split * (first_row + jnp.arange(block_rows)[:, None]) + parity
        allowed = (
            (slot_start[None, :] <= positions)
            & (positions < slot_stop[None, :])
            & (within < slot_length)[None, :]
        )
        scores = (
            jnp.einsum(
                "qhd,kd->hqk",
                moved_cross[first_row : first_row + block_rows],
                image_keys[key_low:key_high],
                preferred_element_type=jnp.float32,
            )
            * score_scale
        )
        weights, present = normalize(scores, allowed[None])
        context = jnp.einsum(
            "hqk,kd->qhd",
            weights,
            image_values[key_low:key_high],
            preferred_element_type=jnp.float32,
        )
        pieces.append((gate_value * context * present[0][:, :, None]).astype(jnp.bfloat16))
    cross_heads = jnp.concatenate(pieces, 0)
    back_self, back_cross = (
        lax.all_to_all(self_heads, "seq", split_axis=0, concat_axis=1, tiled=True),
        lax.all_to_all(cross_heads, "seq", split_axis=0, concat_axis=1, tiled=True),
    )
    cross_context = token_order(back_cross)
    self_context = token_order(back_self)
    return (self_context, cross_context)


def solution(mesh):
    in_specs = (
        P(("doc", "seq"), None),
        P(("doc", "seq"), None, None),
        P(("doc", "seq"), None, None),
        P(("doc", "seq"), None),
        P(("doc", "seq"), None, None, None),
        P("doc"),
        P("doc"),
        P("doc"),
        P("doc"),
    )
    out_specs = (P(("doc", "seq"), None), P(("doc", "seq"), None))
    return jax.shard_map(shards, mesh=mesh, in_specs=in_specs, out_specs=out_specs, check_vma=False)
```

profile of v0, /device:TPU:56, one launch (start us, length us, event | category | flops | bytes accessed | tf_op | source)
XLA Modules:
  0.0 211.0 jit_solution(901827864974145460)
XLA Ops:
  0.7 0.8 copy.36
  1.5 0.6 broadcast_in_dim.157
  2.1 13.2 %all-to-all-start = ((bf16[8,32,256]{2,0,1:T(8,128)(2,1)}), bf16[8,32,256]{2,0,1:T(8,128)(2,1)S(1)}, u32[]{:S(2)}, u32[]{:S(2)}) async-start(bf16[8,32,256]{2,0,1:T(8,128)(2,1)} %bitcast), calls=%async_computation | async-start | bytes 262144 | tf_op jit(solution)/shard_map/all_to_all | solution.py:67
  15.3 0.8 fusion.123
  16.3 0.8 fusion.122
  17.1 0.8 fusion.121
  18.0 1.1 copy.47
  19.2 1.0 copy.38
  20.3 1.0 copy.42
  23.0 2.5 %all-to-all-done = bf16[8,32,256]{2,0,1:T(8,128)(2,1)S(1)} async-done(((bf16[8,32,256]{2,0,1:T(8,128)(2,1)}), bf16[8,32,256]{2,0,1:T(8,128)(2,1)S(1)}, u32[]{:S(2)}, u32[]{:S(2)}) %all-to-all-start) | async-done | bytes 131104 | tf_op jit(solution)/shard_map/all_to_all | solution.py:67
  25.6 7.3 %all-to-all-start.2 = ((bf16[64,32,128]{2,0,1:T(8,128)(2,1)}), bf16[64,32,128]{2,0,1:T(8,128)(2,1)S(1)}, u32[]{:S(2)}, u32[]{:S(2)}) async-start(bf16[64,32,128]{2,0,1:T(8,128)(2,1)} %bitcast.17), calls=%async_computation.2 | async-start | bytes 1048576 | tf_op jit(solution)/shard_map/all_to_all | solution.py:64
  34.2 15.4 %all-to-all-done.2 = bf16[64,32,128]{2,0,1:T(8,128)(2,1)S(1)} async-done(((bf16[64,32,128]{2,0,1:T(8,128)(2,1)}), bf16[64,32,128]{2,0,1:T(8,128)(2,1)S(1)}, u32[]{:S(2)}, u32[]{:S(2)}) %all-to-all-start.2) | async-done | bytes 524320 | tf_op jit(solution)/shard_map/all_to_all | solution.py:64
  49.5 5.2 %all-to-all-start.5 = ((bf16[64,32,128]{2,0,1:T(8,128)(2,1)}), bf16[64,32,128]{2,0,1:T(8,128)(2,1)S(1)}, u32[]{:S(2)}, u32[]{:S(2)}) async-start(bf16[64,32,128]{2,0,1:T(8,128)(2,1)} %bitcast.56), calls=%async_computation.5 | async-start | bytes 1048576 | tf_op jit(solution)/shard_map/all_to_all | solution.py:65
  55.0 0.9 fusion.14
  55.9 15.4 %all-to-all-done.5 = bf16[64,32,128]{2,0,1:T(8,128)(2,1)S(1)} async-done(((bf16[64,32,128]{2,0,1:T(8,128)(2,1)}), bf16[64,32,128]{2,0,1:T(8,128)(2,1)S(1)}, u32[]{:S(2)}, u32[]{:S(2)}) %all-to-all-start.5) | async-done | bytes 524320 | tf_op jit(solution)/shard_map/all_to_all | solution.py:65
  71.3 0.9 broadcast_in_dim.172
  72.2 5.1 %all-to-all-start.4 = ((bf16[32,32,256]{2,0,1:T(8,128)(2,1)}), bf16[32,32,256]{2,0,1:T(8,128)(2,1)S(1)}, u32[]{:S(2)}, u32[]{:S(2)}) async-start(bf16[32,32,256]{2,0,1:T(8,128)(2,1)} %bitcast.50), calls=%async_computation.4 | async-start | bytes 1048576 | tf_op jit(solution)/shard_map/all_to_all | solution.py:68
  77.3 1.5 fusion.5
  78.8 2.2 %fusion.1 = pred[512]{0:T(512)(128)(4,1)S(1)} fusion(s32[512]{0:T(512)S(1)} %get-tuple-element.40, s32[3328]{0:T(1024)S(1)} %iota_add_fusion.1, pred[3328]{0:T(1024)(128)(4,1)S(1)} %iota_compare_fusion.1), kind=kLoop, calls=%fused_computation.9 | loop fusion | flops 5111296 | bytes 19200 | tf_op jit(solution)/shard_map/reduce_or | solution.py:15
  81.0 3.0 %fusion = pred[512]{0:T(512)(128)(4,1)S(1)} fusion(s32[512]{0:T(512)S(1)} %get-tuple-element.39, s32[4352]{0:T(1024)S(1)} %iota_add_fusion, pred[4352]{0:T(1024)(128)(4,1)S(1)} %iota_compare_fusion), kind=kLoop, calls=%fused_computation.4 | loop fusion | flops 6684160 | bytes 24320 | tf_op jit(solution)/shard_map/reduce_or | solution.py:15
  84.0 9.6 %all-to-all-done.4 = bf16[32,32,256]{2,0,1:T(8,128)(2,1)S(1)} async-done(((bf16[32,32,256]{2,0,1:T(8,128)(2,1)}), bf16[32,32,256]{2,0,1:T(8,128)(2,1)S(1)}, u32[]{:S(2)}, u32[]{:S(2)}) %all-to-all-start.4) | async-done | bytes 524320 | tf_op jit(solution)/shard_map/all_to_all | solution.py:68
  93.5 1.6 broadcast_in_dim.158
  95.1 5.2 %all-to-all-start.1 = ((bf16[128,32,256]{2,0,1:T(8,128)(2,1)}), bf16[128,32,256]{2,0,1:T(8,128)(2,1)S(1)}, u32[]{:S(2)}, u32[]{:S(2)}) async-start(bf16[128,32,256]{2,0,1:T(8,128)(2,1)} %bitcast.270), calls=%async_computation.1 | async-start | bytes 4194304 | tf_op jit(solution)/shard_map/all_to_all | solution.py:66
  100.4 1.2 fusion.131
  106.3 1.7 reduce.25
  108.0 2.0 reshape.1339
  110.0 39.6 %all-to-all-done.1 = bf16[128,32,256]{2,0,1:T(8,128)(2,1)S(1)} async-done(((bf16[128,32,256]{2,0,1:T(8,128)(2,1)}), bf16[128,32,256]{2,0,1:T(8,128)(2,1)S(1)}, u32[]{:S(2)}, u32[]{:S(2)}) %all-to-all-start.1) | async-done | bytes 2097184 | tf_op jit(solution)/shard_map/all_to_all | solution.py:66
  149.5 6.0 %all-to-all-start.6 = ((bf16[32,2,4096]{2,1,0:T(2,128)(2,1)}), bf16[32,2,4096]{2,1,0:T(2,128)(2,1)S(1)}, u32[]{:S(2)}, u32[]{:S(2)}) async-start(bf16[32,2,4096]{2,1,0:T(2,128)(2,1)} %reshape.1339), calls=%async_computation.6 | async-start | bytes 1048576 | tf_op jit(solution)/shard_map/all_to_all | solution.py:134
  155.7 2.2 %fusion.124 = (f32[512]{0:T(512)S(1)}, f32[1,512,4352]{1,2,0:T(8,128)S(1)}) fusion(bf16[512,128]{1,0:T(8,128)(2,1)S(1)} %bitcast.296, bf16[256,128]{1,0:T(8,128)(2,1)S(1)} %get-tuple-element.13, bf16[4096,128]{1,0:T(8,128)(2,1)S(1)} %get-tuple-element.3, s32[512]{0:T(512)S(1)} %get-tuple-element.39, s32[4352]{0:T(1024)S(1)} %iota_add_fusion, ...), kind=kOutput, calls=%fused_computation.189 | convolution fusion | flops 583794176 | bytes 10183936 | tf_op jit(solution)/shard_map/qhd,kd->hqk/dot_general | solution.py:77
  158.0 1.7 fusion.125
  159.7 3.9 %fusion.2 = f32[512]{0:T(512)S(1)} fusion(f32[1,512,4352]{1,2,0:T(8,128)S(1)} %get-tuple-element.24, f32[512]{0:T(512)S(1)} %get-tuple-element.23, s32[512]{0:T(512)S(1)} %get-tuple-element.39, s32[4352]{0:T(1024)S(1)} %iota_add_fusion, pred[4352]{0:T(1024)(128)(4,1)S(1)} %iota_compare_fusion), kind=kLoop, calls=%fused_computation.10 | loop fusion | flops 11140608 | bytes 8940800 | tf_op jit(solution)/shard_map/reduce_sum | solution.py:16
  163.7 2.8 %fusion.4 = f32[512]{0:T(512)S(1)} fusion(f32[1,512,3328]{1,2,0:T(8,128)S(1)} %get-tuple-element.26, f32[512]{0:T(512)S(1)} %get-tuple-element.25, s32[512]{0:T(512)S(1)} %get-tuple-element.40, s32[3328]{0:T(1024)S(1)} %iota_add_fusion.1, pred[3328]{0:T(1024)(128)(4,1)S(1)} %iota_compare_fusion.1), kind=kLoop, calls=%fused_computation.13 | loop fusion | flops 8519168 | bytes 6838528 | tf_op jit(solution)/shard_map/reduce_sum | solution.py:16
  166.4 3.5 %fusion.59 = bf16[512,1,128]{0,2,1:T(8,128)(2,1)S(1)} fusion(f32[512]{0:T(512)S(1)} %select_add_fusion.4, f32[1,512,4352]{1,2,0:T(8,128)S(1)} %get-tuple-element.24, f32[512]{0:T(512)S(1)} %get-tuple-element.23, s32[512]{0:T(512)S(1)} %get-tuple-element.39, s32[4352]{0:T(1024)S(1)} %iota_add_fusion, pred[4352]{0:T(1024)(128)(4,1)S(1)} %iota_compare_fusion, ...), kind=kOutput, calls=%fused_computation.79 | convolution fusion | flops 586088448 | bytes 10185984 | tf_op jit(solution)/shard_map/hqk,kd->qhd/dot_general | solution.py:89
  170.0 2.7 %fusion.62 = bf16[512,1,128]{0,2,1:T(8,128)(2,1)S(1)} fusion(f32[512]{0:T(512)S(1)} %select_add_fusion.5, f32[1,512,3328]{1,2,0:T(8,128)S(1)} %get-tuple-element.26, f32[512]{0:T(512)S(1)} %get-tuple-element.25, s32[512]{0:T(512)S(1)} %get-tuple-element.40, s32[3328]{0:T(1024)S(1)} %iota_add_fusion.1, pred[3328]{0:T(1024)(128)(4,1)S(1)} %iota_compare_fusion.1, ...), kind=kOutput, calls=%fused_computation.80 | convolution fusion | flops 448200704 | bytes 8083712 | tf_op jit(solution)/shard_map/hqk,kd->qhd/dot_general | solution.py:89
  172.7 1.3 fusion.126
  174.0 0.8 fusion.127
  174.8 1.1 fusion.17
  175.9 1.2 fusion.52
  177.1 2.3 %fusion.11 = f32[512]{0:T(512)S(1)} fusion(f32[1,512,2304]{1,2,0:T(8,128)S(1)} %get-tuple-element.28, f32[512]{0:T(512)S(1)} %get-tuple-element.27, s32[512]{0:T(512)S(1)} %get-tuple-element.41, s32[2304]{0:T(1024)S(1)} %iota_add_fusion.2, pred[2304]{0:T(1024)(128)(4,1)S(1)} %iota_compare_fusion.2), kind=kLoop, calls=%fused_computation.24 | loop fusion | flops 5897728 | bytes 4736256 | tf_op jit(solution)/shard_map/reduce_sum | solution.py:16
  179.4 1.9 fusion.65
  181.4 1.0 reduce.24
  182.7 0.9 reshape.1337
  183.6 9.6 %all-to-all-start.3 = ((bf16[32,2,4096]{2,1,0:T(2,128)(2,1)}), bf16[32,2,4096]{2,1,0:T(2,128)(2,1)S(1)}, u32[]{:S(2)}, u32[]{:S(2)}) async-start(bf16[32,2,4096]{2,1,0:T(2,128)(2,1)} %reshape.1337), calls=%async_computation.3 | async-start | bytes 1048576 | tf_op jit(solution)/shard_map/all_to_all | solution.py:133
  193.2 0.5 reshape.1340
  194.2 0.9 copy.53
  195.2 13.9 %all-to-all-done.3 = bf16[32,2,4096]{2,1,0:T(2,128)(2,1)S(1)} async-done(((bf16[32,2,4096]{2,1,0:T(2,128)(2,1)}), bf16[32,2,4096]{2,1,0:T(2,128)(2,1)S(1)}, u32[]{:S(2)}, u32[]{:S(2)}) %all-to-all-start.3) | async-done | bytes 524320 | tf_op jit(solution)/shard_map/all_to_all | solution.py:133
  209.1 0.5 reshape.1338
  210.1 0.9 copy.54
  (97 shorter events, 8.9 us)
Async XLA Ops:
  0.6 19.5 %copy-start.3 = (bf16[128,4,256]{2,1,0:T(4,128)(2,1)S(1)}, bf16[128,4,256]{2,1,0:T(4,128)(2,1)}, u32[]{:S(2)}) copy-start(bf16[128,4,256]{2,1,0:T(4,128)(2,1)} %param.10) | copy-start | bytes 786436
  0.6 19.6 %copy-start = (bf16[128,2048]{1,0:T(8,128)(2,1)S(1)}, bf16[128,2048]{1,0:T(8,128)(2,1)}, u32[]{:S(2)}) copy-start(bf16[128,2048]{1,0:T(8,128)(2,1)} %param.12) | copy-start | bytes 1572868
  0.7 20.7 %copy-start.4 = (bf16[1,32,4,256]{3,2,1,0:T(4,128)(2,1)S(1)}, bf16[1,32,4,256]{3,2,1,0:T(4,128)(2,1)}, u32[]{:S(2)}) copy-start(bf16[1,32,4,256]{3,2,1,0:T(4,128)(2,1)} %param.13) | copy-start | bytes 196612
  2.1 23.4 %all-to-all-start = ((bf16[8,32,256]{2,0,1:T(8,128)(2,1)}), bf16[8,32,256]{2,0,1:T(8,128)(2,1)S(1)}, u32[]{:S(2)}, u32[]{:S(2)}) async-start(bf16[8,32,256]{2,0,1:T(8,128)(2,1)} %bitcast), calls=%async_computation | async-start | bytes 262144 | tf_op jit(solution)/shard_map/all_to_all | solution.py:67
  19.1 14.6 %copy-start.5 = (s32[32]{0:T(128)S(1)}, s32[32]{0:T(128)}, u32[]{:S(2)}) copy-start(s32[32]{0:T(128)} %param.16) | copy-start | bytes 388
  19.1 14.7 %copy-start.6 = (s32[32]{0:T(128)S(1)}, s32[32]{0:T(128)}, u32[]{:S(2)}) copy-start(s32[32]{0:T(128)} %param.15) | copy-start | bytes 388
  19.1 14.9 %copy-start.7 = (s32[32]{0:T(128)S(1)}, s32[32]{0:T(128)}, u32[]{:S(2)}) copy-start(s32[32]{0:T(128)} %param.14) | copy-start | bytes 388
  25.6 24.0 %all-to-all-start.2 = ((bf16[64,32,128]{2,0,1:T(8,128)(2,1)}), bf16[64,32,128]{2,0,1:T(8,128)(2,1)S(1)}, u32[]{:S(2)}, u32[]{:S(2)}) async-start(bf16[64,32,128]{2,0,1:T(8,128)(2,1)} %bitcast.17), calls=%async_computation.2 | async-start | bytes 1048576 | tf_op jit(solution)/shard_map/all_to_all | solution.py:64
  49.5 21.8 %all-to-all-start.5 = ((bf16[64,32,128]{2,0,1:T(8,128)(2,1)}), bf16[64,32,128]{2,0,1:T(8,128)(2,1)S(1)}, u32[]{:S(2)}, u32[]{:S(2)}) async-start(bf16[64,32,128]{2,0,1:T(8,128)(2,1)} %bitcast.56), calls=%async_computation.5 | async-start | bytes 1048576 | tf_op jit(solution)/shard_map/all_to_all | solution.py:65
  72.2 21.4 %all-to-all-start.4 = ((bf16[32,32,256]{2,0,1:T(8,128)(2,1)}), bf16[32,32,256]{2,0,1:T(8,128)(2,1)S(1)}, u32[]{:S(2)}, u32[]{:S(2)}) async-start(bf16[32,32,256]{2,0,1:T(8,128)(2,1)} %bitcast.50), calls=%async_computation.4 | async-start | bytes 1048576 | tf_op jit(solution)/shard_map/all_to_all | solution.py:68
  93.5 1.6 copy-start.1
  95.1 54.4 %all-to-all-start.1 = ((bf16[128,32,256]{2,0,1:T(8,128)(2,1)}), bf16[128,32,256]{2,0,1:T(8,128)(2,1)S(1)}, u32[]{:S(2)}, u32[]{:S(2)}) async-start(bf16[128,32,256]{2,0,1:T(8,128)(2,1)} %bitcast.270), calls=%async_computation.1 | async-start | bytes 4194304 | tf_op jit(solution)/shard_map/all_to_all | solution.py:66
  100.4 1.5 copy-start.2
  149.5 34.1 %all-to-all-start.6 = ((bf16[32,2,4096]{2,1,0:T(2,128)(2,1)}), bf16[32,2,4096]{2,1,0:T(2,128)(2,1)S(1)}, u32[]{:S(2)}, u32[]{:S(2)}) async-start(bf16[32,2,4096]{2,1,0:T(2,128)(2,1)} %reshape.1339), calls=%async_computation.6 | async-start | bytes 1048576 | tf_op jit(solution)/shard_map/all_to_all | solution.py:134
  183.6 25.5 %all-to-all-start.3 = ((bf16[32,2,4096]{2,1,0:T(2,128)(2,1)}), bf16[32,2,4096]{2,1,0:T(2,128)(2,1)S(1)}, u32[]{:S(2)}, u32[]{:S(2)}) async-start(bf16[32,2,4096]{2,1,0:T(2,128)(2,1)} %reshape.1337), calls=%async_computation.3 | async-start | bytes 1048576 | tf_op jit(solution)/shard_map/all_to_all | solution.py:133
where the time goes:
time: 212 us; the launch traced here: 211 us
  waiting for transfers between devices  96.4 us (45%)
  starting transfers between devices  51.6 us (24%)
  other arithmetic  22.5 us (11%)
  matrix products  19.5 us (9%)
  local copies, waits for them, and re-layouts  19.2 us (9%)
    all_to_all x1, waiting for transfers between devices, shards(): lax.all_to_all(spread(stretch_kv), 'seq', split_axis=1, concat_axis=0, ti...  39.6 us
    all_to_all x1, waiting for transfers between devices, shards(): lax.all_to_all(head_split(cross_query), 'seq', split_axis=1, concat_axis=...  15.4 us
    all_to_all x1, waiting for transfers between devices, shards(): lax.all_to_all(head_split(text_query), 'seq', split_axis=1, concat_axis=0...  15.4 us
    all_to_all x1, waiting for transfers between devices, shards(): lax.all_to_all(self_heads, 'seq', split_axis=0, concat_axis=1, tiled=True)  13.9 us
    all_to_all x1, starting transfers between devices, shards(): lax.all_to_all(spread(cache_kv), 'seq', split_axis=1, concat_axis=0, tile...  13.2 us
    reduce_sum x8, other arithmetic, normalize(): jnp.sum(weights, axis=-1, keepdims=True) + jnp.where(present, 0.0, 1.0)  11.2 us
    all_to_all x1, starting transfers between devices, shards(): lax.all_to_all(self_heads, 'seq', split_axis=0, concat_axis=1, tiled=True)  9.62 us
    all_to_all x1, waiting for transfers between devices, shards(): lax.all_to_all(spread(own_image), 'seq', split_axis=1, concat_axis=0, til...  9.57 us
  transfers between devices with their start and end apart: 7, of which 6 were waited for; matrix products, arithmetic and copies ran while one was open for 26% of the time, Pallas kernels for 0%

commit v1 on v0

v1 whole, which is shorter than its diff:
```python
import functools
import math

import jax
import jax.numpy as jnp
from jax import lax
from jax.experimental import pallas as pl
from jax.experimental.pallas import tpu as pltpu
from jax.sharding import PartitionSpec as P

LOW_SCORE = -1e30
LOG2E = 1.4426950408889634
NT = (((1,), (1,)), ((), ()))
NN = (((1,), (0,)), ((), ()))


def self_kernel(
    steps,
    head_rows,
    cached_rows,
    place_ref,
    own_ref,
    *refs,
):
    pieces = refs[: len(steps)]
    out_ref, keys, values, peak, total = refs[len(steps) :]
    parts = own_ref.shape[0]
    width = own_ref.shape[2]
    rows = head_rows
    heads = out_ref.shape[2] // width
    ring = len(steps) + 1
    here = place_ref[0]
    cached = cached_rows * parts * ring
    stretch = rows * ring
    scale = LOG2E / math.sqrt(width)

    ones = jnp.ones((rows, width), jnp.bfloat16)
    for start in range(0, cached + parts * stretch, rows):
        values[pl.ds(start, rows), width:] = ones

    def place(ref, base, owner):
        for part in range(parts):
            spot = pl.multiple_of(cached + part * stretch + owner * rows, rows)
            keys[pl.ds(spot, rows), :] = ref[part, base : base + rows, :]
            values[pl.ds(spot, rows), :width] = ref[part, base + rows : base + 2 * rows, :]
        tails = [
            ref[part, base + 2 * rows : base + 2 * rows + 2 * cached_rows, :].astype(jnp.float32)
            for part in range(parts)
        ]
        count = cached_rows * parts
        spot = pl.multiple_of(owner * count, count)
        keys[pl.ds(spot, count), :] = jnp.concatenate(
            [tail[:cached_rows] for tail in tails], 0
        ).astype(jnp.bfloat16)
        values[pl.ds(spot, count), :width] = jnp.concatenate(
            [tail[cached_rows:] for tail in tails], 0
        ).astype(jnp.bfloat16)

    place(own_ref, heads * rows, here)
    for step, ref in zip(steps, pieces):
        place(ref, 0, lax.rem(here + step + ring, ring))

    def fold(part, start, count, mask, first=False):
        block_keys = keys[pl.ds(start, count), :]
        block_values = values[pl.ds(start, count), :]
        for head in range(heads):
            query = own_ref[part, head * rows : (head + 1) * rows, :]
            scores = lax.dot_general(query, block_keys, NT, preferred_element_type=jnp.float32)
            if mask is not None:
                scores = jnp.where(mask, scores, LOW_SCORE)
            highest = jnp.max(scores, axis=1, keepdims=True)
            if first:
                top = jnp.broadcast_to(highest, (rows, width))
            else:
                top = jnp.maximum(peak[head], highest)
            weights = jnp.exp2((scores - top[:, :1]) * scale)
            added = lax.dot_general(
                weights.astype(jnp.bfloat16), block_values, NN, preferred_element_type=jnp.float32
            )
            if first:
                total[head] = added
            else:
                fade = jnp.exp2((peak[head] - top) * scale)
                total[head] = total[head] * jnp.concatenate([fade, fade], 1) + added
            peak[head] = top

    for part in range(parts):
        fold(part, 0, cached, None, first=True)
        for chunk in range(part):
            fold(part, cached + chunk * stretch, stretch, None)
        base = cached + part * stretch
        pair = 2 * rows

        def step_body(index, carry):
            fold(part, pl.multiple_of(base + index * pair, rows), pair, None)
            return carry

        lax.fori_loop(0, here // 2, step_body, 0)
        last = (here // 2) * pair
        offset = here * rows - last
        column = lax.broadcasted_iota(jnp.int32, (rows, pair), 1)
        line = lax.broadcasted_iota(jnp.int32, (rows, pair), 0)
        fold(part, pl.multiple_of(base + last, rows), pair, column <= line + offset)
        for head in range(heads):
            result = total[head]
            out_ref[part, :, head * width : (head + 1) * width] = (
                result[:, :width] / result[:, width:]
            ).astype(jnp.bfloat16)


def cross_kernel(
    slots,
    span_ref,
    gate_ref,
    query_ref,
    before_ref,
    own_ref,
    out_ref,
):
    rows = query_ref.shape[0]
    width = query_ref.shape[1]
    kv_width = own_ref.shape[1]
    head_dim = 128
    kv_heads = kv_width // (2 * head_dim)
    group = width // head_dim // kv_heads
    gate = gate_ref[0]
    column = lax.broadcasted_iota(jnp.int32, (rows, 2 * slots), 1)
    line = lax.broadcasted_iota(jnp.int32, (rows, 2 * slots), 0) + span_ref[0]
    late = column >= slots
    start = jnp.where(late, span_ref[4], span_ref[1])
    stop = jnp.where(late, span_ref[5], span_ref[2])
    length = jnp.where(late, span_ref[6] + slots, span_ref[3])
    allowed = (start <= line) & (line < stop) & (column < length)
    scale = 1.0 / math.sqrt(head_dim)
    for kv_head in range(kv_heads):
        base = kv_head * 2 * head_dim
        image_keys = jnp.concatenate(
            [before_ref[:, base : base + head_dim], own_ref[:, base : base + head_dim]], 0
        )
        image_values = jnp.concatenate(
            [
                before_ref[:, base + head_dim : base + 2 * head_dim],
                own_ref[:, base + head_dim : base + 2 * head_dim],
            ],
            0,
        )
        for member in range(group):
            spot = (kv_head * group + member) * head_dim
            query = query_ref[:, spot : spot + head_dim]
            scores = lax.dot_general(query, image_keys, NT, preferred_element_type=jnp.float32)
            scores = jnp.where(allowed, scores * scale, LOW_SCORE)
            highest = jnp.max(scores, axis=1, keepdims=True)
            weights = jnp.where(allowed, jnp.exp(scores - highest), 0.0)
            sums = jnp.sum(weights, axis=1, keepdims=True)
            sums = jnp.where(sums > 0.0, sums, 1.0)
            context = lax.dot_general(
                (weights / sums).astype(jnp.bfloat16),
                image_values,
                NN,
                preferred_element_type=jnp.float32,
            )
            out_ref[:, spot : spot + head_dim] = (gate * context).astype(jnp.bfloat16)


def shards(
    text_query,
    stretch_kv,
    cache_kv,
    cross_query,
    image_kv,
    image_start,
    image_stop,
    image_lengths,
    cross_gate,
):
    devices = lax.axis_size("seq")
    me = lax.axis_index("seq")
    rows, query_width = text_query.shape
    kv_heads = stretch_kv.shape[1]
    head_dim = stretch_kv.shape[2] // 2
    group = query_width // head_dim // kv_heads
    ring = devices // kv_heads
    cached_rows = cache_kv.shape[0]
    slots = image_kv.shape[1]
    columns = [[part * ring + spot for part in range(kv_heads)] for spot in range(ring)]

    def shift(values, step):
        pairs = [
            (part * ring + spot, part * ring + (spot + step) % ring)
            for part in range(kv_heads)
            for spot in range(ring)
        ]
        return lax.ppermute(values, "seq", pairs)

    query = jnp.transpose(
        text_query.reshape(rows, kv_heads, group, head_dim), (1, 2, 0, 3)
    ).reshape(kv_heads, group * rows, head_dim)

    def halves(values):
        swapped = jnp.transpose(values, (1, 0, 2))
        return [swapped[:, :, :head_dim], swapped[:, :, head_dim:]]

    message = jnp.concatenate([query] + halves(stretch_kv) + halves(cache_kv), 1)
    arrived = lax.all_to_all(
        message, "seq", split_axis=0, concat_axis=0, axis_index_groups=columns, tiled=True
    )

    own_image = image_kv.reshape(slots, kv_heads * 2 * head_dim)
    image_before = lax.ppermute(own_image, "seq", [(i, i + 1) for i in range(devices - 1)])

    block = arrived[:, group * rows :, :]
    up, down = block, block
    pieces, steps = [], []
    for step in range(1, ring // 2):
        up, down = shift(up, 1), shift(down, -1)
        pieces += [up, down]
        steps += [-step, step]
    half = kv_heads // 2
    far_up, far_down = shift(up[:half], 1), shift(down[half:], -1)
    pieces.append(jnp.concatenate([far_up, far_down], 0))
    steps.append(ring // 2)

    total_keys = kv_heads * ring * (rows + cached_rows)
    vmem = pl.BlockSpec(memory_space=pltpu.VMEM)
    smem = pl.BlockSpec(memory_space=pltpu.SMEM)
    self_heads = pl.pallas_call(
        functools.partial(self_kernel, tuple(steps), rows, cached_rows),
        out_shape=jax.ShapeDtypeStruct((kv_heads, rows, group * head_dim), jnp.bfloat16),
        in_specs=[smem] + [vmem] * (1 + len(pieces)),
        out_specs=vmem,
        scratch_shapes=[
            pltpu.VMEM((total_keys, head_dim), jnp.bfloat16),
            pltpu.VMEM((total_keys, 2 * head_dim), jnp.bfloat16),
            pltpu.VMEM((group, rows, head_dim), jnp.float32),
            pltpu.VMEM((group, rows, 2 * head_dim), jnp.float32),
        ],
        compiler_params=pltpu.CompilerParams(vmem_limit_bytes=48 * 2**20),
        name="self_attention",
    )((me % ring).reshape(1), arrived, *pieces)

    before = jnp.maximum(me - 1, 0)
    spans = jnp.stack(
        [
            me * rows,
            image_start[before],
            jnp.where(me > 0, image_stop[before], 0),
            image_lengths[before],
            image_start[me],
            image_stop[me],
            image_lengths[me],
        ]
    ).astype(jnp.int32)
    cross_context = pl.pallas_call(
        functools.partial(cross_kernel, slots),
        out_shape=jax.ShapeDtypeStruct(cross_query.shape, jnp.bfloat16),
        in_specs=[smem, smem, vmem, vmem, vmem],
        out_specs=vmem,
        compiler_params=pltpu.CompilerParams(vmem_limit_bytes=16 * 2**20),
        cost_estimate=pl.CostEstimate(
            flops=40_000_000, bytes_accessed=1_200_000, transcendentals=200_000
        ),
        name="cross_attention",
    )(spans, jnp.tanh(cross_gate), cross_query, image_before, own_image)

    returned = lax.all_to_all(
        self_heads, "seq", split_axis=0, concat_axis=0, axis_index_groups=columns, tiled=True
    )
    self_context = jnp.transpose(returned, (1, 0, 2)).reshape(rows, query_width)
    return (self_context, cross_context)


def solution(mesh):
    in_specs = (
        P(("doc", "seq"), None),
        P(("doc", "seq"), None, None),
        P(("doc", "seq"), None, None),
        P(("doc", "seq"), None),
        P(("doc", "seq"), None, None, None),
        P("doc"),
        P("doc"),
        P("doc"),
        P("doc"),
    )
    out_specs = (P(("doc", "seq"), None), P(("doc", "seq"), None))
    return jax.shard_map(shards, mesh=mesh, in_specs=in_specs, out_specs=out_specs, check_vma=False)
```

time: 212 us -> 101 us (0.48)
  the two profiles are of different devices: /device:TPU:56 before, /device:TPU:54 now
where the time goes in v1:
time: 101 us
  starting transfers between devices  41.6 us (41%)
  waiting for transfers between devices  20.4 us (20%)
  blocking collectives  15 us (15%)
  Pallas kernels  12.5 us (12%)
  local copies, waits for them, and re-layouts  8.9 us (9%)
  between operations  2.18 us (2%)
    ppermute x8, starting transfers between devices, shift(): return lax.ppermute(values, 'seq', pairs)  34 us
    all_to_all x1, blocking collectives, shards(): lax.all_to_all(message, 'seq', split_axis=0, concat_axis=0, axis_index_gr...  15 us
    ppermute x8, waiting for transfers between devices, shift(): return lax.ppermute(values, 'seq', pairs)  11.2 us
    pallas_call x1, Pallas kernels, shards(): pl.pallas_call(functools.partial(self_kernel, tuple(steps), rows, cached_...  9.97 us
    ppermute x1, waiting for transfers between devices, shards(): lax.ppermute(own_image, 'seq', [(i, i + 1) for i in range(devices - 1)])  9.22 us
    all_to_all x1, starting transfers between devices, shards(): lax.all_to_all(self_heads, 'seq', split_axis=0, concat_axis=0, axis_index...  5.64 us
    unnamed x22, local copies, waits for them, and re-layouts  3.55 us
    another operation x1, local copies, waits for them, and re-layouts, shards(): jnp.stack([me * rows, image_start[before], jnp.where(me > 0, image_stop[b...  3.2 us
  transfers between devices with their start and end apart: 10, of which 6 were waited for; matrix products, arithmetic and copies ran while one was open for 5% of the time, Pallas kernels for 2%

profile of v1, /device:TPU:54, one launch (start us, length us, event | category | flops | bytes accessed | tf_op | source)
XLA Modules:
  0.0 100.5 jit_solution(16047396897817584279)
XLA Ops:
  0.6 0.0 copy-start.1
  0.6 1.0 %copy.22 = bf16[128,4,256]{2,0,1:T(8,128)(2,1)S(1)} copy(bf16[128,4,256]{2,1,0:T(4,128)(2,1)} %param.10) | data formatting | bytes 524288 | tf_op args[1]
  1.7 0.1 copy-done.1
  1.8 0.4 reshape.20
  2.1 0.1 copy.14
  2.3 0.0 copy-start.3
  2.4 0.7 copy-done.3
  3.1 15.0 %all_to_all.10.own_ref = bf16[4,784,128]{2,1,0:T(8,128)(2,1)S(1)} all-to-all(bf16[4,784,128]{2,1,0:T(8,128)(2,1)S(1)} %constant_dynamic-update-slice_fusion), channel_id=1, replica_groups={{0,8,16,24},{1,9,17,25},{2,10,18,26},{3,11,19,27},{4,12,20,28},{5,13,21..., dimensions={0} | all-to-all | bytes 1605632 | tf_op jit(solution)/shard_map/all_to_all | solution.py:204
  18.1 4.3 %collective-permute-start = (bf16[4,272,128]{2,1,0:T(8,128)(2,1)S(1)}, bf16[4,272,128]{2,1,0:T(8,128)(2,1)S(1)}, u32[]{:S(2)}, u32[]{:S(2)}) collective-permute-start(bf16[4,272,128]{2,1,0:T(8,128)(2,1)S(1)} %slice.32), channel_id=1, source_target_pairs={{0,1},{1,2},{2,3},{3,4},{4,5},{5,6},{6,7},{7,0},{8,9},{9,10},{10,1... | collective-permute-start | bytes 835592 | tf_op jit(solution)/shard_map/ppermute | solution.py:193
  22.4 8.6 %collective-permute-start.1 = (bf16[4,272,128]{2,1,0:T(8,128)(2,1)S(1)}, bf16[4,272,128]{2,1,0:T(8,128)(2,1)S(1)}, u32[]{:S(2)}, u32[]{:S(2)}) collective-permute-start(bf16[4,272,128]{2,1,0:T(8,128)(2,1)S(1)} %slice.32), channel_id=1, source_target_pairs={{0,7},{1,0},{2,1},{3,2},{4,3},{5,4},{6,5},{7,6},{8,15},{9,8},{10,9... | collective-permute-start | bytes 835592 | tf_op jit(solution)/shard_map/ppermute | solution.py:193
  31.0 3.5 %collective-permute-done.refs_0_ = bf16[4,272,128]{2,1,0:T(8,128)(2,1)S(1)} collective-permute-done((bf16[4,272,128]{2,1,0:T(8,128)(2,1)S(1)}, bf16[4,272,128]{2,1,0:T(8,128)(2,1)S(1)}, u32[]{:S(2)}, u32[]{:S(2)}) %collective-permute-start) | collective-permute-done | bytes 278560 | tf_op jit(solution)/shard_map/ppermute | solution.py:193
  34.4 1.9 %collective-permute-start.2 = (bf16[4,272,128]{2,1,0:T(8,128)(2,1)S(1)}, bf16[4,272,128]{2,1,0:T(8,128)(2,1)S(1)}, u32[]{:S(2)}, u32[]{:S(2)}) collective-permute-start(bf16[4,272,128]{2,1,0:T(8,128)(2,1)S(1)} %collective-permute-done.refs_0_), channel_id=1, source_target_pairs={{0,1},{1,2},{2,3},{3,4},{4,5},{5,6},{6,7},{7,0},{8,9},{9,10},{10,1... | collective-permute-start | bytes 835592 | tf_op jit(solution)/shard_map/ppermute | solution.py:193
  36.4 0.0 collective-permute-done.1.refs_1_
  36.4 5.1 %collective-permute-start.3 = (bf16[4,272,128]{2,1,0:T(8,128)(2,1)S(1)}, bf16[4,272,128]{2,1,0:T(8,128)(2,1)S(1)}, u32[]{:S(2)}, u32[]{:S(2)}) collective-permute-start(bf16[4,272,128]{2,1,0:T(8,128)(2,1)S(1)} %collective-permute-done.1.refs_1_), channel_id=1, source_target_pairs={{0,7},{1,0},{2,1},{3,2},{4,3},{5,4},{6,5},{7,6},{8,15},{9,8},{10,9... | collective-permute-start | bytes 835592 | tf_op jit(solution)/shard_map/ppermute | solution.py:193
  41.5 2.6 %collective-permute-done.2.refs_2_ = bf16[4,272,128]{2,1,0:T(8,128)(2,1)S(1)} collective-permute-done((bf16[4,272,128]{2,1,0:T(8,128)(2,1)S(1)}, bf16[4,272,128]{2,1,0:T(8,128)(2,1)S(1)}, u32[]{:S(2)}, u32[]{:S(2)}) %collective-permute-start.2) | collective-permute-done | bytes 278560 | tf_op jit(solution)/shard_map/ppermute | solution.py:193
  44.1 1.9 %collective-permute-start.4 = (bf16[4,272,128]{2,1,0:T(8,128)(2,1)S(1)}, bf16[4,272,128]{2,1,0:T(8,128)(2,1)S(1)}, u32[]{:S(2)}, u32[]{:S(2)}) collective-permute-start(bf16[4,272,128]{2,1,0:T(8,128)(2,1)S(1)} %collective-permute-done.2.refs_2_), channel_id=1, source_target_pairs={{0,1},{1,2},{2,3},{3,4},{4,5},{5,6},{6,7},{7,0},{8,9},{9,10},{10,1... | collective-permute-start | bytes 835592 | tf_op jit(solution)/shard_map/ppermute | solution.py:193
  46.0 0.0 collective-permute-done.3.refs_3_
  46.0 5.1 %collective-permute-start.5 = (bf16[4,272,128]{2,1,0:T(8,128)(2,1)S(1)}, bf16[4,272,128]{2,1,0:T(8,128)(2,1)S(1)}, u32[]{:S(2)}, u32[]{:S(2)}) collective-permute-start(bf16[4,272,128]{2,1,0:T(8,128)(2,1)S(1)} %collective-permute-done.3.refs_3_), channel_id=1, source_target_pairs={{0,7},{1,0},{2,1},{3,2},{4,3},{5,4},{6,5},{7,6},{8,15},{9,8},{10,9... | collective-permute-start | bytes 835592 | tf_op jit(solution)/shard_map/ppermute | solution.py:193
  51.1 2.6 %collective-permute-done.4.refs_4_ = bf16[4,272,128]{2,1,0:T(8,128)(2,1)S(1)} collective-permute-done((bf16[4,272,128]{2,1,0:T(8,128)(2,1)S(1)}, bf16[4,272,128]{2,1,0:T(8,128)(2,1)S(1)}, u32[]{:S(2)}, u32[]{:S(2)}) %collective-permute-start.4) | collective-permute-done | bytes 278560 | tf_op jit(solution)/shard_map/ppermute | solution.py:193
  53.7 1.9 %collective-permute-start.6 = (bf16[2,272,128]{2,1,0:T(8,128)(2,1)S(1)}, bf16[2,272,128]{2,1,0:T(8,128)(2,1)S(1)}, u32[]{:S(2)}, u32[]{:S(2)}) collective-permute-start(bf16[2,272,128]{2,1,0:T(8,128)(2,1)S(1)} %slice.33), channel_id=1, source_target_pairs={{0,1},{1,2},{2,3},{3,4},{4,5},{5,6},{6,7},{7,0},{8,9},{9,10},{10,1... | collective-permute-start | bytes 417800 | tf_op jit(solution)/shard_map/ppermute | solution.py:193
  55.7 0.0 collective-permute-done.5.refs_5_
  55.7 5.1 %collective-permute-start.7 = (bf16[2,272,128]{2,1,0:T(8,128)(2,1)S(1)}, bf16[2,272,128]{2,1,0:T(8,128)(2,1)S(1)}, u32[]{:S(2)}, u32[]{:S(2)}) collective-permute-start(bf16[2,272,128]{2,1,0:T(8,128)(2,1)S(1)} %slice.34), channel_id=1, source_target_pairs={{0,7},{1,0},{2,1},{3,2},{4,3},{5,4},{6,5},{7,6},{8,15},{9,8},{10,9... | collective-permute-start | bytes 417800 | tf_op jit(solution)/shard_map/ppermute | solution.py:193
  60.8 1.0 %collective-permute-done.6 = bf16[2,272,128]{2,1,0:T(8,128)(2,1)S(1)} collective-permute-done((bf16[2,272,128]{2,1,0:T(8,128)(2,1)S(1)}, bf16[2,272,128]{2,1,0:T(8,128)(2,1)S(1)}, u32[]{:S(2)}, u32[]{:S(2)}) %collective-permute-start.6) | collective-permute-done | bytes 139296 | tf_op jit(solution)/shard_map/ppermute | solution.py:193
  61.9 1.5 %collective-permute-done.7 = bf16[2,272,128]{2,1,0:T(8,128)(2,1)S(1)} collective-permute-done((bf16[2,272,128]{2,1,0:T(8,128)(2,1)S(1)}, bf16[2,272,128]{2,1,0:T(8,128)(2,1)S(1)}, u32[]{:S(2)}, u32[]{:S(2)}) %collective-permute-start.7) | collective-permute-done | bytes 139296 | tf_op jit(solution)/shard_map/ppermute | solution.py:193
  63.4 10.0 %self_attention.1 = bf16[4,128,512]{2,1,0:T(8,128)(2,1)} custom-call(s32[1]{0:T(128)} %bitcast.place_ref, bf16[4,784,128]{2,1,0:T(8,128)(2,1)S(1)} %all_to_all.10.own_ref, bf16[4,272,128]{2,1,0:T(8,128)(2,1)S(1)} %collective-permute-done.refs_0_, bf16[4,272,128]{2,1,0:T(8,128)(2,1)S(1)} %collective-permute-done.1.refs_1_, ...), custom_call_target="tpu_custom_call" | custom-call | tf_op jit(solution)/shard_map/self_attention/pallas_call | solution.py:226
  73.4 0.0 copy-start.2
  73.4 0.0 copy-start
  73.4 5.6 %all-to-all-start.1 = ((bf16[4,128,512]{2,1,0:T(8,128)(2,1)}), bf16[4,128,512]{2,1,0:T(8,128)(2,1)S(1)}, u32[]{:S(2)}, u32[]{:S(2)}) async-start(bf16[4,128,512]{2,1,0:T(8,128)(2,1)} %self_attention.1), calls=%async_computation.1 | async-start | bytes 1048576 | tf_op jit(solution)/shard_map/all_to_all | solution.py:265
  79.1 0.0 copy-done.2
  79.1 0.0 copy-start.6
  79.1 1.9 %collective-permute-start.8 = (bf16[32,1024]{1,0:T(8,128)(2,1)S(1)}, bf16[32,1024]{1,0:T(8,128)(2,1)S(1)}, u32[]{:S(2)}, u32[]{:S(2)}) collective-permute-start(bf16[32,1024]{1,0:T(8,128)(2,1)S(1)} %bitcast.18), channel_id=1, source_target_pairs={{0,1},{1,2},{2,3},{3,4},{4,5},{5,6},{6,7},{7,8},{8,9},{9,10},{10,1... | collective-permute-start | bytes 196616 | tf_op jit(solution)/shard_map/ppermute | solution.py:209
  81.7 0.0 copy-start.4
  81.7 0.0 copy-start.5
  81.7 0.6 copy-done.4
  82.3 0.0 copy-done.5
  82.3 0.7 fusion
  83.6 0.0 copy-done.6
  83.6 0.7 fusion.2
  84.3 3.2 %stack.11.span_ref = s32[7]{0:T(128)S(1)} concatenate(s32[1]{0:T(128)} %bitcast.7, s32[1]{0:T(128)} %get-tuple-element.9, s32[1]{0:T(128)} %bitcast.9, s32[1]{0:T(128)} %get-tuple-element.5, s32[1]{0:T(128)} %get-tuple-element.8, s32[1]{0:T(128)} %get-tuple-element.11, s32[1]{0:T(128)} %get-tuple-element.4), dimensions={0} | concatenate | bytes 56 | tf_op jit(solution)/shard_map/stack | solution.py:242
  87.5 9.2 %collective-permute-done.8.before_ref = bf16[32,1024]{1,0:T(8,128)(2,1)S(1)} collective-permute-done((bf16[32,1024]{1,0:T(8,128)(2,1)S(1)}, bf16[32,1024]{1,0:T(8,128)(2,1)S(1)}, u32[]{:S(2)}, u32[]{:S(2)}) %collective-permute-start.8) | collective-permute-done | bytes 65568 | tf_op jit(solution)/shard_map/ppermute | solution.py:209
  96.7 0.0 copy-done
  96.7 2.5 %cross_attention.1 = bf16[128,2048]{1,0:T(8,128)(2,1)} custom-call(s32[7]{0:T(128)S(1)} %stack.11.span_ref, f32[1]{0:T(128)S(6)} %tanh.3.gate_ref, bf16[128,2048]{1,0:T(8,128)(2,1)S(1)} %copy-done, bf16[32,1024]{1,0:T(8,128)(2,1)S(1)} %collective-permute-done.8.before_ref, bf16[32,1024]{1,0:T(8,128)(2,1)S(1)} %bitcast.19), custom_call_target="tpu_custom_call" | custom-call | flops 40000000 | bytes 1200000 | tf_op jit(solution)/shard_map/cross_attention/pallas_call | solution.py:253
  99.2 0.0 all-to-all-done.1
  99.2 0.3 copy.17
  99.5 1.0 %copy.18 = bf16[128,2048]{1,0:T(8,128)(2,1)} copy(bf16[128,2048]{0,1:T(8,128)(2,1)S(1)} %bitcast.22) | data formatting | bytes 1048576
  (11 shorter events, 0.2 us)
Async XLA Ops:
  0.6 1.1 %copy-start.1 = (bf16[128,2048]{1,0:T(8,128)(2,1)S(1)}, bf16[128,2048]{1,0:T(8,128)(2,1)}, u32[]{:S(2)}) copy-start(bf16[128,2048]{1,0:T(8,128)(2,1)} %param.9) | copy-start | bytes 1572868
  2.3 0.7 copy-start.3
  18.1 16.4 %collective-permute-start = (bf16[4,272,128]{2,1,0:T(8,128)(2,1)S(1)}, bf16[4,272,128]{2,1,0:T(8,128)(2,1)S(1)}, u32[]{:S(2)}, u32[]{:S(2)}) collective-permute-start(bf16[4,272,128]{2,1,0:T(8,128)(2,1)S(1)} %slice.32), channel_id=1, source_target_pairs={{0,1},{1,2},{2,3},{3,4},{4,5},{5,6},{6,7},{7,0},{8,9},{9,10},{10,1... | collective-permute-start | bytes 835592 | tf_op jit(solution)/shard_map/ppermute | solution.py:193
  22.4 14.0 %collective-permute-start.1 = (bf16[4,272,128]{2,1,0:T(8,128)(2,1)S(1)}, bf16[4,272,128]{2,1,0:T(8,128)(2,1)S(1)}, u32[]{:S(2)}, u32[]{:S(2)}) collective-permute-start(bf16[4,272,128]{2,1,0:T(8,128)(2,1)S(1)} %slice.32), channel_id=1, source_target_pairs={{0,7},{1,0},{2,1},{3,2},{4,3},{5,4},{6,5},{7,6},{8,15},{9,8},{10,9... | collective-permute-start | bytes 835592 | tf_op jit(solution)/shard_map/ppermute | solution.py:193
  34.4 9.6 %collective-permute-start.2 = (bf16[4,272,128]{2,1,0:T(8,128)(2,1)S(1)}, bf16[4,272,128]{2,1,0:T(8,128)(2,1)S(1)}, u32[]{:S(2)}, u32[]{:S(2)}) collective-permute-start(bf16[4,272,128]{2,1,0:T(8,128)(2,1)S(1)} %collective-permute-done.refs_0_), channel_id=1, source_target_pairs={{0,1},{1,2},{2,3},{3,4},{4,5},{5,6},{6,7},{7,0},{8,9},{9,10},{10,1... | collective-permute-start | bytes 835592 | tf_op jit(solution)/shard_map/ppermute | solution.py:193
  36.4 9.6 %collective-permute-start.3 = (bf16[4,272,128]{2,1,0:T(8,128)(2,1)S(1)}, bf16[4,272,128]{2,1,0:T(8,128)(2,1)S(1)}, u32[]{:S(2)}, u32[]{:S(2)}) collective-permute-start(bf16[4,272,128]{2,1,0:T(8,128)(2,1)S(1)} %collective-permute-done.1.refs_1_), channel_id=1, source_target_pairs={{0,7},{1,0},{2,1},{3,2},{4,3},{5,4},{6,5},{7,6},{8,15},{9,8},{10,9... | collective-permute-start | bytes 835592 | tf_op jit(solution)/shard_map/ppermute | solution.py:193
  44.1 9.6 %collective-permute-start.4 = (bf16[4,272,128]{2,1,0:T(8,128)(2,1)S(1)}, bf16[4,272,128]{2,1,0:T(8,128)(2,1)S(1)}, u32[]{:S(2)}, u32[]{:S(2)}) collective-permute-start(bf16[4,272,128]{2,1,0:T(8,128)(2,1)S(1)} %collective-permute-done.2.refs_2_), channel_id=1, source_target_pairs={{0,1},{1,2},{2,3},{3,4},{4,5},{5,6},{6,7},{7,0},{8,9},{9,10},{10,1... | collective-permute-start | bytes 835592 | tf_op jit(solution)/shard_map/ppermute | solution.py:193
  46.0 9.7 %collective-permute-start.5 = (bf16[4,272,128]{2,1,0:T(8,128)(2,1)S(1)}, bf16[4,272,128]{2,1,0:T(8,128)(2,1)S(1)}, u32[]{:S(2)}, u32[]{:S(2)}) collective-permute-start(bf16[4,272,128]{2,1,0:T(8,128)(2,1)S(1)} %collective-permute-done.3.refs_3_), channel_id=1, source_target_pairs={{0,7},{1,0},{2,1},{3,2},{4,3},{5,4},{6,5},{7,6},{8,15},{9,8},{10,9... | collective-permute-start | bytes 835592 | tf_op jit(solution)/shard_map/ppermute | solution.py:193
  53.7 8.2 %collective-permute-start.6 = (bf16[2,272,128]{2,1,0:T(8,128)(2,1)S(1)}, bf16[2,272,128]{2,1,0:T(8,128)(2,1)S(1)}, u32[]{:S(2)}, u32[]{:S(2)}) collective-permute-start(bf16[2,272,128]{2,1,0:T(8,128)(2,1)S(1)} %slice.33), channel_id=1, source_target_pairs={{0,1},{1,2},{2,3},{3,4},{4,5},{5,6},{6,7},{7,0},{8,9},{9,10},{10,1... | collective-permute-start | bytes 417800 | tf_op jit(solution)/shard_map/ppermute | solution.py:193
  55.7 7.7 %collective-permute-start.7 = (bf16[2,272,128]{2,1,0:T(8,128)(2,1)S(1)}, bf16[2,272,128]{2,1,0:T(8,128)(2,1)S(1)}, u32[]{:S(2)}, u32[]{:S(2)}) collective-permute-start(bf16[2,272,128]{2,1,0:T(8,128)(2,1)S(1)} %slice.34), channel_id=1, source_target_pairs={{0,7},{1,0},{2,1},{3,2},{4,3},{5,4},{6,5},{7,6},{8,15},{9,8},{10,9... | collective-permute-start | bytes 417800 | tf_op jit(solution)/shard_map/ppermute | solution.py:193
  73.4 5.7 %copy-start.2 = (bf16[1,32,4,256]{3,2,1,0:T(4,128)(2,1)S(1)}, bf16[1,32,4,256]{3,2,1,0:T(4,128)(2,1)}, u32[]{:S(2)}) copy-start(bf16[1,32,4,256]{3,2,1,0:T(4,128)(2,1)} %param.13) | copy-start | bytes 196612
  73.4 23.3 %copy-start = (bf16[128,2048]{1,0:T(8,128)(2,1)S(1)}, bf16[128,2048]{1,0:T(8,128)(2,1)}, u32[]{:S(2)}) copy-start(bf16[128,2048]{1,0:T(8,128)(2,1)} %query_ref.1) | copy-start | bytes 1572868
  73.4 25.8 %all-to-all-start.1 = ((bf16[4,128,512]{2,1,0:T(8,128)(2,1)}), bf16[4,128,512]{2,1,0:T(8,128)(2,1)S(1)}, u32[]{:S(2)}, u32[]{:S(2)}) async-start(bf16[4,128,512]{2,1,0:T(8,128)(2,1)} %self_attention.1), calls=%async_computation.1 | async-start | bytes 1048576 | tf_op jit(solution)/shard_map/all_to_all | solution.py:265
  79.1 4.6 %copy-start.6 = (s32[32]{0:T(128)S(1)}, s32[32]{0:T(128)}, u32[]{:S(2)}) copy-start(s32[32]{0:T(128)} %param.14) | copy-start | bytes 388
  79.1 17.6 %collective-permute-start.8 = (bf16[32,1024]{1,0:T(8,128)(2,1)S(1)}, bf16[32,1024]{1,0:T(8,128)(2,1)S(1)}, u32[]{:S(2)}, u32[]{:S(2)}) collective-permute-start(bf16[32,1024]{1,0:T(8,128)(2,1)S(1)} %bitcast.18), channel_id=1, source_target_pairs={{0,1},{1,2},{2,3},{3,4},{4,5},{5,6},{6,7},{7,8},{8,9},{9,10},{10,1... | collective-permute-start | bytes 196616 | tf_op jit(solution)/shard_map/ppermute | solution.py:209
  81.7 0.7 copy-start.4
  81.7 0.7 copy-start.5

commit v2 on v1

v2 whole, which is shorter than its diff:
```python
import functools
import math

import jax
import jax.numpy as jnp
from jax import lax
from jax.experimental import pallas as pl
from jax.experimental.pallas import tpu as pltpu
from jax.sharding import PartitionSpec as P

LOW_SCORE = -1e30
LOG2E = 1.4426950408889634
MOST_TILES = 8
NT = (((1,), (1,)), ((), ()))
NN = (((1,), (0,)), ((), ()))


def pack_kernel(query_ref, stretch_ref, cache_ref, out_ref):
    rows = query_ref.shape[0]
    parts, _, width = out_ref.shape
    heads = query_ref.shape[1] // width // parts
    for part in range(parts):
        for head in range(heads):
            spot = (part * heads + head) * width
            out_ref[part, head * rows : (head + 1) * rows, :] = query_ref[:, spot : spot + width]
        base = heads * rows
        both = stretch_ref[:, part, :]
        out_ref[part, base : base + rows, :] = both[:, :width]
        out_ref[part, base + rows : base + 2 * rows, :] = both[:, width:]
        both = cache_ref[:, part, :].astype(jnp.float32)
        out_ref[part, base + 2 * rows :, :] = jnp.concatenate(
            [both[:, :width], both[:, width:]], 0
        ).astype(jnp.bfloat16)


def split(low, high):
    tiles = (high - low) // 128
    count = -(-tiles // MOST_TILES)
    edges = [low + 128 * (tiles * number // count) for number in range(count)] + [high]
    return list(zip(edges[:-1], edges[1:]))


def self_kernel(
    steps,
    counts,
    rows,
    ring,
    cached_rows,
    first,
    last,
    hold,
    caches,
    me_ref,
    own_ref,
    *refs,
):
    parts, _, width = own_ref.shape
    tail = 2 * cached_rows
    lines = own_ref.shape[1] - 2 * rows - tail
    heads = lines // rows
    here = lax.rem(me_ref[0], ring)
    scale = LOG2E / math.sqrt(width)
    refs = list(refs)

    def take(count):
        taken = refs[:count]
        del refs[:count]
        return taken

    pieces = [take(count) for count in counts]
    carried_caches = take(caches)
    carried = [] if first else take(3)
    if last:
        (out_ref,) = take(1)
    else:
        out_total, out_peak, out_sums = take(3)
    if hold:
        (out_cache,) = take(1)
    keys, values = refs

    sources = []
    for piece in pieces:
        if piece:
            sources.append([(ref, index, 0) for ref in piece for index in range(ref.shape[0])])
        else:
            sources.append([(own_ref, index, lines) for index in range(parts)])

    count = cached_rows * parts
    present = 0 if hold else count * len(steps) + sum(ref.shape[1] for ref in carried_caches)
    cached = -(-present // rows) * rows
    stretch = rows * len(steps)
    ones = jnp.ones((rows, width), jnp.bfloat16)
    for start in range(0, cached + parts * stretch, rows):
        values[start : start + rows, width:] = ones
    found = []
    for number, source in enumerate(sources):
        tails = []
        for part, (ref, index, base) in enumerate(source):
            place = cached + part * stretch + number * rows
            keys[place : place + rows, :] = ref[index, base : base + rows, :]
            values[place : place + rows, :width] = ref[index, base + rows : base + 2 * rows, :]
            tails.append(ref[index, base + 2 * rows : base + 2 * rows + tail, :].astype(jnp.float32))
        found.append(
            [
                jnp.concatenate([both[:cached_rows] for both in tails], 0).astype(jnp.bfloat16),
                jnp.concatenate([both[cached_rows:] for both in tails], 0).astype(jnp.bfloat16),
            ]
        )
    if hold:
        for number, pair in enumerate(found):
            for side in range(2):
                out_cache[side, number * count : (number + 1) * count, :] = pair[side]
    else:
        found += [(ref[0], ref[1]) for ref in carried_caches]
        place = 0
        for cache_keys, cache_values in found:
            size = cache_keys.shape[0]
            keys[place : place + size, :] = cache_keys
            values[place : place + size, :width] = cache_values
            place += size
        if place < cached:
            blank = jnp.zeros((cached - place, width), jnp.bfloat16)
            keys[place:cached, :] = blank
            values[place:cached, :width] = blank
    lane = lax.broadcasted_iota(jnp.int32, (1, rows), 1)
    edge = jnp.where(lane < present - (cached - rows), 0.0, LOW_SCORE)

    shifts = []
    for step in steps:
        if step == 0:
            line = lax.broadcasted_iota(jnp.int32, (lines, rows), 0) % rows
            column = lax.broadcasted_iota(jnp.int32, (lines, rows), 1)
            shifts.append(jnp.where(column <= line, 0.0, LOW_SCORE))
        else:
            owner = lax.rem(here + step + ring, ring)
            shifts.append(jnp.where(owner < here, 0.0, LOW_SCORE))

    for part in range(parts):
        query = own_ref[part, :lines, :]
        peak, total = None, None
        if not first:
            total = jnp.concatenate([carried[0][part], carried[2][part]], 1)
            peak = carried[1][part]
        full = cached + part * stretch
        chunks = split(0, full + stretch)
        if first:
            chunks = chunks[::-1]
        for low, high in chunks:
            scores = lax.dot_general(
                query, keys[low:high, :], NT, preferred_element_type=jnp.float32
            )
            tiles = []
            for spot in range(low, high, rows):
                tile = scores[:, spot - low : spot - low + rows] * scale
                if spot >= full:
                    tile = tile + shifts[(spot - full) // rows]
                elif spot == cached - rows and present < cached:
                    tile = tile + edge
                tiles.append(tile)
            top = jnp.max(functools.reduce(jnp.maximum, tiles), axis=1, keepdims=True)
            top = jnp.broadcast_to(top, (lines, width))
            if peak is not None:
                top = jnp.maximum(peak, top)
            weights = jnp.concatenate([jnp.exp2(tile - top) for tile in tiles], 1)
            added = lax.dot_general(
                weights.astype(jnp.bfloat16),
                values[low:high, :],
                NN,
                preferred_element_type=jnp.float32,
            )
            if peak is None:
                total = added
            else:
                fade = jnp.exp2(peak - top)
                total = total * jnp.concatenate([fade, fade], 1) + added
            peak = top
        if last:
            result = (total[:, :width] / total[:, width:]).astype(jnp.bfloat16)
            for head in range(heads):
                out_ref[part, :, head * width : (head + 1) * width] = result[
                    head * rows : (head + 1) * rows
                ]
        else:
            out_total[part] = total[:, :width]
            out_sums[part] = total[:, width:]
            out_peak[part] = peak


def cross_kernel(
    slots,
    me_ref,
    start_ref,
    stop_ref,
    length_ref,
    gate_ref,
    query_ref,
    before_ref,
    own_ref,
    out_ref,
):
    rows = query_ref.shape[0]
    width = query_ref.shape[1]
    kv_heads = own_ref.shape[1]
    head_dim = own_ref.shape[2] // 2
    group = width // head_dim // kv_heads
    me = me_ref[0]
    before = jnp.maximum(me - 1, 0)
    before_stop = jnp.where(me > 0, stop_ref[before], 0)
    gate = jnp.tanh(jnp.full((rows, head_dim), gate_ref[0], jnp.float32))
    column = lax.broadcasted_iota(jnp.int32, (rows, 2 * slots), 1)
    line = lax.broadcasted_iota(jnp.int32, (rows, 2 * slots), 0) + me * rows
    late = column >= slots
    start = jnp.where(late, start_ref[me], start_ref[before])
    stop = jnp.where(late, stop_ref[me], before_stop)
    length = jnp.where(late, length_ref[me] + slots, length_ref[before])
    allowed = (start <= line) & (line < stop) & (column < length)
    scale = 1.0 / math.sqrt(head_dim)
    for kv_head in range(kv_heads):
        image = jnp.concatenate([before_ref[:, kv_head, :], own_ref[:, kv_head, :]], 0)
        image_keys = image[:, :head_dim]
        image_values = image[:, head_dim:]
        for member in range(group):
            spot = (kv_head * group + member) * head_dim
            query = query_ref[:, spot : spot + head_dim]
            scores = lax.dot_general(query, image_keys, NT, preferred_element_type=jnp.float32)
            scores = jnp.where(allowed, scores * scale, LOW_SCORE)
            highest = jnp.max(scores, axis=1, keepdims=True)
            weights = jnp.where(allowed, jnp.exp(scores - highest), 0.0)
            sums = jnp.sum(weights, axis=1, keepdims=True)
            sums = jnp.where(sums > 0.0, sums, 1.0)
            context = lax.dot_general(
                (weights / sums).astype(jnp.bfloat16),
                image_values,
                NN,
                preferred_element_type=jnp.float32,
            )
            out_ref[:, spot : spot + head_dim] = (gate * context).astype(jnp.bfloat16)


def shards(
    text_query,
    stretch_kv,
    cache_kv,
    cross_query,
    image_kv,
    image_start,
    image_stop,
    image_lengths,
    cross_gate,
):
    devices = lax.axis_size("seq")
    me = lax.axis_index("seq")
    rows, query_width = text_query.shape
    kv_heads = stretch_kv.shape[1]
    head_dim = stretch_kv.shape[2] // 2
    group = query_width // head_dim // kv_heads
    ring = devices // kv_heads
    cached_rows = cache_kv.shape[0]
    slots = image_kv.shape[1]
    columns = [[part * ring + spot for part in range(kv_heads)] for spot in range(ring)]

    def shift(values, step):
        pairs = [
            (part * ring + spot, part * ring + (spot + step) % ring)
            for part in range(kv_heads)
            for spot in range(ring)
        ]
        return lax.ppermute(values, "seq", pairs)

    vmem = pl.BlockSpec(memory_space=pltpu.VMEM)
    smem = pl.BlockSpec(memory_space=pltpu.SMEM)
    lines = group * rows
    message = pl.pallas_call(
        pack_kernel,
        out_shape=jax.ShapeDtypeStruct(
            (kv_heads, lines + 2 * rows + 2 * cached_rows, head_dim), jnp.bfloat16
        ),
        in_specs=[vmem] * 3,
        out_specs=vmem,
        name="pack_message",
    )(text_query, stretch_kv, cache_kv)
    me_array = me.reshape(1).astype(jnp.int32)
    own_image = image_kv.reshape(image_kv.shape[1:])
    message, own_image = lax.optimization_barrier((message, own_image))
    image_before = lax.ppermute(own_image, "seq", [(i, i + 1) for i in range(devices - 1)])
    cross_context = pl.pallas_call(
        functools.partial(cross_kernel, slots),
        out_shape=jax.ShapeDtypeStruct(cross_query.shape, jnp.bfloat16),
        in_specs=[smem] * 5 + [vmem] * 3,
        out_specs=vmem,
        compiler_params=pltpu.CompilerParams(vmem_limit_bytes=16 * 2**20),
        cost_estimate=pl.CostEstimate(
            flops=400_000_000, bytes_accessed=1_200_000, transcendentals=200_000
        ),
        name="cross_attention",
    )(
        me_array,
        image_start,
        image_stop,
        image_lengths,
        cross_gate,
        cross_query,
        image_before,
        own_image,
    )

    arrived = lax.all_to_all(
        message, "seq", split_axis=0, concat_axis=0, axis_index_groups=columns, tiled=True
    )
    arrived, cross_context = lax.optimization_barrier((arrived, cross_context))

    def attend(steps, first, last, hold, caches, carried):
        pieces = [piece for step in steps for piece in arrivals[step]]
        count = kv_heads * cached_rows
        held = sum(cache.shape[1] for cache in caches) // count
        total_keys = kv_heads * len(steps) * rows
        if not hold:
            total_keys += -(-count * (len(steps) + held) // rows) * rows
        if last:
            out_shape = [jax.ShapeDtypeStruct((kv_heads, rows, group * head_dim), jnp.bfloat16)]
        else:
            out_shape = [jax.ShapeDtypeStruct((kv_heads, lines, head_dim), jnp.float32)] * 3
        if hold:
            out_shape.append(
                jax.ShapeDtypeStruct((2, count * len(steps), head_dim), jnp.bfloat16)
            )
        work = kv_heads * lines * len(steps) * rows * 3
        return pl.pallas_call(
            functools.partial(
                self_kernel,
                steps,
                tuple(len(arrivals[step]) for step in steps),
                rows,
                ring,
                cached_rows,
                first,
                last,
                hold,
                len(caches),
            ),
            out_shape=out_shape,
            in_specs=[smem] + [vmem] * (1 + len(pieces) + len(caches) + len(carried)),
            out_specs=[vmem] * len(out_shape),
            scratch_shapes=[
                pltpu.VMEM((total_keys, head_dim), jnp.bfloat16),
                pltpu.VMEM((total_keys, 2 * head_dim), jnp.bfloat16),
            ],
            compiler_params=pltpu.CompilerParams(vmem_limit_bytes=32 * 2**20),
            cost_estimate=pl.CostEstimate(
                flops=4 * work * head_dim, bytes_accessed=2_000_000, transcendentals=work
            ),
            name="self_attention",
        )(me_array, arrived, *pieces, *caches, *carried)

    up = down = arrived[:, lines:, :]
    arrivals = {0: ()}
    state, caches = (), ()
    steps = (0,)
    for step in range(1, ring // 2):
        up, down = shift(up, 1), shift(down, -1)
        *state, cache = attend(steps, step == 1, False, True, (), state)
        caches += (cache,)
        up, state = lax.optimization_barrier((up, state))
        arrivals[-step], arrivals[step] = (up,), (down,)
        steps = (-step, step)
    arrivals[ring // 2] = (shift(up, 1),)
    state = attend(steps, False, False, False, caches, state)
    (self_heads,) = attend((ring // 2,), False, True, False, (), state)

    returned = lax.all_to_all(
        self_heads, "seq", split_axis=0, concat_axis=0, axis_index_groups=columns, tiled=True
    )
    self_context = jnp.concatenate([returned[part] for part in range(kv_heads)], 1)
    return (self_context, cross_context)


def solution(mesh):
    in_specs = (
        P(("doc", "seq"), None),
        P(("doc", "seq"), None, None),
        P(("doc", "seq"), None, None),
        P(("doc", "seq"), None),
        P(("doc", "seq"), None, None, None),
        P("doc"),
        P("doc"),
        P("doc"),
        P("doc"),
    )
    out_specs = (P(("doc", "seq"), None), P(("doc", "seq"), None))
    return jax.shard_map(shards, mesh=mesh, in_specs=in_specs, out_specs=out_specs, check_vma=False)
```

time: 101 us -> 79.6 us (0.79)
  the two profiles are of different devices: /device:TPU:54 before, /device:TPU:56 now
where the time goes in v2:
time: 79.6 us; the launch traced here: 79.2 us
  starting transfers between devices  37.8 us (47%)
  Pallas kernels  17.4 us (22%)
  waiting for transfers between devices  11.2 us (14%)
  blocking collectives  10.5 us (13%)
  between operations  1.46 us (2%)
  other arithmetic  0.85 us (1%)
    ppermute x7, starting transfers between devices, shift(): return lax.ppermute(values, 'seq', pairs)  29.1 us
    pallas_call x5, Pallas kernels, attend(): pl.pallas_call(functools.partial(self_kernel, steps, tuple((len(arrivals[...  12.1 us
    all_to_all x1, blocking collectives, shards(): lax.all_to_all(self_heads, 'seq', split_axis=0, concat_axis=0, axis_index...  10.5 us
    ppermute x7, waiting for transfers between devices, shift(): return lax.ppermute(values, 'seq', pairs)  6.31 us
    all_to_all x1, starting transfers between devices, shards(): lax.all_to_all(message, 'seq', split_axis=0, concat_axis=0, axis_index_gr...  4.42 us
    ppermute x1, starting transfers between devices, shards(): lax.ppermute(own_image, 'seq', [(i, i + 1) for i in range(devices - 1)])  4.27 us
    all_to_all x1, waiting for transfers between devices, shards(): lax.all_to_all(message, 'seq', split_axis=0, concat_axis=0, axis_index_gr...  3.65 us
    pallas_call x1, Pallas kernels, shards(): pl.pallas_call(pack_kernel, out_shape=jax.ShapeDtypeStruct((kv_heads, lin...  2.73 us
  transfers between devices with their start and end apart: 9, of which 4 were waited for; matrix products, arithmetic and copies ran while one was open for 0% of the time, Pallas kernels for 16%

profile of v2, /device:TPU:56, one launch (start us, length us, event | category | flops | bytes accessed | tf_op | source)
XLA Modules:
  0.0 79.2 jit_solution(17250655302933256361)
XLA Ops:
  0.6 2.7 %pack_message.1 = bf16[4,784,128]{2,1,0:T(8,128)(2,1)} custom-call(bf16[128,2048]{1,0:T(8,128)(2,1)} %query_ref.2, bf16[128,4,256]{2,1,0:T(4,128)(2,1)} %stretch_ref.1, bf16[8,4,256]{2,1,0:T(4,128)(2,1)} %cache_ref.1), custom_call_target="tpu_custom_call" | custom-call | tf_op jit(solution)/shard_map/pack_message/pallas_call | solution.py:273
  3.4 0.0 copy-start.1
  3.4 0.0 copy-start
  3.4 4.4 %all-to-all-start = ((bf16[4,784,128]{2,1,0:T(8,128)(2,1)}), bf16[4,784,128]{2,1,0:T(8,128)(2,1)S(1)}, u32[]{:S(2)}, u32[]{:S(2)}) async-start(bf16[4,784,128]{2,1,0:T(8,128)(2,1)} %pack_message.1), calls=%async_computation | async-start | bytes 1605632 | tf_op jit(solution)/shard_map/all_to_all | solution.py:307
  7.8 0.0 copy-done.1
  7.8 4.3 %collective-permute-start = (bf16[32,4,256]{2,1,0:T(4,128)(2,1)S(1)}, bf16[32,4,256]{2,1,0:T(4,128)(2,1)S(1)}, u32[]{:S(2)}, u32[]{:S(2)}) collective-permute-start(bf16[32,4,256]{2,1,0:T(4,128)(2,1)S(1)} %bitcast.10), channel_id=1, source_target_pairs={{0,1},{1,2},{2,3},{3,4},{4,5},{5,6},{6,7},{7,8},{8,9},{9,10},{10,1... | collective-permute-start | bytes 196616 | tf_op jit(solution)/shard_map/ppermute | solution.py:285
  12.7 0.0 copy-start.2
  12.7 0.0 copy-start.3
  12.7 0.0 copy-start.4
  12.8 1.2 %collective-permute-done.before_ref = bf16[32,4,256]{2,1,0:T(4,128)(2,1)S(1)} collective-permute-done((bf16[32,4,256]{2,1,0:T(4,128)(2,1)S(1)}, bf16[32,4,256]{2,1,0:T(4,128)(2,1)S(1)}, u32[]{:S(2)}, u32[]{:S(2)}) %collective-permute-start) | collective-permute-done | bytes 65568 | tf_op jit(solution)/shard_map/ppermute | solution.py:285
  14.0 0.0 copy-done
  14.0 0.0 copy-done.2
  14.0 0.0 copy-done.3
  14.0 0.0 copy-done.4
  14.0 2.6 %cross_attention.1 = bf16[128,2048]{1,0:T(8,128)(2,1)} custom-call(s32[1]{0:T(128)} %bitcast.me_ref, s32[32]{0:T(128)S(1)} %copy-done.2, s32[32]{0:T(128)S(1)} %copy-done.3, s32[32]{0:T(128)S(1)} %copy-done.4, f32[1]{0:T(128)S(6)} %copy.11.gate_ref, bf16[128,2048]{1,0:T(8,128)(2,1)S(1)} %copy-done, bf16[32,4,256]{2,1,0:T(4,128)(2,1)S(1)} %collective-permute-done.before_ref, ...), custom_call_target="tpu_custom_call" | custom-call | flops 400000000 | bytes 1200000 | tf_op jit(solution)/shard_map/cross_attention/pallas_call | solution.py:286
  16.6 3.7 %all-to-all-done.own_ref = bf16[4,784,128]{2,1,0:T(8,128)(2,1)S(1)} async-done(((bf16[4,784,128]{2,1,0:T(8,128)(2,1)}), bf16[4,784,128]{2,1,0:T(8,128)(2,1)S(1)}, u32[]{:S(2)}, u32[]{:S(2)}) %all-to-all-start) | async-done | bytes 802848 | tf_op jit(solution)/shard_map/all_to_all | solution.py:307
  20.3 4.3 %collective-permute-start.1 = (bf16[4,272,128]{2,1,0:T(8,128)(2,1)S(1)}, bf16[4,272,128]{2,1,0:T(8,128)(2,1)S(1)}, u32[]{:S(2)}, u32[]{:S(2)}) collective-permute-start(bf16[4,272,128]{2,1,0:T(8,128)(2,1)S(1)} %slice.15), channel_id=1, source_target_pairs={{0,1},{1,2},{2,3},{3,4},{4,5},{5,6},{6,7},{7,0},{8,9},{9,10},{10,1... | collective-permute-start | bytes 835592 | tf_op jit(solution)/shard_map/ppermute | solution.py:268
  24.6 8.6 %collective-permute-start.3 = (bf16[4,272,128]{2,1,0:T(8,128)(2,1)S(1)}, bf16[4,272,128]{2,1,0:T(8,128)(2,1)S(1)}, u32[]{:S(2)}, u32[]{:S(2)}) collective-permute-start(bf16[4,272,128]{2,1,0:T(8,128)(2,1)S(1)} %slice.15), channel_id=1, source_target_pairs={{0,7},{1,0},{2,1},{3,2},{4,3},{5,4},{6,5},{7,6},{8,15},{9,8},{10,9... | collective-permute-start | bytes 835592 | tf_op jit(solution)/shard_map/ppermute | solution.py:268
  33.2 1.3 %self_attention.5 = (f32[4,512,128]{2,1,0:T(8,128)S(1)}, f32[4,512,128]{2,1,0:T(8,128)S(1)}, f32[4,512,128]{2,1,0:T(8,128)S(1)}, bf16[2,32,128]{2,1,0:T(8,128)(2,1)S(1)}) custom-call(s32[1]{0:T(128)} %bitcast.me_ref, bf16[4,784,128]{2,1,0:T(8,128)(2,1)S(1)} %all-to-all-done.own_ref), custom_call_target="tpu_custom_call" | custom-call | flops 402653184 | bytes 2000000 | tf_op jit(solution)/shard_map/self_attention/pallas_call | solution.py:328
  34.5 2.2 %collective-permute-done.1.refs_0_ = bf16[4,272,128]{2,1,0:T(8,128)(2,1)S(1)} collective-permute-done((bf16[4,272,128]{2,1,0:T(8,128)(2,1)S(1)}, bf16[4,272,128]{2,1,0:T(8,128)(2,1)S(1)}, u32[]{:S(2)}, u32[]{:S(2)}) %collective-permute-start.1) | collective-permute-done | bytes 278560 | tf_op jit(solution)/shard_map/ppermute | solution.py:268
  36.7 1.9 %collective-permute-start.2 = (bf16[4,272,128]{2,1,0:T(8,128)(2,1)S(1)}, bf16[4,272,128]{2,1,0:T(8,128)(2,1)S(1)}, u32[]{:S(2)}, u32[]{:S(2)}) collective-permute-start(bf16[4,272,128]{2,1,0:T(8,128)(2,1)S(1)} %collective-permute-done.1.refs_0_), channel_id=1, source_target_pairs={{0,1},{1,2},{2,3},{3,4},{4,5},{5,6},{6,7},{7,0},{8,9},{9,10},{10,1... | collective-permute-start | bytes 835592 | tf_op jit(solution)/shard_map/ppermute | solution.py:268
  38.6 0.0 collective-permute-done.3.refs_1_
  38.6 5.1 %collective-permute-start.5 = (bf16[4,272,128]{2,1,0:T(8,128)(2,1)S(1)}, bf16[4,272,128]{2,1,0:T(8,128)(2,1)S(1)}, u32[]{:S(2)}, u32[]{:S(2)}) collective-permute-start(bf16[4,272,128]{2,1,0:T(8,128)(2,1)S(1)} %collective-permute-done.3.refs_1_), channel_id=1, source_target_pairs={{0,7},{1,0},{2,1},{3,2},{4,3},{5,4},{6,5},{7,6},{8,15},{9,8},{10,9... | collective-permute-start | bytes 835592 | tf_op jit(solution)/shard_map/ppermute | solution.py:268
  43.7 2.6 %self_attention.6 = (f32[4,512,128]{2,1,0:T(8,128)S(1)}, f32[4,512,128]{2,1,0:T(8,128)S(1)}, f32[4,512,128]{2,1,0:T(8,128)S(1)}, bf16[2,64,128]{2,1,0:T(8,128)(2,1)S(1)}) custom-call(s32[1]{0:T(128)} %bitcast.me_ref, bf16[4,784,128]{2,1,0:T(8,128)(2,1)S(1)} %all-to-all-done.own_ref, bf16[4,272,128]{2,1,0:T(8,128)(2,1)S(1)} %collective-permute-done.1.refs_0_, ...), custom_call_target="tpu_custom_call" | custom-call | flops 805306368 | bytes 2000000 | tf_op jit(solution)/shard_map/self_attention/pallas_call | solution.py:328
  46.4 0.0 collective-permute-done.2.refs_0_
  46.4 1.9 %collective-permute-start.4 = (bf16[4,272,128]{2,1,0:T(8,128)(2,1)S(1)}, bf16[4,272,128]{2,1,0:T(8,128)(2,1)S(1)}, u32[]{:S(2)}, u32[]{:S(2)}) collective-permute-start(bf16[4,272,128]{2,1,0:T(8,128)(2,1)S(1)} %collective-permute-done.2.refs_0_), channel_id=1, source_target_pairs={{0,1},{1,2},{2,3},{3,4},{4,5},{5,6},{6,7},{7,0},{8,9},{9,10},{10,1... | collective-permute-start | bytes 835592 | tf_op jit(solution)/shard_map/ppermute | solution.py:268
  48.3 0.0 collective-permute-done.5.refs_1_
  48.3 5.1 %collective-permute-start.7 = (bf16[4,272,128]{2,1,0:T(8,128)(2,1)S(1)}, bf16[4,272,128]{2,1,0:T(8,128)(2,1)S(1)}, u32[]{:S(2)}, u32[]{:S(2)}) collective-permute-start(bf16[4,272,128]{2,1,0:T(8,128)(2,1)S(1)} %collective-permute-done.5.refs_1_), channel_id=1, source_target_pairs={{0,7},{1,0},{2,1},{3,2},{4,3},{5,4},{6,5},{7,6},{8,15},{9,8},{10,9... | collective-permute-start | bytes 835592 | tf_op jit(solution)/shard_map/ppermute | solution.py:268
  53.5 2.6 %self_attention.7 = (f32[4,512,128]{2,1,0:T(8,128)S(1)}, f32[4,512,128]{2,1,0:T(8,128)S(1)}, f32[4,512,128]{2,1,0:T(8,128)S(1)}, bf16[2,64,128]{2,1,0:T(8,128)(2,1)S(1)}) custom-call(s32[1]{0:T(128)} %bitcast.me_ref, bf16[4,784,128]{2,1,0:T(8,128)(2,1)S(1)} %all-to-all-done.own_ref, bf16[4,272,128]{2,1,0:T(8,128)(2,1)S(1)} %collective-permute-done.2.refs_0_, ...), custom_call_target="tpu_custom_call" | custom-call | flops 805306368 | bytes 2000000 | tf_op jit(solution)/shard_map/self_attention/pallas_call | solution.py:328
  56.1 0.0 collective-permute-done.4.refs_0_
  56.1 2.1 %collective-permute-start.6 = (bf16[4,272,128]{2,1,0:T(8,128)(2,1)S(1)}, bf16[4,272,128]{2,1,0:T(8,128)(2,1)S(1)}, u32[]{:S(2)}, u32[]{:S(2)}) collective-permute-start(bf16[4,272,128]{2,1,0:T(8,128)(2,1)S(1)} %collective-permute-done.4.refs_0_), channel_id=1, source_target_pairs={{0,1},{1,2},{2,3},{3,4},{4,5},{5,6},{6,7},{7,0},{8,9},{9,10},{10,1... | collective-permute-start | bytes 835592 | tf_op jit(solution)/shard_map/ppermute | solution.py:268
  58.2 0.0 collective-permute-done.7.refs_1_
  58.2 3.4 %self_attention.8 = (f32[4,512,128]{2,1,0:T(8,128)S(1)}, f32[4,512,128]{2,1,0:T(8,128)S(1)}, f32[4,512,128]{2,1,0:T(8,128)S(1)}) custom-call(s32[1]{0:T(128)} %bitcast.me_ref, bf16[4,784,128]{2,1,0:T(8,128)(2,1)S(1)} %all-to-all-done.own_ref, bf16[4,272,128]{2,1,0:T(8,128)(2,1)S(1)} %collective-permute-done.4.refs_0_, ...), custom_call_target="tpu_custom_call" | custom-call | flops 805306368 | bytes 2000000 | tf_op jit(solution)/shard_map/self_attention/pallas_call | solution.py:328
  61.6 4.1 %collective-permute-done.6.refs_0_ = bf16[4,272,128]{2,1,0:T(8,128)(2,1)S(1)} collective-permute-done((bf16[4,272,128]{2,1,0:T(8,128)(2,1)S(1)}, bf16[4,272,128]{2,1,0:T(8,128)(2,1)S(1)}, u32[]{:S(2)}, u32[]{:S(2)}) %collective-permute-start.6) | collective-permute-done | bytes 278560 | tf_op jit(solution)/shard_map/ppermute | solution.py:268
  65.8 2.1 %self_attention.9 = bf16[4,128,512]{2,1,0:T(8,128)(2,1)S(1)} custom-call(s32[1]{0:T(128)} %bitcast.me_ref, bf16[4,784,128]{2,1,0:T(8,128)(2,1)S(1)} %all-to-all-done.own_ref, bf16[4,272,128]{2,1,0:T(8,128)(2,1)S(1)} %collective-permute-done.6.refs_0_, f32[4,512,128]{2,1,0:T(8,128)S(1)} %get-tuple-element.60.refs_1_, ...), custom_call_target="tpu_custom_call" | custom-call | flops 402653184 | bytes 2000000 | tf_op jit(solution)/shard_map/self_attention/pallas_call | solution.py:328
  67.8 10.5 %all_to_all.10 = bf16[4,128,512]{2,1,0:T(8,128)(2,1)S(1)} all-to-all(bf16[4,128,512]{2,1,0:T(8,128)(2,1)S(1)} %self_attention.9), channel_id=1, replica_groups={{0,8,16,24},{1,9,17,25},{2,10,18,26},{3,11,19,27},{4,12,20,28},{5,13,21..., dimensions={0} | all-to-all | bytes 1048576 | tf_op jit(solution)/shard_map/all_to_all | solution.py:370
  78.3 0.9 %pad_maximum_fusion = bf16[128,2048]{1,0:T(8,128)(2,1)} fusion(bf16[128,512]{1,0:T(8,128)(2,1)S(1)} %get-tuple-element.65, bf16[128,512]{1,0:T(8,128)(2,1)S(1)} %get-tuple-element.66, bf16[128,512]{1,0:T(8,128)(2,1)S(1)} %get-tuple-element.67, bf16[128,512]{1,0:T(8,128)(2,1)S(1)} %get-tuple-element.64), kind=kLoop, calls=%fused_computation | loop fusion | flops 2097152 | bytes 1048576 | tf_op jit(solution)/shard_map/concatenate | solution.py:373
  (2 shorter events, 0.1 us)
Async XLA Ops:
  3.4 4.4 %copy-start.1 = (bf16[1,32,4,256]{3,2,1,0:T(4,128)(2,1)S(1)}, bf16[1,32,4,256]{3,2,1,0:T(4,128)(2,1)}, u32[]{:S(2)}) copy-start(bf16[1,32,4,256]{3,2,1,0:T(4,128)(2,1)} %param.13) | copy-start | bytes 196612
  3.4 10.6 %copy-start = (bf16[128,2048]{1,0:T(8,128)(2,1)S(1)}, bf16[128,2048]{1,0:T(8,128)(2,1)}, u32[]{:S(2)}) copy-start(bf16[128,2048]{1,0:T(8,128)(2,1)} %query_ref.3) | copy-start | bytes 1572868
  3.4 16.9 %all-to-all-start = ((bf16[4,784,128]{2,1,0:T(8,128)(2,1)}), bf16[4,784,128]{2,1,0:T(8,128)(2,1)S(1)}, u32[]{:S(2)}, u32[]{:S(2)}) async-start(bf16[4,784,128]{2,1,0:T(8,128)(2,1)} %pack_message.1), calls=%async_computation | async-start | bytes 1605632 | tf_op jit(solution)/shard_map/all_to_all | solution.py:307
  7.8 6.2 %collective-permute-start = (bf16[32,4,256]{2,1,0:T(4,128)(2,1)S(1)}, bf16[32,4,256]{2,1,0:T(4,128)(2,1)S(1)}, u32[]{:S(2)}, u32[]{:S(2)}) collective-permute-start(bf16[32,4,256]{2,1,0:T(4,128)(2,1)S(1)} %bitcast.10), channel_id=1, source_target_pairs={{0,1},{1,2},{2,3},{3,4},{4,5},{5,6},{6,7},{7,8},{8,9},{9,10},{10,1... | collective-permute-start | bytes 196616 | tf_op jit(solution)/shard_map/ppermute | solution.py:285
  12.7 1.2 %copy-start.2 = (s32[32]{0:T(128)S(1)}, s32[32]{0:T(128)}, u32[]{:S(2)}) copy-start(s32[32]{0:T(128)} %start_ref.1) | copy-start | bytes 388
  12.7 1.2 %copy-start.3 = (s32[32]{0:T(128)S(1)}, s32[32]{0:T(128)}, u32[]{:S(2)}) copy-start(s32[32]{0:T(128)} %stop_ref.1) | copy-start | bytes 388
  12.7 1.2 %copy-start.4 = (s32[32]{0:T(128)S(1)}, s32[32]{0:T(128)}, u32[]{:S(2)}) copy-start(s32[32]{0:T(128)} %length_ref.1) | copy-start | bytes 388
  20.3 16.4 %collective-permute-start.1 = (bf16[4,272,128]{2,1,0:T(8,128)(2,1)S(1)}, bf16[4,272,128]{2,1,0:T(8,128)(2,1)S(1)}, u32[]{:S(2)}, u32[]{:S(2)}) collective-permute-start(bf16[4,272,128]{2,1,0:T(8,128)(2,1)S(1)} %slice.15), channel_id=1, source_target_pairs={{0,1},{1,2},{2,3},{3,4},{4,5},{5,6},{6,7},{7,0},{8,9},{9,10},{10,1... | collective-permute-start | bytes 835592 | tf_op jit(solution)/shard_map/ppermute | solution.py:268
  24.6 14.0 %collective-permute-start.3 = (bf16[4,272,128]{2,1,0:T(8,128)(2,1)S(1)}, bf16[4,272,128]{2,1,0:T(8,128)(2,1)S(1)}, u32[]{:S(2)}, u32[]{:S(2)}) collective-permute-start(bf16[4,272,128]{2,1,0:T(8,128)(2,1)S(1)} %slice.15), channel_id=1, source_target_pairs={{0,7},{1,0},{2,1},{3,2},{4,3},{5,4},{6,5},{7,6},{8,15},{9,8},{10,9... | collective-permute-start | bytes 835592 | tf_op jit(solution)/shard_map/ppermute | solution.py:268
  36.7 9.7 %collective-permute-start.2 = (bf16[4,272,128]{2,1,0:T(8,128)(2,1)S(1)}, bf16[4,272,128]{2,1,0:T(8,128)(2,1)S(1)}, u32[]{:S(2)}, u32[]{:S(2)}) collective-permute-start(bf16[4,272,128]{2,1,0:T(8,128)(2,1)S(1)} %collective-permute-done.1.refs_0_), channel_id=1, source_target_pairs={{0,1},{1,2},{2,3},{3,4},{4,5},{5,6},{6,7},{7,0},{8,9},{9,10},{10,1... | collective-permute-start | bytes 835592 | tf_op jit(solution)/shard_map/ppermute | solution.py:268
  38.6 9.7 %collective-permute-start.5 = (bf16[4,272,128]{2,1,0:T(8,128)(2,1)S(1)}, bf16[4,272,128]{2,1,0:T(8,128)(2,1)S(1)}, u32[]{:S(2)}, u32[]{:S(2)}) collective-permute-start(bf16[4,272,128]{2,1,0:T(8,128)(2,1)S(1)} %collective-permute-done.3.refs_1_), channel_id=1, source_target_pairs={{0,7},{1,0},{2,1},{3,2},{4,3},{5,4},{6,5},{7,6},{8,15},{9,8},{10,9... | collective-permute-start | bytes 835592 | tf_op jit(solution)/shard_map/ppermute | solution.py:268
  46.4 9.7 %collective-permute-start.4 = (bf16[4,272,128]{2,1,0:T(8,128)(2,1)S(1)}, bf16[4,272,128]{2,1,0:T(8,128)(2,1)S(1)}, u32[]{:S(2)}, u32[]{:S(2)}) collective-permute-start(bf16[4,272,128]{2,1,0:T(8,128)(2,1)S(1)} %collective-permute-done.2.refs_0_), channel_id=1, source_target_pairs={{0,1},{1,2},{2,3},{3,4},{4,5},{5,6},{6,7},{7,0},{8,9},{9,10},{10,1... | collective-permute-start | bytes 835592 | tf_op jit(solution)/shard_map/ppermute | solution.py:268
  48.3 9.9 %collective-permute-start.7 = (bf16[4,272,128]{2,1,0:T(8,128)(2,1)S(1)}, bf16[4,272,128]{2,1,0:T(8,128)(2,1)S(1)}, u32[]{:S(2)}, u32[]{:S(2)}) collective-permute-start(bf16[4,272,128]{2,1,0:T(8,128)(2,1)S(1)} %collective-permute-done.5.refs_1_), channel_id=1, source_target_pairs={{0,7},{1,0},{2,1},{3,2},{4,3},{5,4},{6,5},{7,6},{8,15},{9,8},{10,9... | collective-permute-start | bytes 835592 | tf_op jit(solution)/shard_map/ppermute | solution.py:268
  56.1 9.7 %collective-permute-start.6 = (bf16[4,272,128]{2,1,0:T(8,128)(2,1)S(1)}, bf16[4,272,128]{2,1,0:T(8,128)(2,1)S(1)}, u32[]{:S(2)}, u32[]{:S(2)}) collective-permute-start(bf16[4,272,128]{2,1,0:T(8,128)(2,1)S(1)} %collective-permute-done.4.refs_0_), channel_id=1, source_target_pairs={{0,1},{1,2},{2,3},{3,4},{4,5},{5,6},{6,7},{7,0},{8,9},{9,10},{10,1... | collective-permute-start | bytes 835592 | tf_op jit(solution)/shard_map/ppermute | solution.py:268

commit v3 on v2

--- a/solution.py
+++ b/solution.py
@@ -23,14 +23,14 @@
         for head in range(heads):
             spot = (part * heads + head) * width
             out_ref[part, head * rows : (head + 1) * rows, :] = query_ref[:, spot : spot + width]
-        base = heads * rows
-        both = stretch_ref[:, part, :]
-        out_ref[part, base : base + rows, :] = both[:, :width]
-        out_ref[part, base + rows : base + 2 * rows, :] = both[:, width:]
-        both = cache_ref[:, part, :].astype(jnp.float32)
-        out_ref[part, base + 2 * rows :, :] = jnp.concatenate(
-            [both[:, :width], both[:, width:]], 0
-        ).astype(jnp.bfloat16)
+    base = heads * rows
+    stretch = jnp.swapaxes(stretch_ref[...], 0, 1)
+    out_ref[:, base : base + rows, :] = stretch[:, :, :width]
+    out_ref[:, base + rows : base + 2 * rows, :] = stretch[:, :, width:]
+    cache = jnp.swapaxes(cache_ref[...].astype(jnp.float32), 0, 1)
+    out_ref[:, base + 2 * rows :, :] = jnp.concatenate(
+        [cache[:, :, :width], cache[:, :, width:]], 1
+    ).astype(jnp.bfloat16)
 
 
 def split(low, high):
@@ -125,24 +125,14 @@
     lane = lax.broadcasted_iota(jnp.int32, (1, rows), 1)
     edge = jnp.where(lane < present - (cached - rows), 0.0, LOW_SCORE)
 
-    shifts = []
-    for step in steps:
-        if step == 0:
-            line = lax.broadcasted_iota(jnp.int32, (lines, rows), 0) % rows
-            column = lax.broadcasted_iota(jnp.int32, (lines, rows), 1)
-            shifts.append(jnp.where(column <= line, 0.0, LOW_SCORE))
-        else:
-            owner = lax.rem(here + step + ring, ring)
-            shifts.append(jnp.where(owner < here, 0.0, LOW_SCORE))
-
-    for part in range(parts):
+    def fold(part, valid):
         query = own_ref[part, :lines, :]
         peak, total = None, None
         if not first:
             total = jnp.concatenate([carried[0][part], carried[2][part]], 1)
             peak = carried[1][part]
         full = cached + part * stretch
-        chunks = split(0, full + stretch)
+        chunks = split(0, full + valid * rows)
         if first:
             chunks = chunks[::-1]
         for low, high in chunks:
@@ -152,8 +142,10 @@
             tiles = []
             for spot in range(low, high, rows):
                 tile = scores[:, spot - low : spot - low + rows] * scale
-                if spot >= full:
-                    tile = tile + shifts[(spot - full) // rows]
+                if spot >= full and steps[(spot - full) // rows] == 0:
+                    line = lax.broadcasted_iota(jnp.int32, (lines, rows), 0) % rows
+                    column = lax.broadcasted_iota(jnp.int32, (lines, rows), 1)
+                    tile = jnp.where(column <= line, tile, LOW_SCORE)
                 elif spot == cached - rows and present < cached:
                     tile = tile + edge
                 tiles.append(tile)
@@ -184,6 +176,19 @@
             out_total[part] = total[:, :width]
             out_sums[part] = total[:, width:]
             out_peak[part] = peak
+
+    if steps == (0,):
+        for part in range(parts):
+            fold(part, 1)
+        return
+    owners = [lax.rem(here + step + ring, ring) for step in steps]
+    earlier = sum((owner < here).astype(jnp.int32) for owner in owners)
+    for valid in range(len(steps) + 1):
+
+        @pl.when(earlier == valid)
+        def _():
+            for part in range(parts):
+                fold(part, valid)
 
 
 def cross_kernel(
@@ -357,13 +362,13 @@
     state, caches = (), ()
     steps = (0,)
     for step in range(1, ring // 2):
-        up, down = shift(up, 1), shift(down, -1)
+        down, up = shift(down, -1), shift(up, 1)
         *state, cache = attend(steps, step == 1, False, True, (), state)
         caches += (cache,)
-        up, state = lax.optimization_barrier((up, state))
+        down, state = lax.optimization_barrier((down, state))
         arrivals[-step], arrivals[step] = (up,), (down,)
         steps = (-step, step)
-    arrivals[ring // 2] = (shift(up, 1),)
+    arrivals[ring // 2] = (shift(down, -1),)
     state = attend(steps, False, False, False, caches, state)
     (self_heads,) = attend((ring // 2,), False, True, False, (), state)
 

time: 79.6 us -> 77.9 us (0.979)
  starting transfers between devices: 37.8 us -> 42.6 us
  waiting for transfers between devices: 11.2 us -> 7.85 us
  Pallas kernels: 17.4 us -> 14.2 us
    ppermute x7, starting transfers between devices: 29.1 us -> 33.9 us  [shift(): return lax.ppermute(values, 'seq', pairs)]
    ppermute x7, waiting for transfers between devices: 6.31 us -> 3 us  [shift(): return lax.ppermute(values, 'seq', pairs)]
    pallas_call x5, Pallas kernels: 12.1 us -> 9.38 us  [attend(): pl.pallas_call(functools.partial(self_kernel, steps, tuple((len(arrivals[...]
  transfers between devices with their start and end apart: 9 -> 9, of which waited for: 4 -> 6; matrix products, arithmetic and copies ran while one was open for 0% -> 0% of each run, Pallas kernels for 16% -> 14%
where the time goes in v3:
time: 77.9 us; the launch traced here: 77.5 us
  starting transfers between devices  42.6 us (55%)
  Pallas kernels  14.2 us (18%)
  blocking collectives  10.5 us (13%)
  waiting for transfers between devices  7.85 us (10%)
  between operations  1.45 us (2%)
  other arithmetic  0.85 us (1%)
    ppermute x7, starting transfers between devices, shift(): return lax.ppermute(values, 'seq', pairs)  33.9 us
    all_to_all x1, blocking collectives, shards(): lax.all_to_all(self_heads, 'seq', split_axis=0, concat_axis=0, axis_index...  10.5 us
    pallas_call x5, Pallas kernels, attend(): pl.pallas_call(functools.partial(self_kernel, steps, tuple((len(arrivals[...  9.38 us
    all_to_all x1, starting transfers between devices, shards(): lax.all_to_all(message, 'seq', split_axis=0, concat_axis=0, axis_index_gr...  4.42 us
    ppermute x1, starting transfers between devices, shards(): lax.ppermute(own_image, 'seq', [(i, i + 1) for i in range(devices - 1)])  4.27 us
    all_to_all x1, waiting for transfers between devices, shards(): lax.all_to_all(message, 'seq', split_axis=0, concat_axis=0, axis_index_gr...  3.65 us
    ppermute x7, waiting for transfers between devices, shift(): return lax.ppermute(values, 'seq', pairs)  3 us
    pallas_call x1, Pallas kernels, shards(): pl.pallas_call(functools.partial(cross_kernel, slots), out_shape=jax.Shap...  2.63 us
  transfers between devices with their start and end apart: 9, of which 6 were waited for; matrix products, arithmetic and copies ran while one was open for 0% of the time, Pallas kernels for 14%

profile of v3, /device:TPU:56, one launch (start us, length us, event | category | flops | bytes accessed | tf_op | source)
XLA Modules:
  0.0 77.5 jit_solution(17982407590811051407)
XLA Ops:
  0.6 2.2 %pack_message.1 = bf16[4,784,128]{2,1,0:T(8,128)(2,1)} custom-call(bf16[128,2048]{1,0:T(8,128)(2,1)} %query_ref.2, bf16[128,4,256]{2,1,0:T(4,128)(2,1)} %stretch_ref.1, bf16[8,4,256]{2,1,0:T(4,128)(2,1)} %cache_ref.1), custom_call_target="tpu_custom_call" | custom-call | tf_op jit(solution)/shard_map/pack_message/pallas_call | solution.py:278
  2.8 0.0 copy-start.1
  2.8 0.0 copy-start
  2.8 4.4 %all-to-all-start = ((bf16[4,784,128]{2,1,0:T(8,128)(2,1)}), bf16[4,784,128]{2,1,0:T(8,128)(2,1)S(1)}, u32[]{:S(2)}, u32[]{:S(2)}) async-start(bf16[4,784,128]{2,1,0:T(8,128)(2,1)} %pack_message.1), calls=%async_computation | async-start | bytes 1605632 | tf_op jit(solution)/shard_map/all_to_all | solution.py:312
  7.3 0.0 copy-done.1
  7.3 4.3 %collective-permute-start = (bf16[32,4,256]{2,1,0:T(4,128)(2,1)S(1)}, bf16[32,4,256]{2,1,0:T(4,128)(2,1)S(1)}, u32[]{:S(2)}, u32[]{:S(2)}) collective-permute-start(bf16[32,4,256]{2,1,0:T(4,128)(2,1)S(1)} %bitcast.10), channel_id=1, source_target_pairs={{0,1},{1,2},{2,3},{3,4},{4,5},{5,6},{6,7},{7,8},{8,9},{9,10},{10,1... | collective-permute-start | bytes 196616 | tf_op jit(solution)/shard_map/ppermute | solution.py:290
  12.2 0.0 copy-start.2
  12.2 0.0 copy-start.3
  12.2 0.0 copy-start.4
  12.2 1.2 %collective-permute-done.before_ref = bf16[32,4,256]{2,1,0:T(4,128)(2,1)S(1)} collective-permute-done((bf16[32,4,256]{2,1,0:T(4,128)(2,1)S(1)}, bf16[32,4,256]{2,1,0:T(4,128)(2,1)S(1)}, u32[]{:S(2)}, u32[]{:S(2)}) %collective-permute-start) | collective-permute-done | bytes 65568 | tf_op jit(solution)/shard_map/ppermute | solution.py:290
  13.4 0.0 copy-done
  13.4 0.0 copy-done.2
  13.4 0.0 copy-done.3
  13.4 0.0 copy-done.4
  13.4 2.6 %cross_attention.1 = bf16[128,2048]{1,0:T(8,128)(2,1)} custom-call(s32[1]{0:T(128)} %bitcast.me_ref, s32[32]{0:T(128)S(1)} %copy-done.2, s32[32]{0:T(128)S(1)} %copy-done.3, s32[32]{0:T(128)S(1)} %copy-done.4, f32[1]{0:T(128)S(6)} %copy.11.gate_ref, bf16[128,2048]{1,0:T(8,128)(2,1)S(1)} %copy-done, bf16[32,4,256]{2,1,0:T(4,128)(2,1)S(1)} %collective-permute-done.before_ref, ...), custom_call_target="tpu_custom_call" | custom-call | flops 400000000 | bytes 1200000 | tf_op jit(solution)/shard_map/cross_attention/pallas_call | solution.py:291
  16.1 3.7 %all-to-all-done.own_ref = bf16[4,784,128]{2,1,0:T(8,128)(2,1)S(1)} async-done(((bf16[4,784,128]{2,1,0:T(8,128)(2,1)}), bf16[4,784,128]{2,1,0:T(8,128)(2,1)S(1)}, u32[]{:S(2)}, u32[]{:S(2)}) %all-to-all-start) | async-done | bytes 802848 | tf_op jit(solution)/shard_map/all_to_all | solution.py:312
  19.7 10.9 %collective-permute-start.1 = (bf16[4,272,128]{2,1,0:T(8,128)(2,1)S(1)}, bf16[4,272,128]{2,1,0:T(8,128)(2,1)S(1)}, u32[]{:S(2)}, u32[]{:S(2)}) collective-permute-start(bf16[4,272,128]{2,1,0:T(8,128)(2,1)S(1)} %slice.15), channel_id=1, source_target_pairs={{0,7},{1,0},{2,1},{3,2},{4,3},{5,4},{6,5},{7,6},{8,15},{9,8},{10,9... | collective-permute-start | bytes 835592 | tf_op jit(solution)/shard_map/ppermute | solution.py:273
  30.7 1.9 %collective-permute-start.3 = (bf16[4,272,128]{2,1,0:T(8,128)(2,1)S(1)}, bf16[4,272,128]{2,1,0:T(8,128)(2,1)S(1)}, u32[]{:S(2)}, u32[]{:S(2)}) collective-permute-start(bf16[4,272,128]{2,1,0:T(8,128)(2,1)S(1)} %slice.15), channel_id=1, source_target_pairs={{0,1},{1,2},{2,3},{3,4},{4,5},{5,6},{6,7},{7,0},{8,9},{9,10},{10,1... | collective-permute-start | bytes 835592 | tf_op jit(solution)/shard_map/ppermute | solution.py:273
  32.6 1.4 %self_attention.5 = (f32[4,512,128]{2,1,0:T(8,128)S(1)}, f32[4,512,128]{2,1,0:T(8,128)S(1)}, f32[4,512,128]{2,1,0:T(8,128)S(1)}, bf16[2,32,128]{2,1,0:T(8,128)(2,1)S(1)}) custom-call(s32[1]{0:T(128)} %bitcast.me_ref, bf16[4,784,128]{2,1,0:T(8,128)(2,1)S(1)} %all-to-all-done.own_ref), custom_call_target="tpu_custom_call" | custom-call | flops 402653184 | bytes 2000000 | tf_op jit(solution)/shard_map/self_attention/pallas_call | solution.py:333
  34.0 1.4 %collective-permute-done.1.refs_1_ = bf16[4,272,128]{2,1,0:T(8,128)(2,1)S(1)} collective-permute-done((bf16[4,272,128]{2,1,0:T(8,128)(2,1)S(1)}, bf16[4,272,128]{2,1,0:T(8,128)(2,1)S(1)}, u32[]{:S(2)}, u32[]{:S(2)}) %collective-permute-start.1) | collective-permute-done | bytes 278560 | tf_op jit(solution)/shard_map/ppermute | solution.py:273
  35.4 5.6 %collective-permute-start.2 = (bf16[4,272,128]{2,1,0:T(8,128)(2,1)S(1)}, bf16[4,272,128]{2,1,0:T(8,128)(2,1)S(1)}, u32[]{:S(2)}, u32[]{:S(2)}) collective-permute-start(bf16[4,272,128]{2,1,0:T(8,128)(2,1)S(1)} %collective-permute-done.1.refs_1_), channel_id=1, source_target_pairs={{0,7},{1,0},{2,1},{3,2},{4,3},{5,4},{6,5},{7,6},{8,15},{9,8},{10,9... | collective-permute-start | bytes 835592 | tf_op jit(solution)/shard_map/ppermute | solution.py:273
  41.0 0.0 collective-permute-done.3.refs_0_
  41.0 1.9 %collective-permute-start.5 = (bf16[4,272,128]{2,1,0:T(8,128)(2,1)S(1)}, bf16[4,272,128]{2,1,0:T(8,128)(2,1)S(1)}, u32[]{:S(2)}, u32[]{:S(2)}) collective-permute-start(bf16[4,272,128]{2,1,0:T(8,128)(2,1)S(1)} %collective-permute-done.3.refs_0_), channel_id=1, source_target_pairs={{0,1},{1,2},{2,3},{3,4},{4,5},{5,6},{6,7},{7,0},{8,9},{9,10},{10,1... | collective-permute-start | bytes 835592 | tf_op jit(solution)/shard_map/ppermute | solution.py:273
  42.9 1.8 %self_attention.6 = (f32[4,512,128]{2,1,0:T(8,128)S(1)}, f32[4,512,128]{2,1,0:T(8,128)S(1)}, f32[4,512,128]{2,1,0:T(8,128)S(1)}, bf16[2,64,128]{2,1,0:T(8,128)(2,1)S(1)}) custom-call(s32[1]{0:T(128)} %bitcast.me_ref, bf16[4,784,128]{2,1,0:T(8,128)(2,1)S(1)} %all-to-all-done.own_ref, bf16[4,272,128]{2,1,0:T(8,128)(2,1)S(1)} %collective-permute-done.3.refs_0_, ...), custom_call_target="tpu_custom_call" | custom-call | flops 805306368 | bytes 2000000 | tf_op jit(solution)/shard_map/self_attention/pallas_call | solution.py:333
  44.7 0.3 collective-permute-done.2.refs_1_
  45.0 5.7 %collective-permute-start.4 = (bf16[4,272,128]{2,1,0:T(8,128)(2,1)S(1)}, bf16[4,272,128]{2,1,0:T(8,128)(2,1)S(1)}, u32[]{:S(2)}, u32[]{:S(2)}) collective-permute-start(bf16[4,272,128]{2,1,0:T(8,128)(2,1)S(1)} %collective-permute-done.2.refs_1_), channel_id=1, source_target_pairs={{0,7},{1,0},{2,1},{3,2},{4,3},{5,4},{6,5},{7,6},{8,15},{9,8},{10,9... | collective-permute-start | bytes 835592 | tf_op jit(solution)/shard_map/ppermute | solution.py:273
  50.8 0.0 collective-permute-done.5.refs_0_
  50.8 1.9 %collective-permute-start.7 = (bf16[4,272,128]{2,1,0:T(8,128)(2,1)S(1)}, bf16[4,272,128]{2,1,0:T(8,128)(2,1)S(1)}, u32[]{:S(2)}, u32[]{:S(2)}) collective-permute-start(bf16[4,272,128]{2,1,0:T(8,128)(2,1)S(1)} %collective-permute-done.5.refs_0_), channel_id=1, source_target_pairs={{0,1},{1,2},{2,3},{3,4},{4,5},{5,6},{6,7},{7,0},{8,9},{9,10},{10,1... | collective-permute-start | bytes 835592 | tf_op jit(solution)/shard_map/ppermute | solution.py:273
  52.7 2.0 %self_attention.7 = (f32[4,512,128]{2,1,0:T(8,128)S(1)}, f32[4,512,128]{2,1,0:T(8,128)S(1)}, f32[4,512,128]{2,1,0:T(8,128)S(1)}, bf16[2,64,128]{2,1,0:T(8,128)(2,1)S(1)}) custom-call(s32[1]{0:T(128)} %bitcast.me_ref, bf16[4,784,128]{2,1,0:T(8,128)(2,1)S(1)} %all-to-all-done.own_ref, bf16[4,272,128]{2,1,0:T(8,128)(2,1)S(1)} %collective-permute-done.5.refs_0_, ...), custom_call_target="tpu_custom_call" | custom-call | flops 805306368 | bytes 2000000 | tf_op jit(solution)/shard_map/self_attention/pallas_call | solution.py:333
  54.7 0.1 collective-permute-done.4.refs_1_
  54.8 5.9 %collective-permute-start.6 = (bf16[4,272,128]{2,1,0:T(8,128)(2,1)S(1)}, bf16[4,272,128]{2,1,0:T(8,128)(2,1)S(1)}, u32[]{:S(2)}, u32[]{:S(2)}) collective-permute-start(bf16[4,272,128]{2,1,0:T(8,128)(2,1)S(1)} %collective-permute-done.4.refs_1_), channel_id=1, source_target_pairs={{0,7},{1,0},{2,1},{3,2},{4,3},{5,4},{6,5},{7,6},{8,15},{9,8},{10,9... | collective-permute-start | bytes 835592 | tf_op jit(solution)/shard_map/ppermute | solution.py:273
  60.7 0.0 collective-permute-done.7.refs_0_
  60.7 2.9 %self_attention.8 = (f32[4,512,128]{2,1,0:T(8,128)S(1)}, f32[4,512,128]{2,1,0:T(8,128)S(1)}, f32[4,512,128]{2,1,0:T(8,128)S(1)}) custom-call(s32[1]{0:T(128)} %bitcast.me_ref, bf16[4,784,128]{2,1,0:T(8,128)(2,1)S(1)} %all-to-all-done.own_ref, bf16[4,272,128]{2,1,0:T(8,128)(2,1)S(1)} %collective-permute-done.7.refs_0_, ...), custom_call_target="tpu_custom_call" | custom-call | flops 805306368 | bytes 2000000 | tf_op jit(solution)/shard_map/self_attention/pallas_call | solution.py:333
  63.6 1.1 %collective-permute-done.6.refs_0_ = bf16[4,272,128]{2,1,0:T(8,128)(2,1)S(1)} collective-permute-done((bf16[4,272,128]{2,1,0:T(8,128)(2,1)S(1)}, bf16[4,272,128]{2,1,0:T(8,128)(2,1)S(1)}, u32[]{:S(2)}, u32[]{:S(2)}) %collective-permute-start.6) | collective-permute-done | bytes 278560 | tf_op jit(solution)/shard_map/ppermute | solution.py:273
  64.7 1.4 %self_attention.9 = bf16[4,128,512]{2,1,0:T(8,128)(2,1)S(1)} custom-call(s32[1]{0:T(128)} %bitcast.me_ref, bf16[4,784,128]{2,1,0:T(8,128)(2,1)S(1)} %all-to-all-done.own_ref, bf16[4,272,128]{2,1,0:T(8,128)(2,1)S(1)} %collective-permute-done.6.refs_0_, f32[4,512,128]{2,1,0:T(8,128)S(1)} %get-tuple-element.60.refs_1_, ...), custom_call_target="tpu_custom_call" | custom-call | flops 402653184 | bytes 2000000 | tf_op jit(solution)/shard_map/self_attention/pallas_call | solution.py:333
  66.1 10.5 %all_to_all.10 = bf16[4,128,512]{2,1,0:T(8,128)(2,1)S(1)} all-to-all(bf16[4,128,512]{2,1,0:T(8,128)(2,1)S(1)} %self_attention.9), channel_id=1, replica_groups={{0,8,16,24},{1,9,17,25},{2,10,18,26},{3,11,19,27},{4,12,20,28},{5,13,21..., dimensions={0} | all-to-all | bytes 1048576 | tf_op jit(solution)/shard_map/all_to_all | solution.py:375
  76.6 0.9 %pad_maximum_fusion = bf16[128,2048]{1,0:T(8,128)(2,1)} fusion(bf16[128,512]{1,0:T(8,128)(2,1)S(1)} %get-tuple-element.65, bf16[128,512]{1,0:T(8,128)(2,1)S(1)} %get-tuple-element.66, bf16[128,512]{1,0:T(8,128)(2,1)S(1)} %get-tuple-element.67, bf16[128,512]{1,0:T(8,128)(2,1)S(1)} %get-tuple-element.64), kind=kLoop, calls=%fused_computation | loop fusion | flops 2097152 | bytes 1048576 | tf_op jit(solution)/shard_map/concatenate | solution.py:378
  (2 shorter events, 0.1 us)
Async XLA Ops:
  2.8 4.4 %copy-start.1 = (bf16[1,32,4,256]{3,2,1,0:T(4,128)(2,1)S(1)}, bf16[1,32,4,256]{3,2,1,0:T(4,128)(2,1)}, u32[]{:S(2)}) copy-start(bf16[1,32,4,256]{3,2,1,0:T(4,128)(2,1)} %param.13) | copy-start | bytes 196612
  2.8 10.6 %copy-start = (bf16[128,2048]{1,0:T(8,128)(2,1)S(1)}, bf16[128,2048]{1,0:T(8,128)(2,1)}, u32[]{:S(2)}) copy-start(bf16[128,2048]{1,0:T(8,128)(2,1)} %query_ref.3) | copy-start | bytes 1572868
  2.8 16.9 %all-to-all-start = ((bf16[4,784,128]{2,1,0:T(8,128)(2,1)}), bf16[4,784,128]{2,1,0:T(8,128)(2,1)S(1)}, u32[]{:S(2)}, u32[]{:S(2)}) async-start(bf16[4,784,128]{2,1,0:T(8,128)(2,1)} %pack_message.1), calls=%async_computation | async-start | bytes 1605632 | tf_op jit(solution)/shard_map/all_to_all | solution.py:312
  7.3 6.2 %collective-permute-start = (bf16[32,4,256]{2,1,0:T(4,128)(2,1)S(1)}, bf16[32,4,256]{2,1,0:T(4,128)(2,1)S(1)}, u32[]{:S(2)}, u32[]{:S(2)}) collective-permute-start(bf16[32,4,256]{2,1,0:T(4,128)(2,1)S(1)} %bitcast.10), channel_id=1, source_target_pairs={{0,1},{1,2},{2,3},{3,4},{4,5},{5,6},{6,7},{7,8},{8,9},{9,10},{10,1... | collective-permute-start | bytes 196616 | tf_op jit(solution)/shard_map/ppermute | solution.py:290
  12.2 1.2 %copy-start.2 = (s32[32]{0:T(128)S(1)}, s32[32]{0:T(128)}, u32[]{:S(2)}) copy-start(s32[32]{0:T(128)} %start_ref.1) | copy-start | bytes 388
  12.2 1.2 %copy-start.3 = (s32[32]{0:T(128)S(1)}, s32[32]{0:T(128)}, u32[]{:S(2)}) copy-start(s32[32]{0:T(128)} %stop_ref.1) | copy-start | bytes 388
  12.2 1.2 %copy-start.4 = (s32[32]{0:T(128)S(1)}, s32[32]{0:T(128)}, u32[]{:S(2)}) copy-start(s32[32]{0:T(128)} %length_ref.1) | copy-start | bytes 388
  19.7 15.7 %collective-permute-start.1 = (bf16[4,272,128]{2,1,0:T(8,128)(2,1)S(1)}, bf16[4,272,128]{2,1,0:T(8,128)(2,1)S(1)}, u32[]{:S(2)}, u32[]{:S(2)}) collective-permute-start(bf16[4,272,128]{2,1,0:T(8,128)(2,1)S(1)} %slice.15), channel_id=1, source_target_pairs={{0,7},{1,0},{2,1},{3,2},{4,3},{5,4},{6,5},{7,6},{8,15},{9,8},{10,9... | collective-permute-start | bytes 835592 | tf_op jit(solution)/shard_map/ppermute | solution.py:273
  30.7 10.3 %collective-permute-start.3 = (bf16[4,272,128]{2,1,0:T(8,128)(2,1)S(1)}, bf16[4,272,128]{2,1,0:T(8,128)(2,1)S(1)}, u32[]{:S(2)}, u32[]{:S(2)}) collective-permute-start(bf16[4,272,128]{2,1,0:T(8,128)(2,1)S(1)} %slice.15), channel_id=1, source_target_pairs={{0,1},{1,2},{2,3},{3,4},{4,5},{5,6},{6,7},{7,0},{8,9},{9,10},{10,1... | collective-permute-start | bytes 835592 | tf_op jit(solution)/shard_map/ppermute | solution.py:273
  35.4 9.6 %collective-permute-start.2 = (bf16[4,272,128]{2,1,0:T(8,128)(2,1)S(1)}, bf16[4,272,128]{2,1,0:T(8,128)(2,1)S(1)}, u32[]{:S(2)}, u32[]{:S(2)}) collective-permute-start(bf16[4,272,128]{2,1,0:T(8,128)(2,1)S(1)} %collective-permute-done.1.refs_1_), channel_id=1, source_target_pairs={{0,7},{1,0},{2,1},{3,2},{4,3},{5,4},{6,5},{7,6},{8,15},{9,8},{10,9... | collective-permute-start | bytes 835592 | tf_op jit(solution)/shard_map/ppermute | solution.py:273
  41.0 9.7 %collective-permute-start.5 = (bf16[4,272,128]{2,1,0:T(8,128)(2,1)S(1)}, bf16[4,272,128]{2,1,0:T(8,128)(2,1)S(1)}, u32[]{:S(2)}, u32[]{:S(2)}) collective-permute-start(bf16[4,272,128]{2,1,0:T(8,128)(2,1)S(1)} %collective-permute-done.3.refs_0_), channel_id=1, source_target_pairs={{0,1},{1,2},{2,3},{3,4},{4,5},{5,6},{6,7},{7,0},{8,9},{9,10},{10,1... | collective-permute-start | bytes 835592 | tf_op jit(solution)/shard_map/ppermute | solution.py:273
  45.0 9.8 %collective-permute-start.4 = (bf16[4,272,128]{2,1,0:T(8,128)(2,1)S(1)}, bf16[4,272,128]{2,1,0:T(8,128)(2,1)S(1)}, u32[]{:S(2)}, u32[]{:S(2)}) collective-permute-start(bf16[4,272,128]{2,1,0:T(8,128)(2,1)S(1)} %collective-permute-done.2.refs_1_), channel_id=1, source_target_pairs={{0,7},{1,0},{2,1},{3,2},{4,3},{5,4},{6,5},{7,6},{8,15},{9,8},{10,9... | collective-permute-start | bytes 835592 | tf_op jit(solution)/shard_map/ppermute | solution.py:273
  50.8 9.9 %collective-permute-start.7 = (bf16[4,272,128]{2,1,0:T(8,128)(2,1)S(1)}, bf16[4,272,128]{2,1,0:T(8,128)(2,1)S(1)}, u32[]{:S(2)}, u32[]{:S(2)}) collective-permute-start(bf16[4,272,128]{2,1,0:T(8,128)(2,1)S(1)} %collective-permute-done.5.refs_0_), channel_id=1, source_target_pairs={{0,1},{1,2},{2,3},{3,4},{4,5},{5,6},{6,7},{7,0},{8,9},{9,10},{10,1... | collective-permute-start | bytes 835592 | tf_op jit(solution)/shard_map/ppermute | solution.py:273
  54.8 9.9 %collective-permute-start.6 = (bf16[4,272,128]{2,1,0:T(8,128)(2,1)S(1)}, bf16[4,272,128]{2,1,0:T(8,128)(2,1)S(1)}, u32[]{:S(2)}, u32[]{:S(2)}) collective-permute-start(bf16[4,272,128]{2,1,0:T(8,128)(2,1)S(1)} %collective-permute-done.4.refs_1_), channel_id=1, source_target_pairs={{0,7},{1,0},{2,1},{3,2},{4,3},{5,4},{6,5},{7,6},{8,15},{9,8},{10,9... | collective-permute-start | bytes 835592 | tf_op jit(solution)/shard_map/ppermute | solution.py:273

commit v4 on v3

--- a/solution.py
+++ b/solution.py
@@ -178,7 +178,7 @@
             out_peak[part] = peak
 
     if steps == (0,):
-        for part in range(parts):
+        for part in reversed(range(parts)):
             fold(part, 1)
         return
     owners = [lax.rem(here + step + ring, ring) for step in steps]
@@ -187,7 +187,7 @@
 
         @pl.when(earlier == valid)
         def _():
-            for part in range(parts):
+            for part in reversed(range(parts)):
                 fold(part, valid)
 
 

time: 77.9 us -> 77.6 us (level)
  waiting for transfers between devices: 7.85 us -> 9.57 us
  Pallas kernels: 14.2 us -> 12.6 us
    ppermute x7, waiting for transfers between devices: 3 us -> 4.72 us  [shift(): return lax.ppermute(values, 'seq', pairs)]
    pallas_call x5, Pallas kernels: 9.38 us -> 7.76 us  [attend(): pl.pallas_call(functools.partial(self_kernel, steps, tuple((len(arrivals[...]
  transfers between devices with their start and end apart: 9 -> 9, of which waited for: 6 -> 6; matrix products, arithmetic and copies ran while one was open for 0% -> 0% of each run, Pallas kernels for 14% -> 12%
where the time goes in v4:
time: 77.6 us; the launch traced here: 77.2 us
  starting transfers between devices  42.2 us (54%)
  Pallas kernels  12.6 us (16%)
  blocking collectives  10.5 us (14%)
  waiting for transfers between devices  9.57 us (12%)
  between operations  1.44 us (2%)
  other arithmetic  0.85 us (1%)
    ppermute x7, starting transfers between devices, shift(): return lax.ppermute(values, 'seq', pairs)  33.5 us
    all_to_all x1, blocking collectives, shards(): lax.all_to_all(self_heads, 'seq', split_axis=0, concat_axis=0, axis_index...  10.5 us
    pallas_call x5, Pallas kernels, attend(): pl.pallas_call(functools.partial(self_kernel, steps, tuple((len(arrivals[...  7.76 us
    ppermute x7, waiting for transfers between devices, shift(): return lax.ppermute(values, 'seq', pairs)  4.72 us
    all_to_all x1, starting transfers between devices, shards(): lax.all_to_all(message, 'seq', split_axis=0, concat_axis=0, axis_index_gr...  4.42 us
    ppermute x1, starting transfers between devices, shards(): lax.ppermute(own_image, 'seq', [(i, i + 1) for i in range(devices - 1)])  4.27 us
    all_to_all x1, waiting for transfers between devices, shards(): lax.all_to_all(message, 'seq', split_axis=0, concat_axis=0, axis_index_gr...  3.65 us
    pallas_call x1, Pallas kernels, shards(): pl.pallas_call(functools.partial(cross_kernel, slots), out_shape=jax.Shap...  2.63 us
  transfers between devices with their start and end apart: 9, of which 6 were waited for; matrix products, arithmetic and copies ran while one was open for 0% of the time, Pallas kernels for 12%

profile of v4, /device:TPU:56, one launch (start us, length us, event | category | flops | bytes accessed | tf_op | source)
XLA Modules:
  0.0 77.2 jit_solution(1287777625951916816)
XLA Ops:
  0.6 2.2 %pack_message.1 = bf16[4,784,128]{2,1,0:T(8,128)(2,1)} custom-call(bf16[128,2048]{1,0:T(8,128)(2,1)} %query_ref.2, bf16[128,4,256]{2,1,0:T(4,128)(2,1)} %stretch_ref.1, bf16[8,4,256]{2,1,0:T(4,128)(2,1)} %cache_ref.1), custom_call_target="tpu_custom_call" | custom-call | tf_op jit(solution)/shard_map/pack_message/pallas_call | solution.py:278
  2.8 0.0 copy-start.1
  2.8 0.0 copy-start
  2.8 4.4 %all-to-all-start = ((bf16[4,784,128]{2,1,0:T(8,128)(2,1)}), bf16[4,784,128]{2,1,0:T(8,128)(2,1)S(1)}, u32[]{:S(2)}, u32[]{:S(2)}) async-start(bf16[4,784,128]{2,1,0:T(8,128)(2,1)} %pack_message.1), calls=%async_computation | async-start | bytes 1605632 | tf_op jit(solution)/shard_map/all_to_all | solution.py:312
  7.3 0.0 copy-done.1
  7.3 4.3 %collective-permute-start = (bf16[32,4,256]{2,1,0:T(4,128)(2,1)S(1)}, bf16[32,4,256]{2,1,0:T(4,128)(2,1)S(1)}, u32[]{:S(2)}, u32[]{:S(2)}) collective-permute-start(bf16[32,4,256]{2,1,0:T(4,128)(2,1)S(1)} %bitcast.10), channel_id=1, source_target_pairs={{0,1},{1,2},{2,3},{3,4},{4,5},{5,6},{6,7},{7,8},{8,9},{9,10},{10,1... | collective-permute-start | bytes 196616 | tf_op jit(solution)/shard_map/ppermute | solution.py:290
  12.2 0.0 copy-start.2
  12.2 0.0 copy-start.3
  12.2 0.0 copy-start.4
  12.2 1.2 %collective-permute-done.before_ref = bf16[32,4,256]{2,1,0:T(4,128)(2,1)S(1)} collective-permute-done((bf16[32,4,256]{2,1,0:T(4,128)(2,1)S(1)}, bf16[32,4,256]{2,1,0:T(4,128)(2,1)S(1)}, u32[]{:S(2)}, u32[]{:S(2)}) %collective-permute-start) | collective-permute-done | bytes 65568 | tf_op jit(solution)/shard_map/ppermute | solution.py:290
  13.4 0.0 copy-done
  13.4 0.0 copy-done.2
  13.4 0.0 copy-done.3
  13.4 0.0 copy-done.4
  13.4 2.6 %cross_attention.1 = bf16[128,2048]{1,0:T(8,128)(2,1)} custom-call(s32[1]{0:T(128)} %bitcast.me_ref, s32[32]{0:T(128)S(1)} %copy-done.2, s32[32]{0:T(128)S(1)} %copy-done.3, s32[32]{0:T(128)S(1)} %copy-done.4, f32[1]{0:T(128)S(6)} %copy.11.gate_ref, bf16[128,2048]{1,0:T(8,128)(2,1)S(1)} %copy-done, bf16[32,4,256]{2,1,0:T(4,128)(2,1)S(1)} %collective-permute-done.before_ref, ...), custom_call_target="tpu_custom_call" | custom-call | flops 400000000 | bytes 1200000 | tf_op jit(solution)/shard_map/cross_attention/pallas_call | solution.py:291
  16.1 3.7 %all-to-all-done.own_ref = bf16[4,784,128]{2,1,0:T(8,128)(2,1)S(1)} async-done(((bf16[4,784,128]{2,1,0:T(8,128)(2,1)}), bf16[4,784,128]{2,1,0:T(8,128)(2,1)S(1)}, u32[]{:S(2)}, u32[]{:S(2)}) %all-to-all-start) | async-done | bytes 802848 | tf_op jit(solution)/shard_map/all_to_all | solution.py:312
  19.7 10.9 %collective-permute-start.1 = (bf16[4,272,128]{2,1,0:T(8,128)(2,1)S(1)}, bf16[4,272,128]{2,1,0:T(8,128)(2,1)S(1)}, u32[]{:S(2)}, u32[]{:S(2)}) collective-permute-start(bf16[4,272,128]{2,1,0:T(8,128)(2,1)S(1)} %slice.15), channel_id=1, source_target_pairs={{0,7},{1,0},{2,1},{3,2},{4,3},{5,4},{6,5},{7,6},{8,15},{9,8},{10,9... | collective-permute-start | bytes 835592 | tf_op jit(solution)/shard_map/ppermute | solution.py:273
  30.7 1.9 %collective-permute-start.3 = (bf16[4,272,128]{2,1,0:T(8,128)(2,1)S(1)}, bf16[4,272,128]{2,1,0:T(8,128)(2,1)S(1)}, u32[]{:S(2)}, u32[]{:S(2)}) collective-permute-start(bf16[4,272,128]{2,1,0:T(8,128)(2,1)S(1)} %slice.15), channel_id=1, source_target_pairs={{0,1},{1,2},{2,3},{3,4},{4,5},{5,6},{6,7},{7,0},{8,9},{9,10},{10,1... | collective-permute-start | bytes 835592 | tf_op jit(solution)/shard_map/ppermute | solution.py:273
  32.6 1.4 %self_attention.5 = (f32[4,512,128]{2,1,0:T(8,128)S(1)}, f32[4,512,128]{2,1,0:T(8,128)S(1)}, f32[4,512,128]{2,1,0:T(8,128)S(1)}, bf16[2,32,128]{2,1,0:T(8,128)(2,1)S(1)}) custom-call(s32[1]{0:T(128)} %bitcast.me_ref, bf16[4,784,128]{2,1,0:T(8,128)(2,1)S(1)} %all-to-all-done.own_ref), custom_call_target="tpu_custom_call" | custom-call | flops 402653184 | bytes 2000000 | tf_op jit(solution)/shard_map/self_attention/pallas_call | solution.py:333
  34.0 1.4 %collective-permute-done.1.refs_1_ = bf16[4,272,128]{2,1,0:T(8,128)(2,1)S(1)} collective-permute-done((bf16[4,272,128]{2,1,0:T(8,128)(2,1)S(1)}, bf16[4,272,128]{2,1,0:T(8,128)(2,1)S(1)}, u32[]{:S(2)}, u32[]{:S(2)}) %collective-permute-start.1) | collective-permute-done | bytes 278560 | tf_op jit(solution)/shard_map/ppermute | solution.py:273
  35.4 5.6 %collective-permute-start.2 = (bf16[4,272,128]{2,1,0:T(8,128)(2,1)S(1)}, bf16[4,272,128]{2,1,0:T(8,128)(2,1)S(1)}, u32[]{:S(2)}, u32[]{:S(2)}) collective-permute-start(bf16[4,272,128]{2,1,0:T(8,128)(2,1)S(1)} %collective-permute-done.1.refs_1_), channel_id=1, source_target_pairs={{0,7},{1,0},{2,1},{3,2},{4,3},{5,4},{6,5},{7,6},{8,15},{9,8},{10,9... | collective-permute-start | bytes 835592 | tf_op jit(solution)/shard_map/ppermute | solution.py:273
  41.0 0.0 collective-permute-done.3.refs_0_
  41.0 1.9 %collective-permute-start.5 = (bf16[4,272,128]{2,1,0:T(8,128)(2,1)S(1)}, bf16[4,272,128]{2,1,0:T(8,128)(2,1)S(1)}, u32[]{:S(2)}, u32[]{:S(2)}) collective-permute-start(bf16[4,272,128]{2,1,0:T(8,128)(2,1)S(1)} %collective-permute-done.3.refs_0_), channel_id=1, source_target_pairs={{0,1},{1,2},{2,3},{3,4},{4,5},{5,6},{6,7},{7,0},{8,9},{9,10},{10,1... | collective-permute-start | bytes 835592 | tf_op jit(solution)/shard_map/ppermute | solution.py:273
  42.9 1.4 %self_attention.6 = (f32[4,512,128]{2,1,0:T(8,128)S(1)}, f32[4,512,128]{2,1,0:T(8,128)S(1)}, f32[4,512,128]{2,1,0:T(8,128)S(1)}, bf16[2,64,128]{2,1,0:T(8,128)(2,1)S(1)}) custom-call(s32[1]{0:T(128)} %bitcast.me_ref, bf16[4,784,128]{2,1,0:T(8,128)(2,1)S(1)} %all-to-all-done.own_ref, bf16[4,272,128]{2,1,0:T(8,128)(2,1)S(1)} %collective-permute-done.3.refs_0_, ...), custom_call_target="tpu_custom_call" | custom-call | flops 805306368 | bytes 2000000 | tf_op jit(solution)/shard_map/self_attention/pallas_call | solution.py:333
  44.4 0.7 collective-permute-done.2.refs_1_
  45.0 5.6 %collective-permute-start.4 = (bf16[4,272,128]{2,1,0:T(8,128)(2,1)S(1)}, bf16[4,272,128]{2,1,0:T(8,128)(2,1)S(1)}, u32[]{:S(2)}, u32[]{:S(2)}) collective-permute-start(bf16[4,272,128]{2,1,0:T(8,128)(2,1)S(1)} %collective-permute-done.2.refs_1_), channel_id=1, source_target_pairs={{0,7},{1,0},{2,1},{3,2},{4,3},{5,4},{6,5},{7,6},{8,15},{9,8},{10,9... | collective-permute-start | bytes 835592 | tf_op jit(solution)/shard_map/ppermute | solution.py:273
  50.6 0.0 collective-permute-done.5.refs_0_
  50.7 1.9 %collective-permute-start.7 = (bf16[4,272,128]{2,1,0:T(8,128)(2,1)S(1)}, bf16[4,272,128]{2,1,0:T(8,128)(2,1)S(1)}, u32[]{:S(2)}, u32[]{:S(2)}) collective-permute-start(bf16[4,272,128]{2,1,0:T(8,128)(2,1)S(1)} %collective-permute-done.5.refs_0_), channel_id=1, source_target_pairs={{0,1},{1,2},{2,3},{3,4},{4,5},{5,6},{6,7},{7,0},{8,9},{9,10},{10,1... | collective-permute-start | bytes 835592 | tf_op jit(solution)/shard_map/ppermute | solution.py:273
  52.6 1.6 %self_attention.7 = (f32[4,512,128]{2,1,0:T(8,128)S(1)}, f32[4,512,128]{2,1,0:T(8,128)S(1)}, f32[4,512,128]{2,1,0:T(8,128)S(1)}, bf16[2,64,128]{2,1,0:T(8,128)(2,1)S(1)}) custom-call(s32[1]{0:T(128)} %bitcast.me_ref, bf16[4,784,128]{2,1,0:T(8,128)(2,1)S(1)} %all-to-all-done.own_ref, bf16[4,272,128]{2,1,0:T(8,128)(2,1)S(1)} %collective-permute-done.5.refs_0_, ...), custom_call_target="tpu_custom_call" | custom-call | flops 805306368 | bytes 2000000 | tf_op jit(solution)/shard_map/self_attention/pallas_call | solution.py:333
  54.2 0.5 collective-permute-done.4.refs_1_
  54.7 5.6 %collective-permute-start.6 = (bf16[4,272,128]{2,1,0:T(8,128)(2,1)S(1)}, bf16[4,272,128]{2,1,0:T(8,128)(2,1)S(1)}, u32[]{:S(2)}, u32[]{:S(2)}) collective-permute-start(bf16[4,272,128]{2,1,0:T(8,128)(2,1)S(1)} %collective-permute-done.4.refs_1_), channel_id=1, source_target_pairs={{0,7},{1,0},{2,1},{3,2},{4,3},{5,4},{6,5},{7,6},{8,15},{9,8},{10,9... | collective-permute-start | bytes 835592 | tf_op jit(solution)/shard_map/ppermute | solution.py:273
  60.3 0.0 collective-permute-done.7.refs_0_
  60.3 1.9 %self_attention.8 = (f32[4,512,128]{2,1,0:T(8,128)S(1)}, f32[4,512,128]{2,1,0:T(8,128)S(1)}, f32[4,512,128]{2,1,0:T(8,128)S(1)}) custom-call(s32[1]{0:T(128)} %bitcast.me_ref, bf16[4,784,128]{2,1,0:T(8,128)(2,1)S(1)} %all-to-all-done.own_ref, bf16[4,272,128]{2,1,0:T(8,128)(2,1)S(1)} %collective-permute-done.7.refs_0_, ...), custom_call_target="tpu_custom_call" | custom-call | flops 805306368 | bytes 2000000 | tf_op jit(solution)/shard_map/self_attention/pallas_call | solution.py:333
  62.3 2.1 %collective-permute-done.6.refs_0_ = bf16[4,272,128]{2,1,0:T(8,128)(2,1)S(1)} collective-permute-done((bf16[4,272,128]{2,1,0:T(8,128)(2,1)S(1)}, bf16[4,272,128]{2,1,0:T(8,128)(2,1)S(1)}, u32[]{:S(2)}, u32[]{:S(2)}) %collective-permute-start.6) | collective-permute-done | bytes 278560 | tf_op jit(solution)/shard_map/ppermute | solution.py:273
  64.3 1.5 %self_attention.9 = bf16[4,128,512]{2,1,0:T(8,128)(2,1)S(1)} custom-call(s32[1]{0:T(128)} %bitcast.me_ref, bf16[4,784,128]{2,1,0:T(8,128)(2,1)S(1)} %all-to-all-done.own_ref, bf16[4,272,128]{2,1,0:T(8,128)(2,1)S(1)} %collective-permute-done.6.refs_0_, f32[4,512,128]{2,1,0:T(8,128)S(1)} %get-tuple-element.60.refs_1_, ...), custom_call_target="tpu_custom_call" | custom-call | flops 402653184 | bytes 2000000 | tf_op jit(solution)/shard_map/self_attention/pallas_call | solution.py:333
  65.8 10.5 %all_to_all.10 = bf16[4,128,512]{2,1,0:T(8,128)(2,1)S(1)} all-to-all(bf16[4,128,512]{2,1,0:T(8,128)(2,1)S(1)} %self_attention.9), channel_id=1, replica_groups={{0,8,16,24},{1,9,17,25},{2,10,18,26},{3,11,19,27},{4,12,20,28},{5,13,21..., dimensions={0} | all-to-all | bytes 1048576 | tf_op jit(solution)/shard_map/all_to_all | solution.py:375
  76.3 0.9 %pad_maximum_fusion = bf16[128,2048]{1,0:T(8,128)(2,1)} fusion(bf16[128,512]{1,0:T(8,128)(2,1)S(1)} %get-tuple-element.65, bf16[128,512]{1,0:T(8,128)(2,1)S(1)} %get-tuple-element.66, bf16[128,512]{1,0:T(8,128)(2,1)S(1)} %get-tuple-element.67, bf16[128,512]{1,0:T(8,128)(2,1)S(1)} %get-tuple-element.64), kind=kLoop, calls=%fused_computation | loop fusion | flops 2097152 | bytes 1048576 | tf_op jit(solution)/shard_map/concatenate | solution.py:378
  (2 shorter events, 0.1 us)
Async XLA Ops:
  2.8 4.4 %copy-start.1 = (bf16[1,32,4,256]{3,2,1,0:T(4,128)(2,1)S(1)}, bf16[1,32,4,256]{3,2,1,0:T(4,128)(2,1)}, u32[]{:S(2)}) copy-start(bf16[1,32,4,256]{3,2,1,0:T(4,128)(2,1)} %param.13) | copy-start | bytes 196612
  2.8 10.6 %copy-start = (bf16[128,2048]{1,0:T(8,128)(2,1)S(1)}, bf16[128,2048]{1,0:T(8,128)(2,1)}, u32[]{:S(2)}) copy-start(bf16[128,2048]{1,0:T(8,128)(2,1)} %query_ref.3) | copy-start | bytes 1572868
  2.8 16.9 %all-to-all-start = ((bf16[4,784,128]{2,1,0:T(8,128)(2,1)}), bf16[4,784,128]{2,1,0:T(8,128)(2,1)S(1)}, u32[]{:S(2)}, u32[]{:S(2)}) async-start(bf16[4,784,128]{2,1,0:T(8,128)(2,1)} %pack_message.1), calls=%async_computation | async-start | bytes 1605632 | tf_op jit(solution)/shard_map/all_to_all | solution.py:312
  7.3 6.2 %collective-permute-start = (bf16[32,4,256]{2,1,0:T(4,128)(2,1)S(1)}, bf16[32,4,256]{2,1,0:T(4,128)(2,1)S(1)}, u32[]{:S(2)}, u32[]{:S(2)}) collective-permute-start(bf16[32,4,256]{2,1,0:T(4,128)(2,1)S(1)} %bitcast.10), channel_id=1, source_target_pairs={{0,1},{1,2},{2,3},{3,4},{4,5},{5,6},{6,7},{7,8},{8,9},{9,10},{10,1... | collective-permute-start | bytes 196616 | tf_op jit(solution)/shard_map/ppermute | solution.py:290
  12.2 1.2 %copy-start.2 = (s32[32]{0:T(128)S(1)}, s32[32]{0:T(128)}, u32[]{:S(2)}) copy-start(s32[32]{0:T(128)} %start_ref.1) | copy-start | bytes 388
  12.2 1.2 %copy-start.3 = (s32[32]{0:T(128)S(1)}, s32[32]{0:T(128)}, u32[]{:S(2)}) copy-start(s32[32]{0:T(128)} %stop_ref.1) | copy-start | bytes 388
  12.2 1.2 %copy-start.4 = (s32[32]{0:T(128)S(1)}, s32[32]{0:T(128)}, u32[]{:S(2)}) copy-start(s32[32]{0:T(128)} %length_ref.1) | copy-start | bytes 388
  19.7 15.7 %collective-permute-start.1 = (bf16[4,272,128]{2,1,0:T(8,128)(2,1)S(1)}, bf16[4,272,128]{2,1,0:T(8,128)(2,1)S(1)}, u32[]{:S(2)}, u32[]{:S(2)}) collective-permute-start(bf16[4,272,128]{2,1,0:T(8,128)(2,1)S(1)} %slice.15), channel_id=1, source_target_pairs={{0,7},{1,0},{2,1},{3,2},{4,3},{5,4},{6,5},{7,6},{8,15},{9,8},{10,9... | collective-permute-start | bytes 835592 | tf_op jit(solution)/shard_map/ppermute | solution.py:273
  30.7 10.3 %collective-permute-start.3 = (bf16[4,272,128]{2,1,0:T(8,128)(2,1)S(1)}, bf16[4,272,128]{2,1,0:T(8,128)(2,1)S(1)}, u32[]{:S(2)}, u32[]{:S(2)}) collective-permute-start(bf16[4,272,128]{2,1,0:T(8,128)(2,1)S(1)} %slice.15), channel_id=1, source_target_pairs={{0,1},{1,2},{2,3},{3,4},{4,5},{5,6},{6,7},{7,0},{8,9},{9,10},{10,1... | collective-permute-start | bytes 835592 | tf_op jit(solution)/shard_map/ppermute | solution.py:273
  35.4 9.6 %collective-permute-start.2 = (bf16[4,272,128]{2,1,0:T(8,128)(2,1)S(1)}, bf16[4,272,128]{2,1,0:T(8,128)(2,1)S(1)}, u32[]{:S(2)}, u32[]{:S(2)}) collective-permute-start(bf16[4,272,128]{2,1,0:T(8,128)(2,1)S(1)} %collective-permute-done.1.refs_1_), channel_id=1, source_target_pairs={{0,7},{1,0},{2,1},{3,2},{4,3},{5,4},{6,5},{7,6},{8,15},{9,8},{10,9... | collective-permute-start | bytes 835592 | tf_op jit(solution)/shard_map/ppermute | solution.py:273
  41.0 9.7 %collective-permute-start.5 = (bf16[4,272,128]{2,1,0:T(8,128)(2,1)S(1)}, bf16[4,272,128]{2,1,0:T(8,128)(2,1)S(1)}, u32[]{:S(2)}, u32[]{:S(2)}) collective-permute-start(bf16[4,272,128]{2,1,0:T(8,128)(2,1)S(1)} %collective-permute-done.3.refs_0_), channel_id=1, source_target_pairs={{0,1},{1,2},{2,3},{3,4},{4,5},{5,6},{6,7},{7,0},{8,9},{9,10},{10,1... | collective-permute-start | bytes 835592 | tf_op jit(solution)/shard_map/ppermute | solution.py:273
  45.0 9.6 %collective-permute-start.4 = (bf16[4,272,128]{2,1,0:T(8,128)(2,1)S(1)}, bf16[4,272,128]{2,1,0:T(8,128)(2,1)S(1)}, u32[]{:S(2)}, u32[]{:S(2)}) collective-permute-start(bf16[4,272,128]{2,1,0:T(8,128)(2,1)S(1)} %collective-permute-done.2.refs_1_), channel_id=1, source_target_pairs={{0,7},{1,0},{2,1},{3,2},{4,3},{5,4},{6,5},{7,6},{8,15},{9,8},{10,9... | collective-permute-start | bytes 835592 | tf_op jit(solution)/shard_map/ppermute | solution.py:273
  50.7 9.6 %collective-permute-start.7 = (bf16[4,272,128]{2,1,0:T(8,128)(2,1)S(1)}, bf16[4,272,128]{2,1,0:T(8,128)(2,1)S(1)}, u32[]{:S(2)}, u32[]{:S(2)}) collective-permute-start(bf16[4,272,128]{2,1,0:T(8,128)(2,1)S(1)} %collective-permute-done.5.refs_0_), channel_id=1, source_target_pairs={{0,1},{1,2},{2,3},{3,4},{4,5},{5,6},{6,7},{7,0},{8,9},{9,10},{10,1... | collective-permute-start | bytes 835592 | tf_op jit(solution)/shard_map/ppermute | solution.py:273
  54.7 9.6 %collective-permute-start.6 = (bf16[4,272,128]{2,1,0:T(8,128)(2,1)S(1)}, bf16[4,272,128]{2,1,0:T(8,128)(2,1)S(1)}, u32[]{:S(2)}, u32[]{:S(2)}) collective-permute-start(bf16[4,272,128]{2,1,0:T(8,128)(2,1)S(1)} %collective-permute-done.4.refs_1_), channel_id=1, source_target_pairs={{0,7},{1,0},{2,1},{3,2},{4,3},{5,4},{6,5},{7,6},{8,15},{9,8},{10,9... | collective-permute-start | bytes 835592 | tf_op jit(solution)/shard_map/ppermute | solution.py:273

commit v5 on v4

--- a/solution.py
+++ b/solution.py
@@ -15,22 +15,28 @@
 NN = (((1,), (0,)), ((), ()))
 
 
-def pack_kernel(query_ref, stretch_ref, cache_ref, out_ref):
+def pack_kernel(query_ref, stretch_ref, cache_ref, out_ref, blocks):
     rows = query_ref.shape[0]
-    parts, _, width = out_ref.shape
+    parts, lines, width = out_ref.shape
     heads = query_ref.shape[1] // width // parts
+    base = heads * rows
+    step = pl.program_id(0)
+
+    @pl.when(step == 0)
+    def _():
+        stretch = jnp.swapaxes(stretch_ref[...], 0, 1)
+        blocks[:, :rows, :] = stretch[:, :, :width]
+        blocks[:, rows : 2 * rows, :] = stretch[:, :, width:]
+        cache = jnp.swapaxes(cache_ref[...].astype(jnp.float32), 0, 1)
+        blocks[:, 2 * rows :, :] = jnp.concatenate(
+            [cache[:, :, :width], cache[:, :, width:]], 1
+        ).astype(jnp.bfloat16)
+
     for part in range(parts):
         for head in range(heads):
             spot = (part * heads + head) * width
             out_ref[part, head * rows : (head + 1) * rows, :] = query_ref[:, spot : spot + width]
-    base = heads * rows
-    stretch = jnp.swapaxes(stretch_ref[...], 0, 1)
-    out_ref[:, base : base + rows, :] = stretch[:, :, :width]
-    out_ref[:, base + rows : base + 2 * rows, :] = stretch[:, :, width:]
-    cache = jnp.swapaxes(cache_ref[...].astype(jnp.float32), 0, 1)
-    out_ref[:, base + 2 * rows :, :] = jnp.concatenate(
-        [cache[:, :, :width], cache[:, :, width:]], 1
-    ).astype(jnp.bfloat16)
+    out_ref[:, base:lines, :] = blocks[pl.ds(step * parts, parts), :, :]
 
 
 def split(low, high):
@@ -280,8 +286,19 @@
         out_shape=jax.ShapeDtypeStruct(
             (kv_heads, lines + 2 * rows + 2 * cached_rows, head_dim), jnp.bfloat16
         ),
-        in_specs=[vmem] * 3,
-        out_specs=vmem,
+        grid=(2,),
+        in_specs=[
+            pl.BlockSpec((rows, query_width // 2), lambda step: (0, step)),
+            pl.BlockSpec(stretch_kv.shape, lambda step: (0, 0, 0)),
+            pl.BlockSpec(cache_kv.shape, lambda step: (0, 0, 0)),
+        ],
+        out_specs=pl.BlockSpec(
+            (kv_heads // 2, lines + 2 * rows + 2 * cached_rows, head_dim),
+            lambda step: (step, 0, 0),
+        ),
+        scratch_shapes=[
+            pltpu.VMEM((kv_heads, 2 * rows + 2 * cached_rows, head_dim), jnp.bfloat16)
+        ],
         name="pack_message",
     )(text_query, stretch_kv, cache_kv)
     me_array = me.reshape(1).astype(jnp.int32)

time: 77.6 us -> 77.5 us (level)
  no operation moved by 1% of the time
where the time goes in v5:
time: 77.5 us; the launch traced here: 77.1 us
  starting transfers between devices  42.2 us (54%)
  Pallas kernels  12.5 us (16%)
  blocking collectives  10.5 us (14%)
  waiting for transfers between devices  9.57 us (12%)
  between operations  1.44 us (2%)
  other arithmetic  0.85 us (1%)
    ppermute x7, starting transfers between devices, shift(): return lax.ppermute(values, 'seq', pairs)  33.5 us
    all_to_all x1, blocking collectives, shards(): lax.all_to_all(self_heads, 'seq', split_axis=0, concat_axis=0, axis_index...  10.5 us
    pallas_call x5, Pallas kernels, attend(): pl.pallas_call(functools.partial(self_kernel, steps, tuple((len(arrivals[...  7.76 us
    ppermute x7, waiting for transfers between devices, shift(): return lax.ppermute(values, 'seq', pairs)  4.72 us
    all_to_all x1, starting transfers between devices, shards(): lax.all_to_all(message, 'seq', split_axis=0, concat_axis=0, axis_index_gr...  4.42 us
    ppermute x1, starting transfers between devices, shards(): lax.ppermute(own_image, 'seq', [(i, i + 1) for i in range(devices - 1)])  4.27 us
    all_to_all x1, waiting for transfers between devices, shards(): lax.all_to_all(message, 'seq', split_axis=0, concat_axis=0, axis_index_gr...  3.66 us
    pallas_call x1, Pallas kernels, shards(): pl.pallas_call(functools.partial(cross_kernel, slots), out_shape=jax.Shap...  2.63 us
  transfers between devices with their start and end apart: 9, of which 6 were waited for; matrix products, arithmetic and copies ran while one was open for 0% of the time, Pallas kernels for 12%

profile of v5, /device:TPU:56, one launch (start us, length us, event | category | flops | bytes accessed | tf_op | source)
XLA Modules:
  0.0 77.1 jit_solution(16536826141571663394)
XLA Ops:
  0.6 2.1 %pack_message.1 = bf16[4,784,128]{2,1,0:T(8,128)(2,1)} custom-call(bf16[128,2048]{1,0:T(8,128)(2,1)} %query_ref.2, bf16[128,4,256]{2,1,0:T(4,128)(2,1)} %stretch_ref.1, bf16[8,4,256]{2,1,0:T(4,128)(2,1)} %cache_ref.1), custom_call_target="tpu_custom_call" | custom-call | tf_op jit(solution)/shard_map/pack_message/pallas_call | solution.py:284
  2.7 0.0 copy-start.1
  2.7 0.0 copy-start
  2.8 4.4 %all-to-all-start = ((bf16[4,784,128]{2,1,0:T(8,128)(2,1)}), bf16[4,784,128]{2,1,0:T(8,128)(2,1)S(1)}, u32[]{:S(2)}, u32[]{:S(2)}) async-start(bf16[4,784,128]{2,1,0:T(8,128)(2,1)} %pack_message.1), calls=%async_computation | async-start | bytes 1605632 | tf_op jit(solution)/shard_map/all_to_all | solution.py:329
  7.2 0.0 copy-done.1
  7.2 4.3 %collective-permute-start = (bf16[32,4,256]{2,1,0:T(4,128)(2,1)S(1)}, bf16[32,4,256]{2,1,0:T(4,128)(2,1)S(1)}, u32[]{:S(2)}, u32[]{:S(2)}) collective-permute-start(bf16[32,4,256]{2,1,0:T(4,128)(2,1)S(1)} %bitcast.10), channel_id=1, source_target_pairs={{0,1},{1,2},{2,3},{3,4},{4,5},{5,6},{6,7},{7,8},{8,9},{9,10},{10,1... | collective-permute-start | bytes 196616 | tf_op jit(solution)/shard_map/ppermute | solution.py:307
  12.1 0.0 copy-start.2
  12.1 0.0 copy-start.3
  12.1 0.0 copy-start.4
  12.1 1.2 %collective-permute-done.before_ref = bf16[32,4,256]{2,1,0:T(4,128)(2,1)S(1)} collective-permute-done((bf16[32,4,256]{2,1,0:T(4,128)(2,1)S(1)}, bf16[32,4,256]{2,1,0:T(4,128)(2,1)S(1)}, u32[]{:S(2)}, u32[]{:S(2)}) %collective-permute-start) | collective-permute-done | bytes 65568 | tf_op jit(solution)/shard_map/ppermute | solution.py:307
  13.3 0.0 copy-done
  13.3 0.0 copy-done.2
  13.3 0.0 copy-done.3
  13.3 0.0 copy-done.4
  13.4 2.6 %cross_attention.1 = bf16[128,2048]{1,0:T(8,128)(2,1)} custom-call(s32[1]{0:T(128)} %bitcast.me_ref, s32[32]{0:T(128)S(1)} %copy-done.2, s32[32]{0:T(128)S(1)} %copy-done.3, s32[32]{0:T(128)S(1)} %copy-done.4, f32[1]{0:T(128)S(6)} %copy.11.gate_ref, bf16[128,2048]{1,0:T(8,128)(2,1)S(1)} %copy-done, bf16[32,4,256]{2,1,0:T(4,128)(2,1)S(1)} %collective-permute-done.before_ref, ...), custom_call_target="tpu_custom_call" | custom-call | flops 400000000 | bytes 1200000 | tf_op jit(solution)/shard_map/cross_attention/pallas_call | solution.py:308
  16.0 3.7 %all-to-all-done.own_ref = bf16[4,784,128]{2,1,0:T(8,128)(2,1)S(1)} async-done(((bf16[4,784,128]{2,1,0:T(8,128)(2,1)}), bf16[4,784,128]{2,1,0:T(8,128)(2,1)S(1)}, u32[]{:S(2)}, u32[]{:S(2)}) %all-to-all-start) | async-done | bytes 802848 | tf_op jit(solution)/shard_map/all_to_all | solution.py:329
  19.7 10.9 %collective-permute-start.1 = (bf16[4,272,128]{2,1,0:T(8,128)(2,1)S(1)}, bf16[4,272,128]{2,1,0:T(8,128)(2,1)S(1)}, u32[]{:S(2)}, u32[]{:S(2)}) collective-permute-start(bf16[4,272,128]{2,1,0:T(8,128)(2,1)S(1)} %slice.15), channel_id=1, source_target_pairs={{0,7},{1,0},{2,1},{3,2},{4,3},{5,4},{6,5},{7,6},{8,15},{9,8},{10,9... | collective-permute-start | bytes 835592 | tf_op jit(solution)/shard_map/ppermute | solution.py:279
  30.6 1.9 %collective-permute-start.3 = (bf16[4,272,128]{2,1,0:T(8,128)(2,1)S(1)}, bf16[4,272,128]{2,1,0:T(8,128)(2,1)S(1)}, u32[]{:S(2)}, u32[]{:S(2)}) collective-permute-start(bf16[4,272,128]{2,1,0:T(8,128)(2,1)S(1)} %slice.15), channel_id=1, source_target_pairs={{0,1},{1,2},{2,3},{3,4},{4,5},{5,6},{6,7},{7,0},{8,9},{9,10},{10,1... | collective-permute-start | bytes 835592 | tf_op jit(solution)/shard_map/ppermute | solution.py:279
  32.5 1.4 %self_attention.5 = (f32[4,512,128]{2,1,0:T(8,128)S(1)}, f32[4,512,128]{2,1,0:T(8,128)S(1)}, f32[4,512,128]{2,1,0:T(8,128)S(1)}, bf16[2,32,128]{2,1,0:T(8,128)(2,1)S(1)}) custom-call(s32[1]{0:T(128)} %bitcast.me_ref, bf16[4,784,128]{2,1,0:T(8,128)(2,1)S(1)} %all-to-all-done.own_ref), custom_call_target="tpu_custom_call" | custom-call | flops 402653184 | bytes 2000000 | tf_op jit(solution)/shard_map/self_attention/pallas_call | solution.py:350
  33.9 1.4 %collective-permute-done.1.refs_1_ = bf16[4,272,128]{2,1,0:T(8,128)(2,1)S(1)} collective-permute-done((bf16[4,272,128]{2,1,0:T(8,128)(2,1)S(1)}, bf16[4,272,128]{2,1,0:T(8,128)(2,1)S(1)}, u32[]{:S(2)}, u32[]{:S(2)}) %collective-permute-start.1) | collective-permute-done | bytes 278560 | tf_op jit(solution)/shard_map/ppermute | solution.py:279
  35.3 5.6 %collective-permute-start.2 = (bf16[4,272,128]{2,1,0:T(8,128)(2,1)S(1)}, bf16[4,272,128]{2,1,0:T(8,128)(2,1)S(1)}, u32[]{:S(2)}, u32[]{:S(2)}) collective-permute-start(bf16[4,272,128]{2,1,0:T(8,128)(2,1)S(1)} %collective-permute-done.1.refs_1_), channel_id=1, source_target_pairs={{0,7},{1,0},{2,1},{3,2},{4,3},{5,4},{6,5},{7,6},{8,15},{9,8},{10,9... | collective-permute-start | bytes 835592 | tf_op jit(solution)/shard_map/ppermute | solution.py:279
  40.9 0.0 collective-permute-done.3.refs_0_
  40.9 1.9 %collective-permute-start.5 = (bf16[4,272,128]{2,1,0:T(8,128)(2,1)S(1)}, bf16[4,272,128]{2,1,0:T(8,128)(2,1)S(1)}, u32[]{:S(2)}, u32[]{:S(2)}) collective-permute-start(bf16[4,272,128]{2,1,0:T(8,128)(2,1)S(1)} %collective-permute-done.3.refs_0_), channel_id=1, source_target_pairs={{0,1},{1,2},{2,3},{3,4},{4,5},{5,6},{6,7},{7,0},{8,9},{9,10},{10,1... | collective-permute-start | bytes 835592 | tf_op jit(solution)/shard_map/ppermute | solution.py:279
  42.9 1.4 %self_attention.6 = (f32[4,512,128]{2,1,0:T(8,128)S(1)}, f32[4,512,128]{2,1,0:T(8,128)S(1)}, f32[4,512,128]{2,1,0:T(8,128)S(1)}, bf16[2,64,128]{2,1,0:T(8,128)(2,1)S(1)}) custom-call(s32[1]{0:T(128)} %bitcast.me_ref, bf16[4,784,128]{2,1,0:T(8,128)(2,1)S(1)} %all-to-all-done.own_ref, bf16[4,272,128]{2,1,0:T(8,128)(2,1)S(1)} %collective-permute-done.3.refs_0_, ...), custom_call_target="tpu_custom_call" | custom-call | flops 805306368 | bytes 2000000 | tf_op jit(solution)/shard_map/self_attention/pallas_call | solution.py:350
  44.3 0.7 collective-permute-done.2.refs_1_
  45.0 5.6 %collective-permute-start.4 = (bf16[4,272,128]{2,1,0:T(8,128)(2,1)S(1)}, bf16[4,272,128]{2,1,0:T(8,128)(2,1)S(1)}, u32[]{:S(2)}, u32[]{:S(2)}) collective-permute-start(bf16[4,272,128]{2,1,0:T(8,128)(2,1)S(1)} %collective-permute-done.2.refs_1_), channel_id=1, source_target_pairs={{0,7},{1,0},{2,1},{3,2},{4,3},{5,4},{6,5},{7,6},{8,15},{9,8},{10,9... | collective-permute-start | bytes 835592 | tf_op jit(solution)/shard_map/ppermute | solution.py:279
  50.6 0.0 collective-permute-done.5.refs_0_
  50.6 1.9 %collective-permute-start.7 = (bf16[4,272,128]{2,1,0:T(8,128)(2,1)S(1)}, bf16[4,272,128]{2,1,0:T(8,128)(2,1)S(1)}, u32[]{:S(2)}, u32[]{:S(2)}) collective-permute-start(bf16[4,272,128]{2,1,0:T(8,128)(2,1)S(1)} %collective-permute-done.5.refs_0_), channel_id=1, source_target_pairs={{0,1},{1,2},{2,3},{3,4},{4,5},{5,6},{6,7},{7,0},{8,9},{9,10},{10,1... | collective-permute-start | bytes 835592 | tf_op jit(solution)/shard_map/ppermute | solution.py:279
  52.5 1.6 %self_attention.7 = (f32[4,512,128]{2,1,0:T(8,128)S(1)}, f32[4,512,128]{2,1,0:T(8,128)S(1)}, f32[4,512,128]{2,1,0:T(8,128)S(1)}, bf16[2,64,128]{2,1,0:T(8,128)(2,1)S(1)}) custom-call(s32[1]{0:T(128)} %bitcast.me_ref, bf16[4,784,128]{2,1,0:T(8,128)(2,1)S(1)} %all-to-all-done.own_ref, bf16[4,272,128]{2,1,0:T(8,128)(2,1)S(1)} %collective-permute-done.5.refs_0_, ...), custom_call_target="tpu_custom_call" | custom-call | flops 805306368 | bytes 2000000 | tf_op jit(solution)/shard_map/self_attention/pallas_call | solution.py:350
  54.1 0.5 collective-permute-done.4.refs_1_
  54.6 5.6 %collective-permute-start.6 = (bf16[4,272,128]{2,1,0:T(8,128)(2,1)S(1)}, bf16[4,272,128]{2,1,0:T(8,128)(2,1)S(1)}, u32[]{:S(2)}, u32[]{:S(2)}) collective-permute-start(bf16[4,272,128]{2,1,0:T(8,128)(2,1)S(1)} %collective-permute-done.4.refs_1_), channel_id=1, source_target_pairs={{0,7},{1,0},{2,1},{3,2},{4,3},{5,4},{6,5},{7,6},{8,15},{9,8},{10,9... | collective-permute-start | bytes 835592 | tf_op jit(solution)/shard_map/ppermute | solution.py:279
  60.2 0.0 collective-permute-done.7.refs_0_
  60.2 1.9 %self_attention.8 = (f32[4,512,128]{2,1,0:T(8,128)S(1)}, f32[4,512,128]{2,1,0:T(8,128)S(1)}, f32[4,512,128]{2,1,0:T(8,128)S(1)}) custom-call(s32[1]{0:T(128)} %bitcast.me_ref, bf16[4,784,128]{2,1,0:T(8,128)(2,1)S(1)} %all-to-all-done.own_ref, bf16[4,272,128]{2,1,0:T(8,128)(2,1)S(1)} %collective-permute-done.7.refs_0_, ...), custom_call_target="tpu_custom_call" | custom-call | flops 805306368 | bytes 2000000 | tf_op jit(solution)/shard_map/self_attention/pallas_call | solution.py:350
  62.2 2.1 %collective-permute-done.6.refs_0_ = bf16[4,272,128]{2,1,0:T(8,128)(2,1)S(1)} collective-permute-done((bf16[4,272,128]{2,1,0:T(8,128)(2,1)S(1)}, bf16[4,272,128]{2,1,0:T(8,128)(2,1)S(1)}, u32[]{:S(2)}, u32[]{:S(2)}) %collective-permute-start.6) | collective-permute-done | bytes 278560 | tf_op jit(solution)/shard_map/ppermute | solution.py:279
  64.2 1.5 %self_attention.9 = bf16[4,128,512]{2,1,0:T(8,128)(2,1)S(1)} custom-call(s32[1]{0:T(128)} %bitcast.me_ref, bf16[4,784,128]{2,1,0:T(8,128)(2,1)S(1)} %all-to-all-done.own_ref, bf16[4,272,128]{2,1,0:T(8,128)(2,1)S(1)} %collective-permute-done.6.refs_0_, f32[4,512,128]{2,1,0:T(8,128)S(1)} %get-tuple-element.60.refs_1_, ...), custom_call_target="tpu_custom_call" | custom-call | flops 402653184 | bytes 2000000 | tf_op jit(solution)/shard_map/self_attention/pallas_call | solution.py:350
  65.7 10.5 %all_to_all.10 = bf16[4,128,512]{2,1,0:T(8,128)(2,1)S(1)} all-to-all(bf16[4,128,512]{2,1,0:T(8,128)(2,1)S(1)} %self_attention.9), channel_id=1, replica_groups={{0,8,16,24},{1,9,17,25},{2,10,18,26},{3,11,19,27},{4,12,20,28},{5,13,21..., dimensions={0} | all-to-all | bytes 1048576 | tf_op jit(solution)/shard_map/all_to_all | solution.py:392
  76.2 0.9 %pad_maximum_fusion = bf16[128,2048]{1,0:T(8,128)(2,1)} fusion(bf16[128,512]{1,0:T(8,128)(2,1)S(1)} %get-tuple-element.65, bf16[128,512]{1,0:T(8,128)(2,1)S(1)} %get-tuple-element.66, bf16[128,512]{1,0:T(8,128)(2,1)S(1)} %get-tuple-element.67, bf16[128,512]{1,0:T(8,128)(2,1)S(1)} %get-tuple-element.64), kind=kLoop, calls=%fused_computation | loop fusion | flops 2097152 | bytes 1048576 | tf_op jit(solution)/shard_map/concatenate | solution.py:395
  (2 shorter events, 0.1 us)
Async XLA Ops:
  2.7 4.4 %copy-start.1 = (bf16[1,32,4,256]{3,2,1,0:T(4,128)(2,1)S(1)}, bf16[1,32,4,256]{3,2,1,0:T(4,128)(2,1)}, u32[]{:S(2)}) copy-start(bf16[1,32,4,256]{3,2,1,0:T(4,128)(2,1)} %param.13) | copy-start | bytes 196612
  2.7 10.6 %copy-start = (bf16[128,2048]{1,0:T(8,128)(2,1)S(1)}, bf16[128,2048]{1,0:T(8,128)(2,1)}, u32[]{:S(2)}) copy-start(bf16[128,2048]{1,0:T(8,128)(2,1)} %query_ref.3) | copy-start | bytes 1572868
  2.8 16.9 %all-to-all-start = ((bf16[4,784,128]{2,1,0:T(8,128)(2,1)}), bf16[4,784,128]{2,1,0:T(8,128)(2,1)S(1)}, u32[]{:S(2)}, u32[]{:S(2)}) async-start(bf16[4,784,128]{2,1,0:T(8,128)(2,1)} %pack_message.1), calls=%async_computation | async-start | bytes 1605632 | tf_op jit(solution)/shard_map/all_to_all | solution.py:329
  7.2 6.2 %collective-permute-start = (bf16[32,4,256]{2,1,0:T(4,128)(2,1)S(1)}, bf16[32,4,256]{2,1,0:T(4,128)(2,1)S(1)}, u32[]{:S(2)}, u32[]{:S(2)}) collective-permute-start(bf16[32,4,256]{2,1,0:T(4,128)(2,1)S(1)} %bitcast.10), channel_id=1, source_target_pairs={{0,1},{1,2},{2,3},{3,4},{4,5},{5,6},{6,7},{7,8},{8,9},{9,10},{10,1... | collective-permute-start | bytes 196616 | tf_op jit(solution)/shard_map/ppermute | solution.py:307
  12.1 1.2 %copy-start.2 = (s32[32]{0:T(128)S(1)}, s32[32]{0:T(128)}, u32[]{:S(2)}) copy-start(s32[32]{0:T(128)} %start_ref.1) | copy-start | bytes 388
  12.1 1.2 %copy-start.3 = (s32[32]{0:T(128)S(1)}, s32[32]{0:T(128)}, u32[]{:S(2)}) copy-start(s32[32]{0:T(128)} %stop_ref.1) | copy-start | bytes 388
  12.1 1.2 %copy-start.4 = (s32[32]{0:T(128)S(1)}, s32[32]{0:T(128)}, u32[]{:S(2)}) copy-start(s32[32]{0:T(128)} %length_ref.1) | copy-start | bytes 388
  19.7 15.7 %collective-permute-start.1 = (bf16[4,272,128]{2,1,0:T(8,128)(2,1)S(1)}, bf16[4,272,128]{2,1,0:T(8,128)(2,1)S(1)}, u32[]{:S(2)}, u32[]{:S(2)}) collective-permute-start(bf16[4,272,128]{2,1,0:T(8,128)(2,1)S(1)} %slice.15), channel_id=1, source_target_pairs={{0,7},{1,0},{2,1},{3,2},{4,3},{5,4},{6,5},{7,6},{8,15},{9,8},{10,9... | collective-permute-start | bytes 835592 | tf_op jit(solution)/shard_map/ppermute | solution.py:279
  30.6 10.3 %collective-permute-start.3 = (bf16[4,272,128]{2,1,0:T(8,128)(2,1)S(1)}, bf16[4,272,128]{2,1,0:T(8,128)(2,1)S(1)}, u32[]{:S(2)}, u32[]{:S(2)}) collective-permute-start(bf16[4,272,128]{2,1,0:T(8,128)(2,1)S(1)} %slice.15), channel_id=1, source_target_pairs={{0,1},{1,2},{2,3},{3,4},{4,5},{5,6},{6,7},{7,0},{8,9},{9,10},{10,1... | collective-permute-start | bytes 835592 | tf_op jit(solution)/shard_map/ppermute | solution.py:279
  35.3 9.6 %collective-permute-start.2 = (bf16[4,272,128]{2,1,0:T(8,128)(2,1)S(1)}, bf16[4,272,128]{2,1,0:T(8,128)(2,1)S(1)}, u32[]{:S(2)}, u32[]{:S(2)}) collective-permute-start(bf16[4,272,128]{2,1,0:T(8,128)(2,1)S(1)} %collective-permute-done.1.refs_1_), channel_id=1, source_target_pairs={{0,7},{1,0},{2,1},{3,2},{4,3},{5,4},{6,5},{7,6},{8,15},{9,8},{10,9... | collective-permute-start | bytes 835592 | tf_op jit(solution)/shard_map/ppermute | solution.py:279
  40.9 9.7 %collective-permute-start.5 = (bf16[4,272,128]{2,1,0:T(8,128)(2,1)S(1)}, bf16[4,272,128]{2,1,0:T(8,128)(2,1)S(1)}, u32[]{:S(2)}, u32[]{:S(2)}) collective-permute-start(bf16[4,272,128]{2,1,0:T(8,128)(2,1)S(1)} %collective-permute-done.3.refs_0_), channel_id=1, source_target_pairs={{0,1},{1,2},{2,3},{3,4},{4,5},{5,6},{6,7},{7,0},{8,9},{9,10},{10,1... | collective-permute-start | bytes 835592 | tf_op jit(solution)/shard_map/ppermute | solution.py:279
  45.0 9.6 %collective-permute-start.4 = (bf16[4,272,128]{2,1,0:T(8,128)(2,1)S(1)}, bf16[4,272,128]{2,1,0:T(8,128)(2,1)S(1)}, u32[]{:S(2)}, u32[]{:S(2)}) collective-permute-start(bf16[4,272,128]{2,1,0:T(8,128)(2,1)S(1)} %collective-permute-done.2.refs_1_), channel_id=1, source_target_pairs={{0,7},{1,0},{2,1},{3,2},{4,3},{5,4},{6,5},{7,6},{8,15},{9,8},{10,9... | collective-permute-start | bytes 835592 | tf_op jit(solution)/shard_map/ppermute | solution.py:279
  50.6 9.6 %collective-permute-start.7 = (bf16[4,272,128]{2,1,0:T(8,128)(2,1)S(1)}, bf16[4,272,128]{2,1,0:T(8,128)(2,1)S(1)}, u32[]{:S(2)}, u32[]{:S(2)}) collective-permute-start(bf16[4,272,128]{2,1,0:T(8,128)(2,1)S(1)} %collective-permute-done.5.refs_0_), channel_id=1, source_target_pairs={{0,1},{1,2},{2,3},{3,4},{4,5},{5,6},{6,7},{7,0},{8,9},{9,10},{10,1... | collective-permute-start | bytes 835592 | tf_op jit(solution)/shard_map/ppermute | solution.py:279
  54.6 9.6 %collective-permute-start.6 = (bf16[4,272,128]{2,1,0:T(8,128)(2,1)S(1)}, bf16[4,272,128]{2,1,0:T(8,128)(2,1)S(1)}, u32[]{:S(2)}, u32[]{:S(2)}) collective-permute-start(bf16[4,272,128]{2,1,0:T(8,128)(2,1)S(1)} %collective-permute-done.4.refs_1_), channel_id=1, source_target_pairs={{0,7},{1,0},{2,1},{3,2},{4,3},{5,4},{6,5},{7,6},{8,15},{9,8},{10,9... | collective-permute-start | bytes 835592 | tf_op jit(solution)/shard_map/ppermute | solution.py:279

commit v6 on v5

--- a/solution.py
+++ b/solution.py
@@ -173,7 +173,8 @@
                 total = total * jnp.concatenate([fade, fade], 1) + added
             peak = top
         if last:
-            result = (total[:, :width] / total[:, width:]).astype(jnp.bfloat16)
+            share = pl.reciprocal(total[:, width:])
+            result = (total[:, :width] * share).astype(jnp.bfloat16)
             for head in range(heads):
                 out_ref[part, :, head * width : (head + 1) * width] = result[
                     head * rows : (head + 1) * rows

time: 77.5 us -> 77.5 us (level)
  no operation moved by 1% of the time
where the time goes in v6:
time: 77.5 us; the launch traced here: 77.1 us
  starting transfers between devices  42.2 us (54%)
  Pallas kernels  12.5 us (16%)
  blocking collectives  10.5 us (14%)
  waiting for transfers between devices  9.57 us (12%)
  between operations  1.44 us (2%)
  other arithmetic  0.85 us (1%)
    ppermute x7, starting transfers between devices, shift(): return lax.ppermute(values, 'seq', pairs)  33.5 us
    all_to_all x1, blocking collectives, shards(): lax.all_to_all(self_heads, 'seq', split_axis=0, concat_axis=0, axis_index...  10.5 us
    pallas_call x5, Pallas kernels, attend(): pl.pallas_call(functools.partial(self_kernel, steps, tuple((len(arrivals[...  7.76 us
    ppermute x7, waiting for transfers between devices, shift(): return lax.ppermute(values, 'seq', pairs)  4.72 us
    all_to_all x1, starting transfers between devices, shards(): lax.all_to_all(message, 'seq', split_axis=0, concat_axis=0, axis_index_gr...  4.42 us
    ppermute x1, starting transfers between devices, shards(): lax.ppermute(own_image, 'seq', [(i, i + 1) for i in range(devices - 1)])  4.27 us
    all_to_all x1, waiting for transfers between devices, shards(): lax.all_to_all(message, 'seq', split_axis=0, concat_axis=0, axis_index_gr...  3.66 us
    pallas_call x1, Pallas kernels, shards(): pl.pallas_call(functools.partial(cross_kernel, slots), out_shape=jax.Shap...  2.63 us
  transfers between devices with their start and end apart: 9, of which 6 were waited for; matrix products, arithmetic and copies ran while one was open for 0% of the time, Pallas kernels for 12%

profile of v6, /device:TPU:56, one launch (start us, length us, event | category | flops | bytes accessed | tf_op | source)
XLA Modules:
  0.0 77.1 jit_solution(16536826141571663394)
XLA Ops:
  0.6 2.1 %pack_message.1 = bf16[4,784,128]{2,1,0:T(8,128)(2,1)} custom-call(bf16[128,2048]{1,0:T(8,128)(2,1)} %query_ref.2, bf16[128,4,256]{2,1,0:T(4,128)(2,1)} %stretch_ref.1, bf16[8,4,256]{2,1,0:T(4,128)(2,1)} %cache_ref.1), custom_call_target="tpu_custom_call" | custom-call | tf_op jit(solution)/shard_map/pack_message/pallas_call | solution.py:285
  2.7 0.0 copy-start.1
  2.7 0.0 copy-start
  2.8 4.4 %all-to-all-start = ((bf16[4,784,128]{2,1,0:T(8,128)(2,1)}), bf16[4,784,128]{2,1,0:T(8,128)(2,1)S(1)}, u32[]{:S(2)}, u32[]{:S(2)}) async-start(bf16[4,784,128]{2,1,0:T(8,128)(2,1)} %pack_message.1), calls=%async_computation | async-start | bytes 1605632 | tf_op jit(solution)/shard_map/all_to_all | solution.py:330
  7.2 0.0 copy-done.1
  7.2 4.3 %collective-permute-start = (bf16[32,4,256]{2,1,0:T(4,128)(2,1)S(1)}, bf16[32,4,256]{2,1,0:T(4,128)(2,1)S(1)}, u32[]{:S(2)}, u32[]{:S(2)}) collective-permute-start(bf16[32,4,256]{2,1,0:T(4,128)(2,1)S(1)} %bitcast.10), channel_id=1, source_target_pairs={{0,1},{1,2},{2,3},{3,4},{4,5},{5,6},{6,7},{7,8},{8,9},{9,10},{10,1... | collective-permute-start | bytes 196616 | tf_op jit(solution)/shard_map/ppermute | solution.py:308
  12.1 0.0 copy-start.2
  12.1 0.0 copy-start.3
  12.1 0.0 copy-start.4
  12.1 1.2 %collective-permute-done.before_ref = bf16[32,4,256]{2,1,0:T(4,128)(2,1)S(1)} collective-permute-done((bf16[32,4,256]{2,1,0:T(4,128)(2,1)S(1)}, bf16[32,4,256]{2,1,0:T(4,128)(2,1)S(1)}, u32[]{:S(2)}, u32[]{:S(2)}) %collective-permute-start) | collective-permute-done | bytes 65568 | tf_op jit(solution)/shard_map/ppermute | solution.py:308
  13.3 0.0 copy-done
  13.3 0.0 copy-done.2
  13.3 0.0 copy-done.3
  13.3 0.0 copy-done.4
  13.4 2.6 %cross_attention.1 = bf16[128,2048]{1,0:T(8,128)(2,1)} custom-call(s32[1]{0:T(128)} %bitcast.me_ref, s32[32]{0:T(128)S(1)} %copy-done.2, s32[32]{0:T(128)S(1)} %copy-done.3, s32[32]{0:T(128)S(1)} %copy-done.4, f32[1]{0:T(128)S(6)} %copy.11.gate_ref, bf16[128,2048]{1,0:T(8,128)(2,1)S(1)} %copy-done, bf16[32,4,256]{2,1,0:T(4,128)(2,1)S(1)} %collective-permute-done.before_ref, ...), custom_call_target="tpu_custom_call" | custom-call | flops 400000000 | bytes 1200000 | tf_op jit(solution)/shard_map/cross_attention/pallas_call | solution.py:309
  16.0 3.7 %all-to-all-done.own_ref = bf16[4,784,128]{2,1,0:T(8,128)(2,1)S(1)} async-done(((bf16[4,784,128]{2,1,0:T(8,128)(2,1)}), bf16[4,784,128]{2,1,0:T(8,128)(2,1)S(1)}, u32[]{:S(2)}, u32[]{:S(2)}) %all-to-all-start) | async-done | bytes 802848 | tf_op jit(solution)/shard_map/all_to_all | solution.py:330
  19.7 10.9 %collective-permute-start.1 = (bf16[4,272,128]{2,1,0:T(8,128)(2,1)S(1)}, bf16[4,272,128]{2,1,0:T(8,128)(2,1)S(1)}, u32[]{:S(2)}, u32[]{:S(2)}) collective-permute-start(bf16[4,272,128]{2,1,0:T(8,128)(2,1)S(1)} %slice.15), channel_id=1, source_target_pairs={{0,7},{1,0},{2,1},{3,2},{4,3},{5,4},{6,5},{7,6},{8,15},{9,8},{10,9... | collective-permute-start | bytes 835592 | tf_op jit(solution)/shard_map/ppermute | solution.py:280
  30.6 1.9 %collective-permute-start.3 = (bf16[4,272,128]{2,1,0:T(8,128)(2,1)S(1)}, bf16[4,272,128]{2,1,0:T(8,128)(2,1)S(1)}, u32[]{:S(2)}, u32[]{:S(2)}) collective-permute-start(bf16[4,272,128]{2,1,0:T(8,128)(2,1)S(1)} %slice.15), channel_id=1, source_target_pairs={{0,1},{1,2},{2,3},{3,4},{4,5},{5,6},{6,7},{7,0},{8,9},{9,10},{10,1... | collective-permute-start | bytes 835592 | tf_op jit(solution)/shard_map/ppermute | solution.py:280
  32.5 1.4 %self_attention.5 = (f32[4,512,128]{2,1,0:T(8,128)S(1)}, f32[4,512,128]{2,1,0:T(8,128)S(1)}, f32[4,512,128]{2,1,0:T(8,128)S(1)}, bf16[2,32,128]{2,1,0:T(8,128)(2,1)S(1)}) custom-call(s32[1]{0:T(128)} %bitcast.me_ref, bf16[4,784,128]{2,1,0:T(8,128)(2,1)S(1)} %all-to-all-done.own_ref), custom_call_target="tpu_custom_call" | custom-call | flops 402653184 | bytes 2000000 | tf_op jit(solution)/shard_map/self_attention/pallas_call | solution.py:351
  33.9 1.4 %collective-permute-done.1.refs_1_ = bf16[4,272,128]{2,1,0:T(8,128)(2,1)S(1)} collective-permute-done((bf16[4,272,128]{2,1,0:T(8,128)(2,1)S(1)}, bf16[4,272,128]{2,1,0:T(8,128)(2,1)S(1)}, u32[]{:S(2)}, u32[]{:S(2)}) %collective-permute-start.1) | collective-permute-done | bytes 278560 | tf_op jit(solution)/shard_map/ppermute | solution.py:280
  35.3 5.6 %collective-permute-start.2 = (bf16[4,272,128]{2,1,0:T(8,128)(2,1)S(1)}, bf16[4,272,128]{2,1,0:T(8,128)(2,1)S(1)}, u32[]{:S(2)}, u32[]{:S(2)}) collective-permute-start(bf16[4,272,128]{2,1,0:T(8,128)(2,1)S(1)} %collective-permute-done.1.refs_1_), channel_id=1, source_target_pairs={{0,7},{1,0},{2,1},{3,2},{4,3},{5,4},{6,5},{7,6},{8,15},{9,8},{10,9... | collective-permute-start | bytes 835592 | tf_op jit(solution)/shard_map/ppermute | solution.py:280
  40.9 0.0 collective-permute-done.3.refs_0_
  40.9 1.9 %collective-permute-start.5 = (bf16[4,272,128]{2,1,0:T(8,128)(2,1)S(1)}, bf16[4,272,128]{2,1,0:T(8,128)(2,1)S(1)}, u32[]{:S(2)}, u32[]{:S(2)}) collective-permute-start(bf16[4,272,128]{2,1,0:T(8,128)(2,1)S(1)} %collective-permute-done.3.refs_0_), channel_id=1, source_target_pairs={{0,1},{1,2},{2,3},{3,4},{4,5},{5,6},{6,7},{7,0},{8,9},{9,10},{10,1... | collective-permute-start | bytes 835592 | tf_op jit(solution)/shard_map/ppermute | solution.py:280
  42.9 1.4 %self_attention.6 = (f32[4,512,128]{2,1,0:T(8,128)S(1)}, f32[4,512,128]{2,1,0:T(8,128)S(1)}, f32[4,512,128]{2,1,0:T(8,128)S(1)}, bf16[2,64,128]{2,1,0:T(8,128)(2,1)S(1)}) custom-call(s32[1]{0:T(128)} %bitcast.me_ref, bf16[4,784,128]{2,1,0:T(8,128)(2,1)S(1)} %all-to-all-done.own_ref, bf16[4,272,128]{2,1,0:T(8,128)(2,1)S(1)} %collective-permute-done.3.refs_0_, ...), custom_call_target="tpu_custom_call" | custom-call | flops 805306368 | bytes 2000000 | tf_op jit(solution)/shard_map/self_attention/pallas_call | solution.py:351
  44.3 0.7 collective-permute-done.2.refs_1_
  45.0 5.6 %collective-permute-start.4 = (bf16[4,272,128]{2,1,0:T(8,128)(2,1)S(1)}, bf16[4,272,128]{2,1,0:T(8,128)(2,1)S(1)}, u32[]{:S(2)}, u32[]{:S(2)}) collective-permute-start(bf16[4,272,128]{2,1,0:T(8,128)(2,1)S(1)} %collective-permute-done.2.refs_1_), channel_id=1, source_target_pairs={{0,7},{1,0},{2,1},{3,2},{4,3},{5,4},{6,5},{7,6},{8,15},{9,8},{10,9... | collective-permute-start | bytes 835592 | tf_op jit(solution)/shard_map/ppermute | solution.py:280
  50.6 0.0 collective-permute-done.5.refs_0_
  50.6 1.9 %collective-permute-start.7 = (bf16[4,272,128]{2,1,0:T(8,128)(2,1)S(1)}, bf16[4,272,128]{2,1,0:T(8,128)(2,1)S(1)}, u32[]{:S(2)}, u32[]{:S(2)}) collective-permute-start(bf16[4,272,128]{2,1,0:T(8,128)(2,1)S(1)} %collective-permute-done.5.refs_0_), channel_id=1, source_target_pairs={{0,1},{1,2},{2,3},{3,4},{4,5},{5,6},{6,7},{7,0},{8,9},{9,10},{10,1... | collective-permute-start | bytes 835592 | tf_op jit(solution)/shard_map/ppermute | solution.py:280
  52.5 1.6 %self_attention.7 = (f32[4,512,128]{2,1,0:T(8,128)S(1)}, f32[4,512,128]{2,1,0:T(8,128)S(1)}, f32[4,512,128]{2,1,0:T(8,128)S(1)}, bf16[2,64,128]{2,1,0:T(8,128)(2,1)S(1)}) custom-call(s32[1]{0:T(128)} %bitcast.me_ref, bf16[4,784,128]{2,1,0:T(8,128)(2,1)S(1)} %all-to-all-done.own_ref, bf16[4,272,128]{2,1,0:T(8,128)(2,1)S(1)} %collective-permute-done.5.refs_0_, ...), custom_call_target="tpu_custom_call" | custom-call | flops 805306368 | bytes 2000000 | tf_op jit(solution)/shard_map/self_attention/pallas_call | solution.py:351
  54.1 0.5 collective-permute-done.4.refs_1_
  54.6 5.6 %collective-permute-start.6 = (bf16[4,272,128]{2,1,0:T(8,128)(2,1)S(1)}, bf16[4,272,128]{2,1,0:T(8,128)(2,1)S(1)}, u32[]{:S(2)}, u32[]{:S(2)}) collective-permute-start(bf16[4,272,128]{2,1,0:T(8,128)(2,1)S(1)} %collective-permute-done.4.refs_1_), channel_id=1, source_target_pairs={{0,7},{1,0},{2,1},{3,2},{4,3},{5,4},{6,5},{7,6},{8,15},{9,8},{10,9... | collective-permute-start | bytes 835592 | tf_op jit(solution)/shard_map/ppermute | solution.py:280
  60.2 0.0 collective-permute-done.7.refs_0_
  60.2 1.9 %self_attention.8 = (f32[4,512,128]{2,1,0:T(8,128)S(1)}, f32[4,512,128]{2,1,0:T(8,128)S(1)}, f32[4,512,128]{2,1,0:T(8,128)S(1)}) custom-call(s32[1]{0:T(128)} %bitcast.me_ref, bf16[4,784,128]{2,1,0:T(8,128)(2,1)S(1)} %all-to-all-done.own_ref, bf16[4,272,128]{2,1,0:T(8,128)(2,1)S(1)} %collective-permute-done.7.refs_0_, ...), custom_call_target="tpu_custom_call" | custom-call | flops 805306368 | bytes 2000000 | tf_op jit(solution)/shard_map/self_attention/pallas_call | solution.py:351
  62.2 2.1 %collective-permute-done.6.refs_0_ = bf16[4,272,128]{2,1,0:T(8,128)(2,1)S(1)} collective-permute-done((bf16[4,272,128]{2,1,0:T(8,128)(2,1)S(1)}, bf16[4,272,128]{2,1,0:T(8,128)(2,1)S(1)}, u32[]{:S(2)}, u32[]{:S(2)}) %collective-permute-start.6) | collective-permute-done | bytes 278560 | tf_op jit(solution)/shard_map/ppermute | solution.py:280
  64.2 1.5 %self_attention.9 = bf16[4,128,512]{2,1,0:T(8,128)(2,1)S(1)} custom-call(s32[1]{0:T(128)} %bitcast.me_ref, bf16[4,784,128]{2,1,0:T(8,128)(2,1)S(1)} %all-to-all-done.own_ref, bf16[4,272,128]{2,1,0:T(8,128)(2,1)S(1)} %collective-permute-done.6.refs_0_, f32[4,512,128]{2,1,0:T(8,128)S(1)} %get-tuple-element.60.refs_1_, ...), custom_call_target="tpu_custom_call" | custom-call | flops 402653184 | bytes 2000000 | tf_op jit(solution)/shard_map/self_attention/pallas_call | solution.py:351
  65.7 10.5 %all_to_all.10 = bf16[4,128,512]{2,1,0:T(8,128)(2,1)S(1)} all-to-all(bf16[4,128,512]{2,1,0:T(8,128)(2,1)S(1)} %self_attention.9), channel_id=1, replica_groups={{0,8,16,24},{1,9,17,25},{2,10,18,26},{3,11,19,27},{4,12,20,28},{5,13,21..., dimensions={0} | all-to-all | bytes 1048576 | tf_op jit(solution)/shard_map/all_to_all | solution.py:393
  76.2 0.9 %pad_maximum_fusion = bf16[128,2048]{1,0:T(8,128)(2,1)} fusion(bf16[128,512]{1,0:T(8,128)(2,1)S(1)} %get-tuple-element.65, bf16[128,512]{1,0:T(8,128)(2,1)S(1)} %get-tuple-element.66, bf16[128,512]{1,0:T(8,128)(2,1)S(1)} %get-tuple-element.67, bf16[128,512]{1,0:T(8,128)(2,1)S(1)} %get-tuple-element.64), kind=kLoop, calls=%fused_computation | loop fusion | flops 2097152 | bytes 1048576 | tf_op jit(solution)/shard_map/concatenate | solution.py:396
  (2 shorter events, 0.1 us)
Async XLA Ops:
  2.7 4.4 %copy-start.1 = (bf16[1,32,4,256]{3,2,1,0:T(4,128)(2,1)S(1)}, bf16[1,32,4,256]{3,2,1,0:T(4,128)(2,1)}, u32[]{:S(2)}) copy-start(bf16[1,32,4,256]{3,2,1,0:T(4,128)(2,1)} %param.13) | copy-start | bytes 196612
  2.7 10.6 %copy-start = (bf16[128,2048]{1,0:T(8,128)(2,1)S(1)}, bf16[128,2048]{1,0:T(8,128)(2,1)}, u32[]{:S(2)}) copy-start(bf16[128,2048]{1,0:T(8,128)(2,1)} %query_ref.3) | copy-start | bytes 1572868
  2.8 16.9 %all-to-all-start = ((bf16[4,784,128]{2,1,0:T(8,128)(2,1)}), bf16[4,784,128]{2,1,0:T(8,128)(2,1)S(1)}, u32[]{:S(2)}, u32[]{:S(2)}) async-start(bf16[4,784,128]{2,1,0:T(8,128)(2,1)} %pack_message.1), calls=%async_computation | async-start | bytes 1605632 | tf_op jit(solution)/shard_map/all_to_all | solution.py:330
  7.2 6.2 %collective-permute-start = (bf16[32,4,256]{2,1,0:T(4,128)(2,1)S(1)}, bf16[32,4,256]{2,1,0:T(4,128)(2,1)S(1)}, u32[]{:S(2)}, u32[]{:S(2)}) collective-permute-start(bf16[32,4,256]{2,1,0:T(4,128)(2,1)S(1)} %bitcast.10), channel_id=1, source_target_pairs={{0,1},{1,2},{2,3},{3,4},{4,5},{5,6},{6,7},{7,8},{8,9},{9,10},{10,1... | collective-permute-start | bytes 196616 | tf_op jit(solution)/shard_map/ppermute | solution.py:308
  12.1 1.2 %copy-start.2 = (s32[32]{0:T(128)S(1)}, s32[32]{0:T(128)}, u32[]{:S(2)}) copy-start(s32[32]{0:T(128)} %start_ref.1) | copy-start | bytes 388
  12.1 1.2 %copy-start.3 = (s32[32]{0:T(128)S(1)}, s32[32]{0:T(128)}, u32[]{:S(2)}) copy-start(s32[32]{0:T(128)} %stop_ref.1) | copy-start | bytes 388
  12.1 1.2 %copy-start.4 = (s32[32]{0:T(128)S(1)}, s32[32]{0:T(128)}, u32[]{:S(2)}) copy-start(s32[32]{0:T(128)} %length_ref.1) | copy-start | bytes 388
  19.7 15.7 %collective-permute-start.1 = (bf16[4,272,128]{2,1,0:T(8,128)(2,1)S(1)}, bf16[4,272,128]{2,1,0:T(8,128)(2,1)S(1)}, u32[]{:S(2)}, u32[]{:S(2)}) collective-permute-start(bf16[4,272,128]{2,1,0:T(8,128)(2,1)S(1)} %slice.15), channel_id=1, source_target_pairs={{0,7},{1,0},{2,1},{3,2},{4,3},{5,4},{6,5},{7,6},{8,15},{9,8},{10,9... | collective-permute-start | bytes 835592 | tf_op jit(solution)/shard_map/ppermute | solution.py:280
  30.6 10.3 %collective-permute-start.3 = (bf16[4,272,128]{2,1,0:T(8,128)(2,1)S(1)}, bf16[4,272,128]{2,1,0:T(8,128)(2,1)S(1)}, u32[]{:S(2)}, u32[]{:S(2)}) collective-permute-start(bf16[4,272,128]{2,1,0:T(8,128)(2,1)S(1)} %slice.15), channel_id=1, source_target_pairs={{0,1},{1,2},{2,3},{3,4},{4,5},{5,6},{6,7},{7,0},{8,9},{9,10},{10,1... | collective-permute-start | bytes 835592 | tf_op jit(solution)/shard_map/ppermute | solution.py:280
  35.3 9.6 %collective-permute-start.2 = (bf16[4,272,128]{2,1,0:T(8,128)(2,1)S(1)}, bf16[4,272,128]{2,1,0:T(8,128)(2,1)S(1)}, u32[]{:S(2)}, u32[]{:S(2)}) collective-permute-start(bf16[4,272,128]{2,1,0:T(8,128)(2,1)S(1)} %collective-permute-done.1.refs_1_), channel_id=1, source_target_pairs={{0,7},{1,0},{2,1},{3,2},{4,3},{5,4},{6,5},{7,6},{8,15},{9,8},{10,9... | collective-permute-start | bytes 835592 | tf_op jit(solution)/shard_map/ppermute | solution.py:280
  40.9 9.7 %collective-permute-start.5 = (bf16[4,272,128]{2,1,0:T(8,128)(2,1)S(1)}, bf16[4,272,128]{2,1,0:T(8,128)(2,1)S(1)}, u32[]{:S(2)}, u32[]{:S(2)}) collective-permute-start(bf16[4,272,128]{2,1,0:T(8,128)(2,1)S(1)} %collective-permute-done.3.refs_0_), channel_id=1, source_target_pairs={{0,1},{1,2},{2,3},{3,4},{4,5},{5,6},{6,7},{7,0},{8,9},{9,10},{10,1... | collective-permute-start | bytes 835592 | tf_op jit(solution)/shard_map/ppermute | solution.py:280
  45.0 9.6 %collective-permute-start.4 = (bf16[4,272,128]{2,1,0:T(8,128)(2,1)S(1)}, bf16[4,272,128]{2,1,0:T(8,128)(2,1)S(1)}, u32[]{:S(2)}, u32[]{:S(2)}) collective-permute-start(bf16[4,272,128]{2,1,0:T(8,128)(2,1)S(1)} %collective-permute-done.2.refs_1_), channel_id=1, source_target_pairs={{0,7},{1,0},{2,1},{3,2},{4,3},{5,4},{6,5},{7,6},{8,15},{9,8},{10,9... | collective-permute-start | bytes 835592 | tf_op jit(solution)/shard_map/ppermute | solution.py:280
  50.6 9.6 %collective-permute-start.7 = (bf16[4,272,128]{2,1,0:T(8,128)(2,1)S(1)}, bf16[4,272,128]{2,1,0:T(8,128)(2,1)S(1)}, u32[]{:S(2)}, u32[]{:S(2)}) collective-permute-start(bf16[4,272,128]{2,1,0:T(8,128)(2,1)S(1)} %collective-permute-done.5.refs_0_), channel_id=1, source_target_pairs={{0,1},{1,2},{2,3},{3,4},{4,5},{5,6},{6,7},{7,0},{8,9},{9,10},{10,1... | collective-permute-start | bytes 835592 | tf_op jit(solution)/shard_map/ppermute | solution.py:280
  54.6 9.6 %collective-permute-start.6 = (bf16[4,272,128]{2,1,0:T(8,128)(2,1)S(1)}, bf16[4,272,128]{2,1,0:T(8,128)(2,1)S(1)}, u32[]{:S(2)}, u32[]{:S(2)}) collective-permute-start(bf16[4,272,128]{2,1,0:T(8,128)(2,1)S(1)} %collective-permute-done.4.refs_1_), channel_id=1, source_target_pairs={{0,7},{1,0},{2,1},{3,2},{4,3},{5,4},{6,5},{7,6},{8,15},{9,8},{10,9... | collective-permute-start | bytes 835592 | tf_op jit(solution)/shard_map/ppermute | solution.py:280
